TPU v7x, 512 devices: a whole 4x4x16 slice. The times are simulated.
512 devices in a mesh: seq: 32 (over z_lo, y, core), fsdp: 16 (over z_hi, x).
Axes of the slice: x: 4, y: 4, z: 16 (z_hi: 4, z_lo: 4; z = z_hi * 4 + z_lo), core: 2. Of those that a mesh axis runs over, the one named last changes fastest.
Arguments:
- tokens: bfloat16 [2048, 4608], P('seq'), may hold values from -6 to 6
- pre_gain: float32 [4608], replicated, may hold values from 0.5 to 1.5
- w_qkv: bfloat16 [4608, 8192], P('seq', 'fsdp'), may hold values from -0.1875 to 0.1875
- w_out: bfloat16 [4096, 4608], P('fsdp', 'seq'), may hold values from -0.09375 to 0.09375
- cache_keys: bfloat16 [8192, 2048], P('seq', 'fsdp'), may hold values from -48 to 48
- cache_values: bfloat16 [8192, 2048], P('seq', 'fsdp'), may hold values from -12 to 12
- cache_len: int32 [1], replicated, may hold values from 4096 to 8192
Outputs:
- layer_out: bfloat16 [2048, 4608], P('seq', 'fsdp')
All inputs are finite; a program needn't handle non-finite values.
Results may differ from a plain program's by a relative error of at most 0.013.
The roundings to bfloat16 on the way count: a program that leaves them out, or rounds other values in their place, can miss the bound.
Values may be sent and summed in bfloat16 or wider, within the bound.
No kernel may reach another device: no remote copies, remote signals or barrier semaphores. Data moves between devices by JAX's collectives and lax.ppermute only.
A program may use at most 64 MiB of HBM per device.

v0:
```python
import jax
import jax.numpy as jnp
from jax import lax
from jax.sharding import PartitionSpec as P

D = 4608
HEAD = 128
KV_DEV = 1


masked_score = -1e30
epsilon = 1e-06


def rotate(values, positions):
    half_dim = values.shape[-1] // 2
    inverse_freq = 10000.0 ** (-jnp.arange(half_dim, dtype=jnp.float32) / half_dim)
    angles = positions.astype(jnp.float32)[:, None] * inverse_freq[None, :]
    target = (values.shape[0],) + (1,) * (values.ndim - 2) + (half_dim,)
    cosine = jnp.cos(angles).reshape(target)
    sine_part = jnp.sin(angles).reshape(target)
    first = values[..., :half_dim]
    second = values[..., half_dim:]
    return jnp.concatenate(
        [first * cosine - second * sine_part, second * cosine + first * sine_part], axis=-1
    )


def attend(queries, keys, values, allowed):
    mask = allowed[:, None, None, :]
    scores = jnp.einsum("qngh,knh->qngk", queries, keys, preferred_element_type=jnp.float32)
    scores = jnp.where(mask, scores, masked_score)
    best = jnp.max(scores, axis=-1)
    weights = jnp.where(mask, jnp.exp(scores - best[..., None]), 0.0)
    weight_sum = jnp.sum(weights, axis=-1)
    numer = jnp.einsum(
        "qngk,knh->qngh", weights.astype(jnp.bfloat16), values, preferred_element_type=jnp.float32
    )
    safe_sum = jnp.where(weight_sum > 0.0, weight_sum, 1.0)
    shares = (numer / safe_sum[..., None]).astype(jnp.bfloat16)
    return (best, weight_sum, shares)


def merge(carry_state, best, weight_sum, shares):
    running, denom, accum = carry_state
    highest = jnp.maximum(running, jnp.max(best, axis=1))
    scale_old = jnp.exp(running - highest)
    weight = weight_sum * jnp.exp(best - highest[:, None])
    denom = jnp.sum(weight, axis=1)
    accum = jnp.sum(weight[..., None] * shares.astype(jnp.float32), axis=1)
    return (highest, denom, accum)


def on_device(tokens, pre_gain, w_qkv, w_out, cache_keys, cache_values, cache_len):
    tok_rows = tokens.shape[0]
    seq_count = lax.axis_size("seq")
    seq_index = lax.axis_index("seq")
    heads_all = 2 * KV_DEV * lax.axis_size("fsdp")
    new_rows = tok_rows * seq_count
    pre_rows = cache_keys.shape[0]
    length = cache_len[0]
    hidden = tokens.astype(jnp.float32)
    normed = (
        hidden * lax.rsqrt(jnp.mean(hidden * hidden, axis=-1, keepdims=True) + epsilon) * pre_gain
    ).astype(jnp.bfloat16)
    qkv_full, out_full = (
        lax.all_gather(w_qkv, "seq", axis=0, tiled=True),
        lax.all_gather(w_out, "seq", axis=1, tiled=True),
    )
    projected = jnp.dot(normed, qkv_full, preferred_element_type=jnp.float32)
    projected = projected.reshape(tok_rows, KV_DEV, 4, HEAD)
    positions = length + seq_index * tok_rows + jnp.arange(tok_rows, dtype=jnp.int32)
    queries = (rotate(projected[:, :, 0:2], positions) * (D // heads_all) ** (-0.5)).astype(
        jnp.bfloat16
    )
    new_keys = rotate(projected[:, :, 2], positions).astype(jnp.bfloat16)
    new_values = projected[:, :, 3].astype(jnp.bfloat16)
    flat_queries = queries.reshape(tok_rows, KV_DEV * 2 * HEAD)
    all_queries = lax.all_gather(flat_queries, "seq", axis=0, tiled=True).reshape(
        new_rows, KV_DEV, 2, HEAD
    )
    key_cache = cache_keys.reshape(pre_rows, KV_DEV, HEAD)
    value_cache = cache_values.reshape(pre_rows, KV_DEV, HEAD)
    slot_index = seq_index * pre_rows + jnp.arange(pre_rows, dtype=jnp.int32)
    prefix_usable = slot_index < length
    own_keys = seq_index * tok_rows + jnp.arange(tok_rows, dtype=jnp.int32)
    rows_each = min(512, new_rows)
    block_count = new_rows // rows_each
    query_blocks = all_queries.reshape(block_count, rows_each, KV_DEV, 2, HEAD)
    block_starts = jnp.arange(block_count, dtype=jnp.int32) * rows_each
    start_state = (
        jnp.full((tok_rows, KV_DEV, 2), masked_score, jnp.float32),
        jnp.zeros((tok_rows, KV_DEV, 2), jnp.float32),
        jnp.zeros((tok_rows, KV_DEV, 2, HEAD), jnp.float32),
    )

    def both_parts(items):
        query_block, first_row = items
        allowed = jnp.broadcast_to(prefix_usable[None, :], (rows_each, pre_rows))
        prefix_part = attend(query_block, key_cache, value_cache, allowed)
        query_index = first_row + jnp.arange(rows_each, dtype=jnp.int32)
        causal_mask = own_keys[None, :] <= query_index[:, None]
        new_part = attend(query_block, new_keys, new_values, causal_mask)
        return tuple(
            (jnp.stack([older, newer], axis=1) for older, newer in zip(prefix_part, new_part))
        )

    best, weight_sum, shares = lax.map(both_parts, (query_blocks, block_starts))
    stacked = 2
    carry_state = start_state
    best = best.reshape(new_rows, stacked, KV_DEV * 2)
    weight_sum = weight_sum.reshape(new_rows, stacked, KV_DEV * 2)
    shares = shares.reshape(new_rows, stacked, KV_DEV * 2 * HEAD)
    best, weight_sum = (
        lax.all_to_all(best, "seq", split_axis=0, concat_axis=1, tiled=True),
        lax.all_to_all(weight_sum, "seq", split_axis=0, concat_axis=1, tiled=True),
    )
    shares = lax.all_to_all(shares, "seq", split_axis=0, concat_axis=1, tiled=True)
    carry_state = merge(
        carry_state,
        best.reshape(tok_rows, -1, KV_DEV, 2),
        weight_sum.reshape(tok_rows, -1, KV_DEV, 2),
        shares.reshape(tok_rows, -1, KV_DEV, 2, HEAD),
    )
    attention = (
        (carry_state[2] / carry_state[1][..., None])
        .astype(jnp.bfloat16)
        .reshape(tok_rows, KV_DEV * 2 * HEAD)
    )
    terms = jnp.dot(attention, out_full, preferred_element_type=jnp.float32)
    summed = lax.psum_scatter(terms, "fsdp", scatter_dimension=1, tiled=True)
    width_dev = summed.shape[1]
    residual = lax.dynamic_slice_in_dim(hidden, lax.axis_index("fsdp") * width_dev, width_dev, 1)
    return (residual + summed).astype(jnp.bfloat16)


def solution(mesh):
    return jax.shard_map(
        on_device,
        mesh=mesh,
        in_specs=(
            P("seq", None),
            P(),
            P("seq", "fsdp"),
            P("fsdp", "seq"),
            P("seq", "fsdp"),
            P("seq", "fsdp"),
            P(),
        ),
        out_specs=P("seq", "fsdp"),
        check_vma=False,
    )
```

profile of v0, /device:TPU:24, one launch (start us, length us, event | category | flops | bytes accessed | tf_op | source)
XLA Modules:
  0.0 434.6 jit_solution(6101716325837757610)
XLA Ops:
  9.5 72.2 %all-gather.4.cloned.1.call-done = bf16[4608,512]{1,0:T(8,128)(2,1)} async-done(((bf16[144,512]{1,0:T(8,128)(2,1)}), bf16[4608,512]{1,0:T(8,128)(2,1)}) %all-gather.4.cloned.1.call-update) | async-done | bytes 4718608 | tf_op jit(solution)/shard_map/all_gather | solution.py:67
  81.7 3.5 fusion.36
  86.8 62.7 %all-gather.6.cloned.1.call-done = bf16[2048,256]{1,0:T(8,128)(2,1)} async-done(((bf16[64,256]{1,0:T(8,128)(2,1)}), bf16[2048,256]{1,0:T(8,128)(2,1)}) %all-gather.6.cloned.1.call-update) | async-done | bytes 1048592 | tf_op jit(solution)/shard_map/all_gather | solution.py:79
  150.8 21.3 %while.15 = (s32[]{:T(128)}, f32[4,512,2,1,2]{1,4,2,3,0:T(2,128)S(1)}, f32[4,512,2,1,2]{1,4,2,3,0:T(2,128)S(1)}, bf16[4,512,2,1,2,128]{5,4,2,1,0,3:T(2,128)(2,1)...) while((s32[]{:T(128)}, ...), condition=%wide.region_6.7_spmd.clone, body=%wide.region_1.6_spmd.clone.sunk | while | flops 171217984 | bytes 7993513 | solution.py:108
  165.5 1.4 copy_dynamic-update-slice_fusion.2
  170.8 1.4 copy_dynamic-update-slice_fusion.2
  173.3 3.5 reshape.409
  176.8 6.5 %all-to-all-start.1 = ((f32[32,1,256]{2,1,0:T(1,128)}), f32[32,1,256]{2,1,0:T(1,128)S(1)}, u32[]{:S(2)}, u32[]{:S(2)}) async-start(f32[32,1,256]{2,1,0:T(1,128)} %reshape.409), calls=%async_computation.1 | async-start | bytes 65536 | tf_op jit(solution)/shard_map/all_to_all | solution.py:115
  184.4 3.5 reshape.407
  189.3 6.4 %all-to-all-start = ((f32[32,1,256]{2,1,0:T(1,128)}), f32[32,1,256]{2,1,0:T(1,128)S(1)}, u32[]{:S(2)}, u32[]{:S(2)}) async-start(f32[32,1,256]{2,1,0:T(1,128)} %reshape.407), calls=%async_computation | async-start | bytes 65536 | tf_op jit(solution)/shard_map/all_to_all | solution.py:116
  195.7 6.8 %reshape.404 = bf16[2048,2,256]{2,1,0:T(2,128)(2,1)} reshape(bf16[4,512,2,1,2,128]{5,4,2,1,0,3:T(2,128)(2,1)} %get-tuple-element.71) | data formatting | bytes 4194304 | tf_op jit(solution)/shard_map/reshape | solution.py:113
  202.4 7.7 %all-to-all-start.2 = ((bf16[2048,2,256]{2,1,0:T(2,128)(2,1)}), bf16[2048,2,256]{2,1,0:T(2,128)(2,1)S(1)}, u32[]{:S(2)}, u32[]{:S(2)}) async-start(bf16[2048,2,256]{2,1,0:T(2,128)(2,1)} %reshape.404), calls=%async_computation.2 | async-start | bytes 4194304 | tf_op jit(solution)/shard_map/all_to_all | solution.py:118
  212.4 4.6 %reshape.410 = f32[2048,2,2]{2,1,0:T(2,128)} reshape(f32[32,256]{1,0:T(8,128)S(1)} %reduce.9) | data formatting | bytes 65536
  216.9 2.8 copy.45
  220.5 4.6 %reshape.408 = f32[2048,2,2]{2,1,0:T(2,128)} reshape(f32[32,256]{1,0:T(8,128)S(1)} %reduce.8) | data formatting | bytes 65536
  225.1 2.8 copy.42
  228.0 2.0 copy.46
  230.0 8.3 %mul.179 = f32[64,64,2,128]{3,2,0,1:T(2,128)} broadcast(f32[64,64,2]{2,0,1:T(8,128)} %copy.46), dimensions={0,1,2} | broadcast | bytes 4227072 | tf_op jit(solution)/shard_map/mul | solution.py:50
  238.3 6.4 %mul.180 = f32[64,32,2,256]{3,0,2,1:T(8,128)} reshape(f32[64,64,2,128]{3,2,0,1:T(2,128)} %mul.179) | data formatting | bytes 8388608 | tf_op jit(solution)/shard_map/mul | solution.py:50
  244.9 18.7 %all-to-all-done.2 = bf16[2048,2,256]{2,1,0:T(2,128)(2,1)S(1)} async-done(((bf16[2048,2,256]{2,1,0:T(2,128)(2,1)}), bf16[2048,2,256]{2,1,0:T(2,128)(2,1)S(1)}, u32[]{:S(2)}, u32[]{:S(2)}) %all-to-all-start.2) | async-done | bytes 2097184 | tf_op jit(solution)/shard_map/all_to_all | solution.py:118
  264.2 1.6 copy-done
  266.9 18.1 %all-gather.8.cloned.1.call-done = bf16[256,4608]{0,1:T(8,128)(2,1)} async-done(((bf16[256,144]{0,1:T(8,128)(2,1)}), bf16[256,4608]{0,1:T(8,128)(2,1)}) %all-gather.8.cloned.1.call-update) | async-done | bytes 2359312 | tf_op jit(solution)/shard_map/all_gather | solution.py:68
  285.1 3.8 convolution_bitcast_fusion.4
  290.1 136.2 %reduce-scatter.4.cloned.1.call-done = f32[288,64]{1,0:T(8,128)} async-done(((f32[4608,64]{1,0:T(8,128)}), f32[288,64]{1,0:T(8,128)}) %reduce-scatter.4.cloned.1.call-update) | async-done | bytes 73744
  (119 shorter events, 34.6 us)
Async XLA Ops:
  6.5 75.2 %all-gather.4.cloned.1.call-start = ((), (), s32[]{:S(2)}) async-start(), calls=%async_computation.4 | async-start | bytes 4866048 | tf_op jit(solution)/shard_map/all_gather | solution.py:67
  7.3 142.2 %all-gather.6.cloned.1.call-start = ((), (), s32[]{:S(2)}) async-start(), calls=%async_computation.5 | async-start | bytes 1081344 | tf_op jit(solution)/shard_map/all_gather | solution.py:79
  85.3 65.6 %copy-start.2 = (bf16[256,128]{1,0:T(8,128)(2,1)S(1)}, bf16[256,128]{1,0:T(8,128)(2,1)}, u32[]{:S(2)}) copy-start(bf16[256,128]{1,0:T(8,128)(2,1)} %param.13) | copy-start | bytes 196612
  85.3 65.6 %copy-start.3 = (bf16[256,128]{1,0:T(8,128)(2,1)S(1)}, bf16[256,128]{1,0:T(8,128)(2,1)}, u32[]{:S(2)}) copy-start(bf16[256,128]{1,0:T(8,128)(2,1)} %param.14) | copy-start | bytes 196612
  176.8 12.4 %all-to-all-start.1 = ((f32[32,1,256]{2,1,0:T(1,128)}), f32[32,1,256]{2,1,0:T(1,128)S(1)}, u32[]{:S(2)}, u32[]{:S(2)}) async-start(f32[32,1,256]{2,1,0:T(1,128)} %reshape.409), calls=%async_computation.1 | async-start | bytes 65536 | tf_op jit(solution)/shard_map/all_to_all | solution.py:115
  189.3 13.2 %all-to-all-start = ((f32[32,1,256]{2,1,0:T(1,128)}), f32[32,1,256]{2,1,0:T(1,128)S(1)}, u32[]{:S(2)}, u32[]{:S(2)}) async-start(f32[32,1,256]{2,1,0:T(1,128)} %reshape.407), calls=%async_computation | async-start | bytes 65536 | tf_op jit(solution)/shard_map/all_to_all | solution.py:116
  202.4 61.1 %all-to-all-start.2 = ((bf16[2048,2,256]{2,1,0:T(2,128)(2,1)}), bf16[2048,2,256]{2,1,0:T(2,128)(2,1)S(1)}, u32[]{:S(2)}, u32[]{:S(2)}) async-start(bf16[2048,2,256]{2,1,0:T(2,128)(2,1)} %reshape.404), calls=%async_computation.2 | async-start | bytes 4194304 | tf_op jit(solution)/shard_map/all_to_all | solution.py:118
  210.2 74.8 %all-gather.8.cloned.1.call-start = ((), (), s32[]{:S(2)}) async-start(), calls=%async_computation.6 | async-start | bytes 2433024 | tf_op jit(solution)/shard_map/all_gather | solution.py:68
  210.9 215.4 %reduce-scatter.4.cloned.1.call-start = ((), (), s32[]{:S(2)}) async-start(), calls=%async_computation.7 | async-start | bytes 2506752
  263.6 2.2 copy-start
  288.9 1.1 copy-start.1
Sparse Core Ops, SparseCore 0:
  9.5 72.1 all-gather.3
  86.4 62.9 all-gather.5
  213.2 71.7 all-gather.7
  289.1 137.1 reduce-scatter.3
where the time goes:
time: 436 us; the launch traced here: 435 us
  waiting for transfers between devices  311 us (71%)
  local copies, waits for them, and re-layouts  62.5 us (14%)
  starting transfers between devices  20.9 us (5%)
  between operations  14.1 us (3%)
  other arithmetic  13.3 us (3%)
  matrix products  12.7 us (3%)
    unnamed x5, waiting for transfers between devices  138 us
    all_gather x1, waiting for transfers between devices, on_device(): lax.all_gather(w_qkv, 'seq', axis=0, tiled=True)  72.2 us
    all_gather x1, waiting for transfers between devices, on_device(): lax.all_gather(flat_queries, 'seq', axis=0, tiled=True)  62.7 us
    unnamed x16, local copies, waits for them, and re-layouts  20.4 us
    all_to_all x1, waiting for transfers between devices, on_device(): lax.all_to_all(shares, 'seq', split_axis=0, concat_axis=1, tiled=True)  18.7 us
    all_gather x1, waiting for transfers between devices, on_device(): lax.all_gather(w_out, 'seq', axis=1, tiled=True)  18.1 us
    mul x2, local copies, waits for them, and re-layouts, merge(): accum = jnp.sum(weight[..., None] * shares.astype(jnp.float32), axis=1)  14.7 us
  transfers between devices with their start and end apart: 7, of which 6 were waited for; matrix products, arithmetic and copies ran while one was open for 11% of the time, Pallas kernels for 0%

commit v1 on v0

v1 whole, which is shorter than its diff:
```python
import jax
import jax.numpy as jnp
from jax import lax
from jax.experimental import pallas as pl
from jax.experimental.pallas import tpu as pltpu
from jax.sharding import Mesh, PartitionSpec as P

D = 4608
HEAD = 128
HEADS = 32
NZ, NY, NC, NW, NX = 4, 4, 2, 4, 4
SEQ = ("z", "y", "c")
FSDP = ("w", "x")

masked_score = -1e30
epsilon = 1e-06
VMEM_BYTES = 40 * 1024 * 1024


def rotate(values, cosine, sine_part):
    half_dim = values.shape[-1] // 2
    first = values[..., :half_dim]
    second = values[..., half_dim:]
    return jnp.concatenate(
        [first * cosine - second * sine_part, second * cosine + first * sine_part], axis=-1
    )


def copies(x, count):
    return jnp.broadcast_to(x[None], (count,) + x.shape)


def exchange(x, axis):
    return lax.all_to_all(x, axis, 0, 0, tiled=True)


def swap_core(x):
    return lax.ppermute(x, "c", [(0, 1), (1, 0)])


def block_result(query, keys, values, allowed):
    scores = lax.dot_general(
        query, keys, (((1,), (1,)), ((), ())), preferred_element_type=jnp.float32
    )
    scores = jnp.where(allowed, scores, masked_score)
    best = jnp.max(scores, axis=-1, keepdims=True)
    weights = jnp.where(allowed, jnp.exp(scores - best), 0.0)
    total = jnp.sum(weights, axis=-1, keepdims=True)
    numer = jnp.dot(weights.astype(jnp.bfloat16), values, preferred_element_type=jnp.float32)
    safe = jnp.where(total > 0.0, total, 1.0)
    share = (numer / safe).astype(jnp.bfloat16)
    return best, total, share


def combine(parts):
    highest = parts[0][0]
    for best, _, _ in parts[1:]:
        highest = jnp.maximum(highest, best)
    denom = 0.0
    accum = 0.0
    for best, total, share in parts:
        factor = jnp.exp(best - highest)
        weight = total * factor
        denom = denom + weight
        accum = accum + weight * share.astype(jnp.float32)
    return highest, denom, accum


def pack_stats(columns):
    rows = columns[0].shape[0]
    lane = lax.broadcasted_iota(jnp.int32, (rows, 128), 1)
    out = jnp.zeros((rows, 128), jnp.float32)
    for i, column in enumerate(columns):
        out = jnp.where(lane == i, column, out)
    return out


ROWS = 128


def prefix_kernel(meta, q_ref, own_ref, other_ref, out_ref):
    length, y, c = meta[0], meta[2], meta[3]
    slots = own_ref.shape[1]
    lane = lax.broadcasted_iota(jnp.int32, (ROWS, slots), 1)
    for chunk in range(q_ref.shape[0] // ROWS):
        rows = slice(chunk * ROWS, (chunk + 1) * ROWS)
        columns = []
        for head in range(2):
            query = q_ref[rows, head * HEAD : (head + 1) * HEAD]
            parts = []
            for source, core in ((own_ref, c), (other_ref, 1 - c)):
                for z in range(NZ):
                    start = ((z * NY + y) * NC + core) * slots
                    parts.append(
                        block_result(
                            query, source[z, :, :HEAD], source[z, :, HEAD:], lane < length - start
                        )
                    )
            highest, denom, accum = combine(parts)
            out_ref[rows, head * HEAD : (head + 1) * HEAD] = accum
            columns += [highest, denom]
        out_ref[rows, 2 * HEAD :] = pack_stats(columns)


def new_kernel(meta, q_ref, own_ref, other_ref, state_ref, out_ref):
    my_z, y, c = meta[1], meta[2], meta[3]
    slots = own_ref.shape[1]
    lane = lax.broadcasted_iota(jnp.int32, (ROWS, slots), 1)
    row = lax.broadcasted_iota(jnp.int32, (ROWS, slots), 0)
    for chunk in range(q_ref.shape[0] // ROWS):
        rows = slice(chunk * ROWS, (chunk + 1) * ROWS)
        row_y = (chunk * ROWS + row) // slots
        token = ((my_z * NY + row_y) * NC + c) * slots + row % slots
        offset = token - lane
        columns = []
        for head in range(2):
            lanes = slice(head * HEAD, (head + 1) * HEAD)
            query = q_ref[rows, lanes]
            parts = []
            for source, core in ((own_ref, c), (other_ref, 1 - c)):
                for z in range(NZ):
                    start = ((z * NY + y) * NC + core) * slots
                    parts.append(
                        block_result(
                            query, source[z, :, :HEAD], source[z, :, HEAD:], offset >= start
                        )
                    )
            highest, denom, accum = combine(parts)
            old_highest = state_ref[rows, 2 * HEAD + 2 * head : 2 * HEAD + 2 * head + 1]
            old_denom = state_ref[rows, 2 * HEAD + 2 * head + 1 : 2 * HEAD + 2 * head + 2]
            both = jnp.maximum(highest, old_highest)
            scale = jnp.exp(highest - both)
            old_scale = jnp.exp(old_highest - both)
            out_ref[rows, lanes] = accum * scale + state_ref[rows, lanes] * old_scale
            columns += [both, denom * scale + old_denom * old_scale]
        out_ref[rows, 2 * HEAD :] = pack_stats(columns)


def merge_kernel(state_ref, out_ref):
    for head in range(2):
        lanes = slice(head * HEAD, (head + 1) * HEAD)
        at = 2 * HEAD + 2 * head
        bests = [state_ref[i, :, at : at + 1] for i in range(NY)]
        highest = bests[0]
        for best in bests[1:]:
            highest = jnp.maximum(highest, best)
        denom = 0.0
        accum = 0.0
        for i in range(NY):
            scale = jnp.exp(bests[i] - highest)
            denom = denom + state_ref[i, :, at + 1 : at + 2] * scale
            accum = accum + state_ref[i, :, lanes] * scale
        attention = (accum / denom).astype(jnp.bfloat16)
        for i in range(NW):
            out_ref[i, :, lanes] = attention


def output_kernel(att_ref, weight_ref, residual_ref, out_ref):
    total = jnp.zeros(out_ref.shape, jnp.float32)
    for w in range(NW):
        for x in range(NX):
            total = total + lax.dot_general(
                att_ref[x, w],
                weight_ref[w * NX + x],
                (((1,), (1,)), ((), ())),
                preferred_element_type=jnp.float32,
            )
    out_ref[...] = (residual_ref[...].astype(jnp.float32) + total).astype(jnp.bfloat16)


def call(kernel, shape, dtype, operands, scalars=0, flops=0):
    specs = [pl.BlockSpec(memory_space=pltpu.SMEM)] * scalars
    specs += [pl.BlockSpec(memory_space=pltpu.VMEM)] * (len(operands) - scalars)
    moved = sum(o.size * o.dtype.itemsize for o in operands)
    return pl.pallas_call(
        kernel,
        out_shape=jax.ShapeDtypeStruct(shape, dtype),
        in_specs=specs,
        out_specs=pl.BlockSpec(memory_space=pltpu.VMEM),
        compiler_params=pltpu.CompilerParams(vmem_limit_bytes=VMEM_BYTES),
        cost_estimate=pl.CostEstimate(flops=flops, bytes_accessed=moved, transcendentals=flops // 512),
    )(*operands)


def on_device(tokens, pre_gain, w_qkv, w_out, cache_keys, cache_values, cache_len):
    tok_rows = tokens.shape[0]
    k_rows = w_qkv.shape[0]
    z, y, c = (lax.axis_index(name) for name in SEQ)
    seq_index = (z * NY + y) * NC + c
    fsdp_index = lax.axis_index("w") * NX + lax.axis_index("x")
    length = cache_len[0]
    meta = jnp.stack([length, z, y, c]).astype(jnp.int32)

    moves = [
        (s * 16 + f, (2 * f + s % 2) * 16 + s // 2) for s in range(32) for f in range(16)
    ]
    out_block = lax.ppermute(w_out.T, SEQ + FSDP, moves)
    out_weights = lax.all_gather(out_block, SEQ, axis=0, tiled=True)
    out_weights = out_weights.reshape(NW * NX, -1, 2 * HEAD)

    hidden = tokens.astype(jnp.float32)
    normed = (
        hidden * lax.rsqrt(jnp.mean(hidden * hidden, axis=-1, keepdims=True) + epsilon) * pre_gain
    ).astype(jnp.bfloat16)
    pieces = normed.reshape(tok_rows, NZ, NY, NC, k_rows).transpose(3, 2, 0, 1, 4)
    pieces = pieces.reshape(NC, NY, tok_rows, NZ * k_rows)
    pieces = jnp.where(c == 0, pieces, pieces[::-1])
    sent = pieces.transpose(1, 0, 2, 3)
    rows_in = exchange(sent, "y")
    w_own = exchange(copies(w_qkv, NZ), "z").reshape(NZ * k_rows, -1)
    w_other = swap_core(w_own)
    cache = jnp.concatenate([cache_keys, cache_values], axis=1)
    cache_own = exchange(copies(cache, NZ), "z")
    cache_other = swap_core(cache_own)

    rows_own = rows_in[:, 0].reshape(NY * tok_rows, -1)
    rows_other = rows_in[:, 1].reshape(NY * tok_rows, -1)
    partial = jnp.dot(rows_own, w_own, preferred_element_type=jnp.float32) + jnp.dot(
        rows_other, w_other, preferred_element_type=jnp.float32
    )
    partial = exchange(partial.reshape(NY, tok_rows, -1), "y")
    projected = jnp.sum(partial, axis=0)

    half_dim = HEAD // 2
    inverse_freq = 10000.0 ** (-jnp.arange(half_dim, dtype=jnp.float32) / half_dim)
    positions = length + seq_index * tok_rows + jnp.arange(tok_rows, dtype=jnp.int32)
    angles = positions.astype(jnp.float32)[:, None] * inverse_freq[None, :]
    cosine, sine_part = jnp.cos(angles), jnp.sin(angles)
    heads = [projected[:, i * HEAD : (i + 1) * HEAD] for i in range(4)]
    scale = (D // HEADS) ** (-0.5)
    queries = jnp.concatenate(
        [rotate(heads[0], cosine, sine_part) * scale, rotate(heads[1], cosine, sine_part) * scale],
        axis=1,
    ).astype(jnp.bfloat16)
    new = jnp.concatenate([rotate(heads[2], cosine, sine_part), heads[3]], axis=1).astype(
        jnp.bfloat16
    )
    all_queries = exchange(copies(queries, NY), "y").reshape(NY * tok_rows, -1)
    new_own = exchange(copies(new, NZ), "z")
    new_other = swap_core(new_own)

    state_shape = (NY * tok_rows, 3 * HEAD)
    state = call(
        prefix_kernel,
        state_shape,
        jnp.float32,
        (meta, all_queries, cache_own, cache_other),
        scalars=1,
        flops=4 * 512 * 2048 * 128,
    )
    state = call(
        new_kernel,
        state_shape,
        jnp.float32,
        (meta, all_queries, new_own, new_other, state),
        scalars=1,
        flops=4 * 512 * 512 * 128,
    )
    states = exchange(state.reshape(NY, tok_rows, -1), "y")
    attention = call(merge_kernel, (NW, tok_rows, 2 * HEAD), jnp.bfloat16, (states,))
    attention = exchange(attention, "w")
    attention = exchange(copies(attention, NX), "x")
    width = D // (NW * NX)
    residual = lax.dynamic_slice_in_dim(tokens, fsdp_index * width, width, 1)
    return call(
        output_kernel,
        (tok_rows, width),
        jnp.bfloat16,
        (attention, out_weights, residual),
        flops=2 * 64 * 4096 * 288,
    )


def solution(mesh):
    fine = Mesh(mesh.devices.reshape(NZ, NY, NC, NW, NX), SEQ + FSDP)
    return jax.shard_map(
        on_device,
        mesh=fine,
        in_specs=(
            P(SEQ, None),
            P(),
            P(SEQ, FSDP),
            P(FSDP, SEQ),
            P(SEQ, FSDP),
            P(SEQ, FSDP),
            P(),
        ),
        out_specs=P(SEQ, FSDP),
        check_vma=False,
    )
```

time: 436 us -> 175 us (0.40)
  waiting for transfers between devices: 311 us -> 36.1 us
  local copies, waits for them, and re-layouts: 62.5 us -> 10.2 us
  blocking collectives: 0 us -> 48.4 us
  starting transfers between devices: 20.9 us -> 49.7 us
  matrix products: 12.7 us -> 1.54 us
  other arithmetic: 13.3 us -> 3.21 us
  Pallas kernels: 0 us -> 9.34 us
    all_gather x3 -> x1, waiting for transfers between devices: 153 us -> 0.01 us  [on_device(): out_weights = lax.all_gather(out_block, SEQ, axis=0, tiled=True)]
    unnamed x5 -> x1, waiting for transfers between devices: 138 us -> 0.02 us
    all_to_all x0 -> x3, blocking collectives: none -> 48.4 us  [exchange(): return lax.all_to_all(x, axis, 0, 0, tiled=True)]
    unnamed x16 -> x12, local copies, waits for them, and re-layouts: 20.4 us -> 2.31 us
    all_to_all x3 -> x6, starting transfers between devices: 20.6 us -> 37.8 us  [exchange(): return lax.all_to_all(x, axis, 0, 0, tiled=True)]
    mul x3 -> x0, local copies, waits for them, and re-layouts: 16.8 us -> none  [the longest x2 14.7 us: merge(): accum = jnp.sum(weight[..., None] * shares.astype(jnp.float32), axis=1)]
    ppermute x0 -> x4, starting transfers between devices: none -> 11.9 us  [the longest x1 6.17 us: on_device(): out_block = lax.ppermute(w_out.T, SEQ + FSDP, moves)]
    all_to_all x3 -> x6, waiting for transfers between devices: 20 us -> 30.4 us  [exchange(): return lax.all_to_all(x, axis, 0, 0, tiled=True)]
  transfers between devices with their start and end apart: 7 -> 11, of which waited for: 6 -> 8; matrix products, arithmetic and copies ran while one was open for 11% -> 4% of each run, Pallas kernels for 0% -> 5%
where the time goes in v1:
time: 175 us; the launch traced here: 173 us
  starting transfers between devices  49.7 us (28%)
  blocking collectives  48.4 us (28%)
  waiting for transfers between devices  36.1 us (21%)
  between operations  14.3 us (8%)
  local copies, waits for them, and re-layouts  10.2 us (6%)
  Pallas kernels  9.34 us (5%)
  other arithmetic  3.21 us (2%)
    all_to_all x3, blocking collectives, exchange(): return lax.all_to_all(x, axis, 0, 0, tiled=True)  48.4 us
    all_to_all x6, starting transfers between devices, exchange(): return lax.all_to_all(x, axis, 0, 0, tiled=True)  37.8 us
    all_to_all x6, waiting for transfers between devices, exchange(): return lax.all_to_all(x, axis, 0, 0, tiled=True)  30.4 us
    pallas_call x4, Pallas kernels, call(): pl.pallas_call(kernel, out_shape=jax.ShapeDtypeStruct(shape, dtype), in_s...  9.34 us
    ppermute x1, starting transfers between devices, on_device(): out_block = lax.ppermute(w_out.T, SEQ + FSDP, moves)  6.17 us
    ppermute x3, starting transfers between devices, swap_core(): return lax.ppermute(x, 'c', [(0, 1), (1, 0)])  5.74 us
    ppermute x1, waiting for transfers between devices, on_device(): out_block = lax.ppermute(w_out.T, SEQ + FSDP, moves)  4.12 us
    broadcast_in_dim x5, local copies, waits for them, and re-layouts, copies(): return jnp.broadcast_to(x[None], (count,) + x.shape)  3.9 us
  transfers between devices with their start and end apart: 11, of which 8 were waited for; matrix products, arithmetic and copies ran while one was open for 4% of the time, Pallas kernels for 5%

profile of v1, /device:TPU:24, one launch (start us, length us, event | category | flops | bytes accessed | tf_op | source)
XLA Modules:
  0.0 172.7 jit_solution(9391871130393805072)
XLA Ops:
  9.1 1.8 %reshape.89 = bf16[64,4,4,2,144]{4,3,2,1,0:T(2,128)(2,1)S(1)} reshape(bf16[64,4608]{1,0:T(8,128)(2,1)S(1)} %fusion.2) | data formatting | bytes 1179648 | tf_op jit(solution)/shard_map/reshape | solution.py:205
  12.2 14.7 %all_to_all.45 = bf16[4,2,64,576]{3,2,1,0:T(8,128)(2,1)S(1)} all-to-all(bf16[4,2,64,576]{3,2,1,0:T(8,128)(2,1)S(1)} %copy.10), channel_id=1, replica_groups=mesh['z'=4,'y'=4,'c'=2,'w'=4,'x'=4] {'y'}, dimensions={0} | all-to-all | bytes 1179648 | tf_op jit(solution)/shard_map/all_to_all | solution.py:34
  27.8 4.5 %all-to-all-start.1 = ((bf16[4,144,512]{2,1,0:T(8,128)(2,1)}), bf16[4,144,512]{2,1,0:T(8,128)(2,1)S(1)}, u32[]{:S(2)}, u32[]{:S(2)}) async-start(bf16[4,144,512]{2,1,0:T(8,128)(2,1)} %broadcast_in_dim.10), calls=%async_computation.1 | async-start | bytes 1179648 | tf_op jit(solution)/shard_map/all_to_all | solution.py:34
  32.3 6.2 %collective-permute-start.3 = (bf16[144,256]{1,0:T(8,128)(2,1)S(1)}, bf16[144,256]{1,0:T(8,128)(2,1)S(1)}, u32[]{:S(2)}, u32[]{:S(2)}) collective-permute-start(bf16[144,256]{1,0:T(8,128)(2,1)S(1)} %bitcast.31), channel_id=1, source_target_pairs={{0,0},{1,32},{2,64},{3,96},{4,128},{5,160},{6,192},{7,224},{8,256}... | collective-permute-start | bytes 221192 | tf_op jit(solution)/shard_map/ppermute | solution.py:197
  38.5 4.1 %collective-permute-done.3 = bf16[144,256]{1,0:T(8,128)(2,1)S(1)} collective-permute-done((bf16[144,256]{1,0:T(8,128)(2,1)S(1)}, bf16[144,256]{1,0:T(8,128)(2,1)S(1)}, u32[]{:S(2)}, u32[]{:S(2)}) %collective-permute-start.3) | collective-permute-done | bytes 73760 | tf_op jit(solution)/shard_map/ppermute | solution.py:197
  43.3 5.3 %all-to-all-done.1 = bf16[4,144,512]{2,1,0:T(8,128)(2,1)S(1)} async-done(((bf16[4,144,512]{2,1,0:T(8,128)(2,1)}), bf16[4,144,512]{2,1,0:T(8,128)(2,1)S(1)}, u32[]{:S(2)}, u32[]{:S(2)}) %all-to-all-start.1) | async-done | bytes 589856 | tf_op jit(solution)/shard_map/all_to_all | solution.py:34
  49.4 15.0 %all-to-all-start.5 = ((bf16[4,256,256]{2,1,0:T(8,128)(2,1)}), bf16[4,256,256]{2,1,0:T(8,128)(2,1)S(1)}, u32[]{:S(2)}, u32[]{:S(2)}) async-start(bf16[4,256,256]{2,1,0:T(8,128)(2,1)} %broadcast_in_dim.13), calls=%async_computation.5 | async-start | bytes 1048576 | tf_op jit(solution)/shard_map/all_to_all | solution.py:34
  64.4 1.9 %collective-permute-start = (bf16[576,512]{1,0:T(8,128)(2,1)S(1)}, bf16[576,512]{1,0:T(8,128)(2,1)S(1)}, u32[]{:S(2)}, u32[]{:S(2)}) collective-permute-start(bf16[576,512]{1,0:T(8,128)(2,1)S(1)} %bitcast.27), channel_id=1, source_target_pairs={{0,16},{16,0},{1,17},{17,1},{2,18},{18,2},{3,19},{19,3},{4,20},{20... | collective-permute-start | bytes 1769480 | tf_op jit(solution)/shard_map/ppermute | solution.py:38
  69.5 5.7 %all-to-all-done.5.own_ref = bf16[4,256,256]{2,1,0:T(8,128)(2,1)S(1)} async-done(((bf16[4,256,256]{2,1,0:T(8,128)(2,1)}), bf16[4,256,256]{2,1,0:T(8,128)(2,1)S(1)}, u32[]{:S(2)}, u32[]{:S(2)}) %all-to-all-start.5) | async-done | bytes 524320 | tf_op jit(solution)/shard_map/all_to_all | solution.py:34
  75.2 6.0 %all-to-all-start.2 = ((f32[4,64,512]{2,1,0:T(8,128)}), f32[4,64,512]{2,1,0:T(8,128)S(1)}, u32[]{:S(2)}, u32[]{:S(2)}) async-start(f32[4,64,512]{2,1,0:T(8,128)} %bitcast.8), calls=%async_computation.2 | async-start | bytes 1048576 | tf_op jit(solution)/shard_map/all_to_all | solution.py:34
  81.8 1.9 %collective-permute-start.2 = (bf16[4,256,256]{2,1,0:T(8,128)(2,1)S(1)}, bf16[4,256,256]{2,1,0:T(8,128)(2,1)S(1)}, u32[]{:S(2)}, u32[]{:S(2)}) collective-permute-start(bf16[4,256,256]{2,1,0:T(8,128)(2,1)S(1)} %all-to-all-done.5.own_ref), channel_id=1, source_target_pairs={{0,16},{16,0},{1,17},{17,1},{2,18},{18,2},{3,19},{19,3},{4,20},{20... | collective-permute-start | bytes 1572872 | tf_op jit(solution)/shard_map/ppermute | solution.py:38
  83.8 4.4 %all-to-all-done.2 = f32[4,64,512]{2,1,0:T(8,128)S(1)} async-done(((f32[4,64,512]{2,1,0:T(8,128)}), f32[4,64,512]{2,1,0:T(8,128)S(1)}, u32[]{:S(2)}, u32[]{:S(2)}) %all-to-all-start.2) | async-done | bytes 524320 | tf_op jit(solution)/shard_map/all_to_all | solution.py:34
  89.2 3.6 %all-to-all-start.4 = ((bf16[4,64,256]{2,1,0:T(8,128)(2,1)}), bf16[4,64,256]{2,1,0:T(8,128)(2,1)S(1)}, u32[]{:S(2)}, u32[]{:S(2)}) async-start(bf16[4,64,256]{2,1,0:T(8,128)(2,1)} %broadcast_in_dim.12), calls=%async_computation.4 | async-start | bytes 262144 | tf_op jit(solution)/shard_map/all_to_all | solution.py:34
  92.9 5.8 %all-to-all-done.4.own_ref = bf16[4,64,256]{2,1,0:T(8,128)(2,1)S(1)} async-done(((bf16[4,64,256]{2,1,0:T(8,128)(2,1)}), bf16[4,64,256]{2,1,0:T(8,128)(2,1)S(1)}, u32[]{:S(2)}, u32[]{:S(2)}) %all-to-all-start.4) | async-done | bytes 131104 | tf_op jit(solution)/shard_map/all_to_all | solution.py:34
  99.4 5.2 %all-to-all-start.3 = ((bf16[4,64,256]{2,1,0:T(8,128)(2,1)}), bf16[4,64,256]{2,1,0:T(8,128)(2,1)S(1)}, u32[]{:S(2)}, u32[]{:S(2)}) async-start(bf16[4,64,256]{2,1,0:T(8,128)(2,1)} %broadcast_in_dim.11), calls=%async_computation.3 | async-start | bytes 262144 | tf_op jit(solution)/shard_map/all_to_all | solution.py:34
  104.7 1.9 %collective-permute-start.1 = (bf16[4,64,256]{2,1,0:T(8,128)(2,1)S(1)}, bf16[4,64,256]{2,1,0:T(8,128)(2,1)S(1)}, u32[]{:S(2)}, u32[]{:S(2)}) collective-permute-start(bf16[4,64,256]{2,1,0:T(8,128)(2,1)S(1)} %all-to-all-done.4.own_ref), channel_id=1, source_target_pairs={{0,16},{16,0},{1,17},{17,1},{2,18},{18,2},{3,19},{19,3},{4,20},{20... | collective-permute-start | bytes 393224 | tf_op jit(solution)/shard_map/ppermute | solution.py:38
  106.7 2.1 %all-to-all-done.3 = bf16[4,64,256]{2,1,0:T(8,128)(2,1)S(1)} async-done(((bf16[4,64,256]{2,1,0:T(8,128)(2,1)}), bf16[4,64,256]{2,1,0:T(8,128)(2,1)S(1)}, u32[]{:S(2)}, u32[]{:S(2)}) %all-to-all-start.3) | async-done | bytes 131104 | tf_op jit(solution)/shard_map/all_to_all | solution.py:34
  108.7 3.3 %shard_map.73.state_ref = f32[256,384]{1,0:T(8,128)S(1)} custom-call(s32[4]{0:T(128)S(1)} %pad_add_fusion.meta, bf16[256,256]{1,0:T(8,128)(2,1)S(1)} %bitcast.24, bf16[4,256,256]{2,1,0:T(8,128)(2,1)S(1)} %all-to-all-done.5.own_ref, bf16[4,256,256]{2,1,0:T(8,128)(2,1)S(1)} %collective-permute-done.2.other_ref), custom_call_target="tpu_custom_call" | custom-call | flops 536870912 | bytes 1179664 | tf_op jit(solution)/shard_map/pallas_call | solution.py:175
  112.0 4.2 %shard_map.74 = f32[256,384]{1,0:T(8,128)S(1)} custom-call(s32[4]{0:T(128)S(1)} %pad_add_fusion.meta, bf16[256,256]{1,0:T(8,128)(2,1)S(1)} %bitcast.25, bf16[4,64,256]{2,1,0:T(8,128)(2,1)S(1)} %all-to-all-done.4.own_ref, bf16[4,64,256]{2,1,0:T(8,128)(2,1)S(1)} %collective-permute-done.1.other_ref, f32[256,384]{1,0:T(8,128)S(1)} %shard_map.73.state_ref), custom_call_target="tpu_custom_call" | custom-call | flops 134217728 | bytes 786448 | tf_op jit(solution)/shard_map/pallas_call | solution.py:175
  116.3 9.9 %all_to_all.46.state_ref = f32[4,64,384]{2,1,0:T(8,128)S(1)} all-to-all(f32[4,64,384]{2,1,0:T(8,128)S(1)} %bitcast.23), channel_id=1, replica_groups=mesh['z'=4,'y'=4,'c'=2,'w'=4,'x'=4] {'y'}, dimensions={0} | all-to-all | bytes 786432 | tf_op jit(solution)/shard_map/all_to_all | solution.py:34
  126.5 23.8 %all_to_all.47 = bf16[4,64,256]{2,1,0:T(8,128)(2,1)S(1)} all-to-all(bf16[4,64,256]{2,1,0:T(8,128)(2,1)S(1)} %shard_map.75), channel_id=1, replica_groups=mesh['z'=4,'y'=4,'c'=2,'w'=4,'x'=4] {'w'}, dimensions={0} | all-to-all | bytes 262144 | tf_op jit(solution)/shard_map/all_to_all | solution.py:34
  151.2 3.5 %all-to-all-start.8 = ((bf16[4,4,64,256]{3,2,1,0:T(8,128)(2,1)}), bf16[4,4,64,256]{3,2,1,0:T(8,128)(2,1)S(1)}, u32[]{:S(2)}, u32[]{:S(2)}) async-start(bf16[4,4,64,256]{3,2,1,0:T(8,128)(2,1)} %broadcast_in_dim.14), calls=%async_computation.8 | async-start | bytes 1048576 | tf_op jit(solution)/shard_map/all_to_all | solution.py:34
  155.6 7.1 %all-to-all-done.8.att_ref = bf16[4,4,64,256]{3,2,1,0:T(8,128)(2,1)S(1)} async-done(((bf16[4,4,64,256]{3,2,1,0:T(8,128)(2,1)}), bf16[4,4,64,256]{3,2,1,0:T(8,128)(2,1)S(1)}, u32[]{:S(2)}, u32[]{:S(2)}) %all-to-all-start.8) | async-done | bytes 524320 | tf_op jit(solution)/shard_map/all_to_all | solution.py:34
  162.7 1.7 copy-done
  (45 shorter events, 14.8 us)
Async XLA Ops:
  12.1 14.8 %copy-start.1 = (bf16[144,512]{1,0:T(8,128)(2,1)S(1)}, bf16[144,512]{1,0:T(8,128)(2,1)}, u32[]{:S(2)}) copy-start(bf16[144,512]{1,0:T(8,128)(2,1)} %param.9) | copy-start | bytes 442372
  26.9 5.4 %copy-start.5 = (bf16[256,144]{0,1:T(8,128)(2,1)S(1)}, bf16[256,144]{0,1:T(8,128)(2,1)}, u32[]{:S(2)}) copy-start(bf16[256,144]{0,1:T(8,128)(2,1)} %param.10) | copy-start | bytes 221188
  26.9 16.3 %copy-start.3 = (bf16[256,128]{1,0:T(8,128)(2,1)S(1)}, bf16[256,128]{1,0:T(8,128)(2,1)}, u32[]{:S(2)}) copy-start(bf16[256,128]{1,0:T(8,128)(2,1)} %param.12) | copy-start | bytes 196612
  27.0 16.3 %copy-start.4 = (bf16[256,128]{1,0:T(8,128)(2,1)S(1)}, bf16[256,128]{1,0:T(8,128)(2,1)}, u32[]{:S(2)}) copy-start(bf16[256,128]{1,0:T(8,128)(2,1)} %param.11) | copy-start | bytes 196612
  27.8 20.8 %all-to-all-start.1 = ((bf16[4,144,512]{2,1,0:T(8,128)(2,1)}), bf16[4,144,512]{2,1,0:T(8,128)(2,1)S(1)}, u32[]{:S(2)}, u32[]{:S(2)}) async-start(bf16[4,144,512]{2,1,0:T(8,128)(2,1)} %broadcast_in_dim.10), calls=%async_computation.1 | async-start | bytes 1179648 | tf_op jit(solution)/shard_map/all_to_all | solution.py:34
  32.3 130.4 %all-gather.2.cloned.1.call-start = ((), (), s32[]{:S(2)}) async-start(), calls=%async_computation.9 | async-start | bytes 2433024 | tf_op jit(solution)/shard_map/all_gather | solution.py:198
  32.3 10.3 %collective-permute-start.3 = (bf16[144,256]{1,0:T(8,128)(2,1)S(1)}, bf16[144,256]{1,0:T(8,128)(2,1)S(1)}, u32[]{:S(2)}, u32[]{:S(2)}) collective-permute-start(bf16[144,256]{1,0:T(8,128)(2,1)S(1)} %bitcast.31), channel_id=1, source_target_pairs={{0,0},{1,32},{2,64},{3,96},{4,128},{5,160},{6,192},{7,224},{8,256}... | collective-permute-start | bytes 221192 | tf_op jit(solution)/shard_map/ppermute | solution.py:197
  42.6 0.6 copy-start.2
  49.4 25.8 %all-to-all-start.5 = ((bf16[4,256,256]{2,1,0:T(8,128)(2,1)}), bf16[4,256,256]{2,1,0:T(8,128)(2,1)S(1)}, u32[]{:S(2)}, u32[]{:S(2)}) async-start(bf16[4,256,256]{2,1,0:T(8,128)(2,1)} %broadcast_in_dim.13), calls=%async_computation.5 | async-start | bytes 1048576 | tf_op jit(solution)/shard_map/all_to_all | solution.py:34
  64.4 3.9 %collective-permute-start = (bf16[576,512]{1,0:T(8,128)(2,1)S(1)}, bf16[576,512]{1,0:T(8,128)(2,1)S(1)}, u32[]{:S(2)}, u32[]{:S(2)}) collective-permute-start(bf16[576,512]{1,0:T(8,128)(2,1)S(1)} %bitcast.27), channel_id=1, source_target_pairs={{0,16},{16,0},{1,17},{17,1},{2,18},{18,2},{3,19},{19,3},{4,20},{20... | collective-permute-start | bytes 1769480 | tf_op jit(solution)/shard_map/ppermute | solution.py:38
  75.2 12.9 %all-to-all-start.2 = ((f32[4,64,512]{2,1,0:T(8,128)}), f32[4,64,512]{2,1,0:T(8,128)S(1)}, u32[]{:S(2)}, u32[]{:S(2)}) async-start(f32[4,64,512]{2,1,0:T(8,128)} %bitcast.8), calls=%async_computation.2 | async-start | bytes 1048576 | tf_op jit(solution)/shard_map/all_to_all | solution.py:34
  81.8 24.8 %collective-permute-start.2 = (bf16[4,256,256]{2,1,0:T(8,128)(2,1)S(1)}, bf16[4,256,256]{2,1,0:T(8,128)(2,1)S(1)}, u32[]{:S(2)}, u32[]{:S(2)}) collective-permute-start(bf16[4,256,256]{2,1,0:T(8,128)(2,1)S(1)} %all-to-all-done.5.own_ref), channel_id=1, source_target_pairs={{0,16},{16,0},{1,17},{17,1},{2,18},{18,2},{3,19},{19,3},{4,20},{20... | collective-permute-start | bytes 1572872 | tf_op jit(solution)/shard_map/ppermute | solution.py:38
  89.2 9.6 %all-to-all-start.4 = ((bf16[4,64,256]{2,1,0:T(8,128)(2,1)}), bf16[4,64,256]{2,1,0:T(8,128)(2,1)S(1)}, u32[]{:S(2)}, u32[]{:S(2)}) async-start(bf16[4,64,256]{2,1,0:T(8,128)(2,1)} %broadcast_in_dim.12), calls=%async_computation.4 | async-start | bytes 262144 | tf_op jit(solution)/shard_map/all_to_all | solution.py:34
  99.4 9.3 %all-to-all-start.3 = ((bf16[4,64,256]{2,1,0:T(8,128)(2,1)}), bf16[4,64,256]{2,1,0:T(8,128)(2,1)S(1)}, u32[]{:S(2)}, u32[]{:S(2)}) async-start(bf16[4,64,256]{2,1,0:T(8,128)(2,1)} %broadcast_in_dim.11), calls=%async_computation.3 | async-start | bytes 262144 | tf_op jit(solution)/shard_map/all_to_all | solution.py:34
  104.7 7.4 %collective-permute-start.1 = (bf16[4,64,256]{2,1,0:T(8,128)(2,1)S(1)}, bf16[4,64,256]{2,1,0:T(8,128)(2,1)S(1)}, u32[]{:S(2)}, u32[]{:S(2)}) collective-permute-start(bf16[4,64,256]{2,1,0:T(8,128)(2,1)S(1)} %all-to-all-done.4.own_ref), channel_id=1, source_target_pairs={{0,16},{16,0},{1,17},{17,1},{2,18},{18,2},{3,19},{19,3},{4,20},{20... | collective-permute-start | bytes 393224 | tf_op jit(solution)/shard_map/ppermute | solution.py:38
  151.2 11.5 %all-to-all-start.8 = ((bf16[4,4,64,256]{3,2,1,0:T(8,128)(2,1)}), bf16[4,4,64,256]{3,2,1,0:T(8,128)(2,1)S(1)}, u32[]{:S(2)}, u32[]{:S(2)}) async-start(bf16[4,4,64,256]{3,2,1,0:T(8,128)(2,1)} %broadcast_in_dim.14), calls=%async_computation.8 | async-start | bytes 1048576 | tf_op jit(solution)/shard_map/all_to_all | solution.py:34
  162.7 1.7 copy-start
Sparse Core Ops, SparseCore 0:
  43.4 78.8 all-gather.1

commit v2 on v1

v2 whole, which is shorter than its diff:
```python
import jax
import jax.numpy as jnp
from jax import lax
from jax.experimental import pallas as pl
from jax.experimental.pallas import tpu as pltpu
from jax.sharding import Mesh, PartitionSpec as P

D = 4608
HEAD = 128
HEADS = 32
NZ, NY, NC, NW, NX = 4, 4, 2, 4, 4
SEQ = ("z", "y", "c")
FSDP = ("w", "x")

masked_score = -1e30
epsilon = 1e-06
VMEM_BYTES = 40 * 1024 * 1024


def exchange(x, axis):
    return lax.all_to_all(x, axis, 0, 0, tiled=True)


def swap_core(x):
    return lax.ppermute(x, "c", [(0, 1), (1, 0)])


def block_result(query, keys, values, allowed):
    scores = lax.dot_general(
        query, keys, (((1,), (1,)), ((), ())), preferred_element_type=jnp.float32
    )
    scores = jnp.where(allowed, scores, masked_score)
    best = jnp.max(scores, axis=-1, keepdims=True)
    weights = jnp.exp(scores - best)
    total = jnp.where(best > 0.5 * masked_score, jnp.sum(weights, axis=-1, keepdims=True), 0.0)
    numer = jnp.dot(weights.astype(jnp.bfloat16), values, preferred_element_type=jnp.float32)
    inverse = 1.0 / jnp.where(total > 0.0, total, 1.0)
    share = (numer * inverse).astype(jnp.bfloat16)
    return best, total, share


def combine(parts):
    highest = parts[0][0]
    for best, _, _ in parts[1:]:
        highest = jnp.maximum(highest, best)
    denom = 0.0
    accum = 0.0
    for best, total, share in parts:
        weight = total * jnp.exp(best - highest)
        denom = denom + weight
        accum = accum + weight * share.astype(jnp.float32)
    return highest, denom, accum


def pack_stats(columns):
    rows = columns[0].shape[0]
    lane = lax.broadcasted_iota(jnp.int32, (rows, 128), 1)
    out = jnp.zeros((rows, 128), jnp.float32)
    for i, column in enumerate(columns):
        out = jnp.where(lane == i, column, out)
    return out


def norm_kernel(meta, tokens_ref, gain_ref, out_ref):
    hidden = tokens_ref[...].astype(jnp.float32)
    mean = jnp.mean(hidden * hidden, axis=-1, keepdims=True)
    normed = (hidden * lax.rsqrt(mean + epsilon) * gain_ref[...]).astype(jnp.bfloat16)
    first = meta[3] == 0
    k_rows = normed.shape[1] // (NZ * NY * NC)
    for y in range(NY):
        for z in range(NZ):
            at = (z * NY + y) * NC * k_rows
            low, high = normed[:, at : at + k_rows], normed[:, at + k_rows : at + 2 * k_rows]
            out_ref[y, 0, :, z * k_rows : (z + 1) * k_rows] = jnp.where(first, low, high)
            out_ref[y, 1, :, z * k_rows : (z + 1) * k_rows] = jnp.where(first, high, low)


def rotary_kernel(part_ref, cos_ref, sin_ref, q_ref, new_ref):
    total = (part_ref[0] + part_ref[1]) + (part_ref[2] + part_ref[3])
    cosine, sine_part = cos_ref[...], sin_ref[...]

    def rotated(i):
        u = total[:, i * HEAD : (i + 1) * HEAD]
        return u * cosine + pltpu.roll(u, HEAD // 2, 1) * sine_part

    scale = (D // HEADS) ** (-0.5)
    q_ref[:, :HEAD] = (rotated(0) * scale).astype(jnp.bfloat16)
    q_ref[:, HEAD:] = (rotated(1) * scale).astype(jnp.bfloat16)
    keys = rotated(2).astype(jnp.bfloat16)
    values = total[:, 3 * HEAD :].astype(jnp.bfloat16)
    for i in range(NZ):
        new_ref[i, :, :HEAD] = keys
        new_ref[i, :, HEAD:] = values


def prefix_kernel(meta, q0, q1, q2, q3, own_ref, other_ref, out_ref):
    length, y, c = meta[0], meta[2], meta[3]
    slots = own_ref.shape[1]
    rows = q0.shape[0]
    lane = lax.broadcasted_iota(jnp.int32, (2 * rows, slots), 1)
    for chunk, (qa, qb) in enumerate(((q0, q1), (q2, q3))):
        columns = []
        places = [lax.rem(y + 2 * chunk + i, NY) for i in range(2)]
        for head in range(2):
            lanes = slice(head * HEAD, (head + 1) * HEAD)
            query = jnp.concatenate([qa[:, lanes], qb[:, lanes]], axis=0)
            parts = []
            for source, core in ((own_ref, c), (other_ref, 1 - c)):
                for z in range(NZ):
                    start = ((z * NY + y) * NC + core) * slots
                    parts.append(
                        block_result(
                            query, source[z, :, :HEAD], source[z, :, HEAD:], lane < length - start
                        )
                    )
            highest, denom, accum = combine(parts)
            for i, place in enumerate(places):
                out_ref[place, :, lanes] = accum[i * rows : (i + 1) * rows]
            columns += [highest, denom]
        stats = pack_stats(columns)
        for i, place in enumerate(places):
            out_ref[place, :, 2 * HEAD :] = stats[i * rows : (i + 1) * rows]


def new_kernel(meta, q0, q1, q2, q3, own_ref, other_ref, state_ref, out_ref):
    my_z, y, c = meta[1], meta[2], meta[3]
    slots = own_ref.shape[1]
    rows = q0.shape[0]
    lane = lax.broadcasted_iota(jnp.int32, (2 * rows, slots), 1)
    row = lax.broadcasted_iota(jnp.int32, (2 * rows, slots), 0)
    for chunk, (qa, qb) in enumerate(((q0, q1), (q2, q3))):
        columns = []
        places = [lax.rem(y + 2 * chunk + i, NY) for i in range(2)]
        bases = [((my_z * NY + place) * NC + c) * slots for place in places]
        offset = jnp.where(row < rows, bases[0] + row, bases[1] + row - rows) - lane
        old_stats = jnp.concatenate([state_ref[place, :, 2 * HEAD :] for place in places], axis=0)
        for head in range(2):
            lanes = slice(head * HEAD, (head + 1) * HEAD)
            query = jnp.concatenate([qa[:, lanes], qb[:, lanes]], axis=0)
            parts = []
            for source, core in ((own_ref, c), (other_ref, 1 - c)):
                for z in range(NZ):
                    start = ((z * NY + y) * NC + core) * slots
                    parts.append(
                        block_result(
                            query, source[z, :, :HEAD], source[z, :, HEAD:], offset >= start
                        )
                    )
            highest, denom, accum = combine(parts)
            old_highest = old_stats[:, 2 * head : 2 * head + 1]
            old_denom = old_stats[:, 2 * head + 1 : 2 * head + 2]
            both = jnp.maximum(highest, old_highest)
            scale = jnp.exp(highest - both)
            old_scale = jnp.exp(old_highest - both)
            accum = accum * scale
            for i, place in enumerate(places):
                part = slice(i * rows, (i + 1) * rows)
                out_ref[place, :, lanes] = (
                    accum[part] + state_ref[place, :, lanes] * old_scale[part]
                )
            columns += [both, denom * scale + old_denom * old_scale]
        stats = pack_stats(columns)
        for i, place in enumerate(places):
            out_ref[place, :, 2 * HEAD :] = stats[i * rows : (i + 1) * rows]


def merge_kernel(state_ref, out_ref):
    for head in range(2):
        lanes = slice(head * HEAD, (head + 1) * HEAD)
        at = 2 * HEAD + 2 * head
        bests = [state_ref[i, :, at : at + 1] for i in range(NY)]
        highest = bests[0]
        for best in bests[1:]:
            highest = jnp.maximum(highest, best)
        denom = 0.0
        accum = 0.0
        for i in range(NY):
            scale = jnp.exp(bests[i] - highest)
            denom = denom + state_ref[i, :, at + 1 : at + 2] * scale
            accum = accum + state_ref[i, :, lanes] * scale
        attention = (accum / denom).astype(jnp.bfloat16)
        for i in range(NW):
            out_ref[i, :, lanes] = attention


def output_kernel(meta, att_ref, own_ref, other_ref, out_ref):
    first = meta[3] == 0
    half = own_ref.shape[2]
    for x in range(NX):
        sums = []
        for source in (own_ref, other_ref):
            total = 0.0
            for w in range(NW):
                total = total + lax.dot_general(
                    att_ref[w],
                    source[x, w],
                    (((1,), (1,)), ((), ())),
                    preferred_element_type=jnp.float32,
                )
            sums.append(total)
        out_ref[x, :, :half] = jnp.where(first, sums[0], sums[1])
        out_ref[x, :, half:] = jnp.where(first, sums[1], sums[0])


def last_kernel(part_ref, residual_ref, out_ref):
    total = (part_ref[0] + part_ref[1]) + (part_ref[2] + part_ref[3])
    out_ref[...] = (residual_ref[...].astype(jnp.float32) + total).astype(jnp.bfloat16)


def call(kernel, out, operands, scalars=0, flops=0):
    specs = [pl.BlockSpec(memory_space=pltpu.SMEM)] * scalars
    specs += [pl.BlockSpec(memory_space=pltpu.VMEM)] * (len(operands) - scalars)
    moved = sum(o.size * o.dtype.itemsize for o in operands)
    shapes = [jax.ShapeDtypeStruct(shape, dtype) for shape, dtype in out]
    results = pl.pallas_call(
        kernel,
        out_shape=shapes,
        in_specs=specs,
        out_specs=[pl.BlockSpec(memory_space=pltpu.VMEM)] * len(out),
        compiler_params=pltpu.CompilerParams(vmem_limit_bytes=VMEM_BYTES),
        cost_estimate=pl.CostEstimate(
            flops=flops, bytes_accessed=moved, transcendentals=flops // 512
        ),
    )(*operands)
    return results if len(out) > 1 else results[0]


def on_device(tokens, pre_gain, w_qkv, w_out, cache_keys, cache_values, cache_len):
    tok_rows = tokens.shape[0]
    k_rows = w_qkv.shape[0]
    bf16, f32 = jnp.bfloat16, jnp.float32
    z, y, c = (lax.axis_index(name) for name in SEQ)
    seq_index = (z * NY + y) * NC + c
    fsdp_index = lax.axis_index("w") * NX + lax.axis_index("x")
    length = cache_len[0]
    meta = jnp.stack([length, z, y, c]).astype(jnp.int32)

    w_own = lax.all_gather(w_qkv, "z", axis=0, tiled=True)
    w_other = swap_core(w_own)
    cache = jnp.concatenate([cache_keys, cache_values], axis=1)
    cache_own = lax.all_gather(cache, "z", axis=0)
    cache_other = swap_core(cache_own)
    trade = [(a * NW + b, b * NW + a) for a in range(NZ) for b in range(NW)]
    out_block = lax.ppermute(w_out.T, ("z", "w"), trade)
    out_block = lax.all_gather(out_block, "z", axis=0)
    out_own = lax.all_gather(out_block, "y", axis=0)
    out_other = swap_core(out_own)

    rows_out = call(
        norm_kernel,
        [((NY, NC, tok_rows, NZ * k_rows), bf16)],
        (meta, tokens, pre_gain.reshape(1, -1)),
        scalars=1,
        flops=tokens.size * 6,
    )
    rows_in = exchange(rows_out, "y")
    rows_own = rows_in[:, 0].reshape(NY * tok_rows, -1)
    rows_other = rows_in[:, 1].reshape(NY * tok_rows, -1)
    partial = jnp.dot(rows_own, w_own, preferred_element_type=f32) + jnp.dot(
        rows_other, w_other, preferred_element_type=f32
    )
    partial = exchange(partial.reshape(NY, tok_rows, -1), "y")

    half_dim = HEAD // 2
    inverse_freq = 10000.0 ** (-jnp.arange(half_dim, dtype=f32) / half_dim)
    positions = length + seq_index * tok_rows + jnp.arange(tok_rows, dtype=jnp.int32)
    angles = positions.astype(f32)[:, None] * inverse_freq[None, :]
    cosine, sine_part = jnp.cos(angles), jnp.sin(angles)
    cosine = jnp.concatenate([cosine, cosine], axis=1)
    sine_part = jnp.concatenate([-sine_part, sine_part], axis=1)
    queries, new = call(
        rotary_kernel,
        [((tok_rows, 2 * HEAD), bf16), ((NZ, tok_rows, 2 * HEAD), bf16)],
        (partial, cosine, sine_part),
    )
    new_own = exchange(new, "z")
    new_other = swap_core(new_own)
    all_queries = [queries] + [
        lax.ppermute(queries, "y", [((i + k) % NY, i) for i in range(NY)]) for k in range(1, NY)
    ]

    state_shape = [((NY, tok_rows, 3 * HEAD), f32)]
    state = call(
        prefix_kernel,
        state_shape,
        (meta, *all_queries, cache_own, cache_other),
        scalars=1,
        flops=4 * 512 * 2048 * 128,
    )
    state = call(
        new_kernel,
        state_shape,
        (meta, *all_queries, new_own, new_other, state),
        scalars=1,
        flops=4 * 512 * 512 * 128,
    )
    states = exchange(state, "y")
    attention = call(merge_kernel, [((NW, tok_rows, 2 * HEAD), bf16)], (states,))
    attention = exchange(attention, "w")
    width = D // (NW * NX)
    terms = call(
        output_kernel,
        [((NX, tok_rows, width), f32)],
        (meta, attention, out_own, out_other),
        scalars=1,
        flops=2 * 64 * 4096 * 288,
    )
    terms = exchange(terms, "x")
    residual = lax.dynamic_slice_in_dim(tokens, fsdp_index * width, width, 1)
    return call(last_kernel, [((tok_rows, width), bf16)], (terms, residual))


def solution(mesh):
    fine = Mesh(mesh.devices.reshape(NZ, NY, NC, NW, NX), SEQ + FSDP)
    return jax.shard_map(
        on_device,
        mesh=fine,
        in_specs=(
            P(SEQ, None),
            P(),
            P(SEQ, FSDP),
            P(FSDP, SEQ),
            P(SEQ, FSDP),
            P(SEQ, FSDP),
            P(),
        ),
        out_specs=P(SEQ, FSDP),
        check_vma=False,
    )
```

time: 175 us -> 184 us (1.051)
  blocking collectives: 48.4 us -> 82.7 us
  waiting for transfers between devices: 36.1 us -> 21 us
  local copies, waits for them, and re-layouts: 10.2 us -> 2.8 us
  starting transfers between devices: 49.7 us -> 43 us
  Pallas kernels: 9.34 us -> 14.5 us
  other arithmetic: 3.21 us -> 0.39 us
    all_gather x0 -> x3, blocking collectives: none -> 54.3 us  [the longest x1 23.2 us: on_device(): out_block = lax.all_gather(out_block, 'z', axis=0)]
    all_to_all x3 -> x2, blocking collectives: 48.4 us -> 28.4 us  [exchange(): return lax.all_to_all(x, axis, 0, 0, tiled=True)]
    all_to_all x6 -> x4, starting transfers between devices: 37.8 us -> 23.4 us  [exchange(): return lax.all_to_all(x, axis, 0, 0, tiled=True)]
    all_to_all x6 -> x4, waiting for transfers between devices: 30.4 us -> 18.2 us  [exchange(): return lax.all_to_all(x, axis, 0, 0, tiled=True)]
    ppermute x1 -> x4, starting transfers between devices: 6.17 us -> 12 us  [the longest x3 10.4 us: on_device(): lax.ppermute(queries, 'y', [((i + k) % NY, i) for i in range(NY)])]
    pallas_call x4 -> x7, Pallas kernels: 9.34 us -> 14.5 us  [call(): pl.pallas_call(kernel, out_shape=shapes, in_specs=specs, out_specs=[pl.Bl...]
    broadcast_in_dim x5 -> x0, local copies, waits for them, and re-layouts: 3.9 us -> none  [copies(): return jnp.broadcast_to(x[None], (count,) + x.shape)]
    reshape x3 -> x1, local copies, waits for them, and re-layouts: 2.89 us -> 0.74 us  [on_device(): pre_gain.reshape(1, -1)]
  transfers between devices with their start and end apart: 11 -> 13, of which waited for: 8 -> 4; matrix products, arithmetic and copies ran while one was open for 4% -> 3% of each run, Pallas kernels for 5% -> 6%
where the time goes in v2:
time: 184 us; the launch traced here: 181 us
  blocking collectives  82.7 us (45%)
  starting transfers between devices  43 us (23%)
  waiting for transfers between devices  21 us (11%)
  Pallas kernels  14.5 us (8%)
  between operations  14.3 us (8%)
  local copies, waits for them, and re-layouts  2.8 us (2%)
  matrix products  2.59 us (1%)
    all_to_all x2, blocking collectives, exchange(): return lax.all_to_all(x, axis, 0, 0, tiled=True)  28.4 us
    all_to_all x4, starting transfers between devices, exchange(): return lax.all_to_all(x, axis, 0, 0, tiled=True)  23.4 us
    all_gather x1, blocking collectives, on_device(): out_block = lax.all_gather(out_block, 'z', axis=0)  23.2 us
    all_to_all x4, waiting for transfers between devices, exchange(): return lax.all_to_all(x, axis, 0, 0, tiled=True)  18.2 us
    all_gather x1, blocking collectives, on_device(): cache_own = lax.all_gather(cache, 'z', axis=0)  16.2 us
    all_gather x1, blocking collectives, on_device(): w_own = lax.all_gather(w_qkv, 'z', axis=0, tiled=True)  14.9 us
    pallas_call x7, Pallas kernels, call(): pl.pallas_call(kernel, out_shape=shapes, in_specs=specs, out_specs=[pl.Bl...  14.5 us
    ppermute x3, starting transfers between devices, on_device(): lax.ppermute(queries, 'y', [((i + k) % NY, i) for i in range(NY)])  10.4 us
  transfers between devices with their start and end apart: 13, of which 4 were waited for; matrix products, arithmetic and copies ran while one was open for 3% of the time, Pallas kernels for 6%

profile of v2, /device:TPU:24, one launch (start us, length us, event | category | flops | bytes accessed | tf_op | source)
XLA Modules:
  0.0 181.3 jit_solution(3859152182748797157)
XLA Ops:
  10.6 3.1 %shard_map.73 = bf16[4,2,64,576]{3,2,1,0:T(8,128)(2,1)} custom-call(s32[4]{0:T(128)S(1)} %pad_add_fusion.meta, bf16[64,4608]{1,0:T(8,128)(2,1)S(1)} %copy-done.1, f32[1,4608]{1,0:T(1,128)S(1)} %reshape.17.gain_ref), custom_call_target="tpu_custom_call" | custom-call | flops 1769472 | bytes 608272 | tf_op jit(solution)/shard_map/pallas_call | solution.py:215
  13.7 9.2 %all-to-all-start = ((bf16[4,2,64,576]{3,2,1,0:T(8,128)(2,1)}), bf16[4,2,64,576]{3,2,1,0:T(8,128)(2,1)S(1)}, u32[]{:S(2)}, u32[]{:S(2)}) async-start(bf16[4,2,64,576]{3,2,1,0:T(8,128)(2,1)} %shard_map.73), calls=%async_computation | async-start | bytes 1310720 | tf_op jit(solution)/shard_map/all_to_all | solution.py:21
  22.9 23.2 %all-gather.1 = bf16[576,256]{1,0:T(8,128)(2,1)} all-gather(bf16[144,256]{1,0:T(8,128)(2,1)S(1)} %collective-permute-done.6), channel_id=3, replica_groups=mesh['z'=4,'y'=4,'c'=2,'w'=4,'x'=4] {'z'}, dimensions={0}, use_global_device_ids=true | all-gather | bytes 368640 | tf_op jit(solution)/shard_map/all_gather | solution.py:245
  46.1 14.9 %all_gather.21 = bf16[576,512]{1,0:T(8,128)(2,1)S(1)} all-gather(bf16[144,512]{1,0:T(8,128)(2,1)S(1)} %copy-done.2), channel_id=1, replica_groups=mesh['z'=4,'y'=4,'c'=2,'w'=4,'x'=4] {'z'}, dimensions={0}, use_global_device_ids=true | all-gather | bytes 737280 | tf_op jit(solution)/shard_map/all_gather | solution.py:238
  61.0 1.9 %collective-permute-start = (bf16[576,512]{1,0:T(8,128)(2,1)S(1)}, bf16[576,512]{1,0:T(8,128)(2,1)}, u32[]{:S(2)}, u32[]{:S(2)}) collective-permute-start(bf16[576,512]{1,0:T(8,128)(2,1)S(1)} %all_gather.21), channel_id=1, source_target_pairs={{0,16},{16,0},{1,17},{17,1},{2,18},{18,2},{3,19},{19,3},{4,20},{20... | collective-permute-start | bytes 1769480 | tf_op jit(solution)/shard_map/ppermute | solution.py:25
  63.0 16.2 %all-gather = bf16[1024,256]{1,0:T(8,128)(2,1)S(1)} all-gather(bf16[256,256]{1,0:T(8,128)(2,1)S(1)} %pad_maximum_fusion), channel_id=2, replica_groups=mesh['z'=4,'y'=4,'c'=2,'w'=4,'x'=4] {'z'}, dimensions={0}, use_global_device_ids=true | all-gather | bytes 655360 | tf_op jit(solution)/shard_map/all_gather | solution.py:241
  79.1 1.9 %collective-permute-start.5 = (bf16[4,256,256]{2,1,0:T(8,128)(2,1)S(1)}, bf16[4,256,256]{2,1,0:T(8,128)(2,1)S(1)}, u32[]{:S(2)}, u32[]{:S(2)}) collective-permute-start(bf16[4,256,256]{2,1,0:T(8,128)(2,1)S(1)} %bitcast.18), channel_id=1, source_target_pairs={{0,16},{16,0},{1,17},{17,1},{2,18},{18,2},{3,19},{19,3},{4,20},{20... | collective-permute-start | bytes 1572872 | tf_op jit(solution)/shard_map/ppermute | solution.py:25
  81.6 2.2 %convolution_add_fusion = f32[256,512]{1,0:T(8,128)} fusion(f32[256,512]{1,0:T(8,128)S(1)} %fusion.2, bf16[256,576]{1,0:T(8,128)(2,1)S(1)} %bitcast.21, bf16[576,512]{1,0:T(8,128)(2,1)} %collective-permute-done), kind=kOutput, calls=%fused_computation | convolution fusion | flops 151126016 | bytes 1933312 | tf_op jit(solution)/shard_map/dot_general | solution.py:259
  83.8 5.2 %all-to-all-start.1 = ((f32[4,64,512]{2,1,0:T(8,128)}), f32[4,64,512]{2,1,0:T(8,128)S(1)}, u32[]{:S(2)}, u32[]{:S(2)}) async-start(f32[4,64,512]{2,1,0:T(8,128)} %bitcast.5), calls=%async_computation.1 | async-start | bytes 1048576 | tf_op jit(solution)/shard_map/all_to_all | solution.py:21
  89.3 7.8 %all-to-all-done.1.part_ref = f32[4,64,512]{2,1,0:T(8,128)S(1)} async-done(((f32[4,64,512]{2,1,0:T(8,128)}), f32[4,64,512]{2,1,0:T(8,128)S(1)}, u32[]{:S(2)}, u32[]{:S(2)}) %all-to-all-start.1) | async-done | bytes 524320 | tf_op jit(solution)/shard_map/all_to_all | solution.py:21
  97.8 4.7 %all-to-all-start.2 = ((bf16[4,64,256]{2,1,0:T(8,128)(2,1)}), bf16[4,64,256]{2,1,0:T(8,128)(2,1)S(1)}, u32[]{:S(2)}, u32[]{:S(2)}) async-start(bf16[4,64,256]{2,1,0:T(8,128)(2,1)} %get-tuple-element.8), calls=%async_computation.2 | async-start | bytes 262144 | tf_op jit(solution)/shard_map/all_to_all | solution.py:21
  104.5 4.0 %all-to-all-done.2.own_ref = bf16[4,64,256]{2,1,0:T(8,128)(2,1)S(1)} async-done(((bf16[4,64,256]{2,1,0:T(8,128)(2,1)}), bf16[4,64,256]{2,1,0:T(8,128)(2,1)S(1)}, u32[]{:S(2)}, u32[]{:S(2)}) %all-to-all-start.2) | async-done | bytes 131104 | tf_op jit(solution)/shard_map/all_to_all | solution.py:21
  108.5 1.9 %collective-permute-start.4 = (bf16[4,64,256]{2,1,0:T(8,128)(2,1)S(1)}, bf16[4,64,256]{2,1,0:T(8,128)(2,1)S(1)}, u32[]{:S(2)}, u32[]{:S(2)}) collective-permute-start(bf16[4,64,256]{2,1,0:T(8,128)(2,1)S(1)} %all-to-all-done.2.own_ref), channel_id=1, source_target_pairs={{0,16},{16,0},{1,17},{17,1},{2,18},{18,2},{3,19},{19,3},{4,20},{20... | collective-permute-start | bytes 393224 | tf_op jit(solution)/shard_map/ppermute | solution.py:25
  110.4 1.9 %collective-permute-start.1 = (bf16[64,256]{1,0:T(8,128)(2,1)S(1)}, bf16[64,256]{1,0:T(8,128)(2,1)S(1)}, u32[]{:S(2)}, u32[]{:S(2)}) collective-permute-start(bf16[64,256]{1,0:T(8,128)(2,1)S(1)} %get-tuple-element.7.q0), channel_id=1, source_target_pairs={{32,0},{64,32},{96,64},{0,96},{33,1},{65,33},{97,65},{1,97},{34,2}... | collective-permute-start | bytes 98312 | tf_op jit(solution)/shard_map/ppermute | solution.py:279
  112.3 5.4 %collective-permute-start.2 = (bf16[64,256]{1,0:T(8,128)(2,1)S(1)}, bf16[64,256]{1,0:T(8,128)(2,1)S(1)}, u32[]{:S(2)}, u32[]{:S(2)}) collective-permute-start(bf16[64,256]{1,0:T(8,128)(2,1)S(1)} %get-tuple-element.7.q0), channel_id=1, source_target_pairs={{64,0},{96,32},{0,64},{32,96},{65,1},{97,33},{1,65},{33,97},{66,2}... | collective-permute-start | bytes 98312 | tf_op jit(solution)/shard_map/ppermute | solution.py:279
  117.8 3.1 %collective-permute-start.3 = (bf16[64,256]{1,0:T(8,128)(2,1)S(1)}, bf16[64,256]{1,0:T(8,128)(2,1)S(1)}, u32[]{:S(2)}, u32[]{:S(2)}) collective-permute-start(bf16[64,256]{1,0:T(8,128)(2,1)S(1)} %get-tuple-element.7.q0), channel_id=1, source_target_pairs={{96,0},{0,32},{32,64},{64,96},{97,1},{1,33},{33,65},{65,97},{98,2}... | collective-permute-start | bytes 98312 | tf_op jit(solution)/shard_map/ppermute | solution.py:279
  120.9 2.7 %collective-permute-done.3.q3 = bf16[64,256]{1,0:T(8,128)(2,1)S(1)} collective-permute-done((bf16[64,256]{1,0:T(8,128)(2,1)S(1)}, bf16[64,256]{1,0:T(8,128)(2,1)S(1)}, u32[]{:S(2)}, u32[]{:S(2)}) %collective-permute-start.3) | collective-permute-done | bytes 32800 | tf_op jit(solution)/shard_map/ppermute | solution.py:279
  123.6 3.3 %shard_map.75.state_ref = f32[4,64,384]{2,1,0:T(8,128)S(1)} custom-call(s32[4]{0:T(128)S(1)} %pad_add_fusion.meta, bf16[64,256]{1,0:T(8,128)(2,1)S(1)} %get-tuple-element.7.q0, bf16[64,256]{1,0:T(8,128)(2,1)S(1)} %collective-permute-done.1.q1, bf16[64,256]{1,0:T(8,128)(2,1)S(1)} %collective-permute-done.2.q2, bf16[64,256]{1,0:T(8,128)(2,1)S(1)} %collective-permute-done.3.q3, ...), custom_call_target="tpu_custom_call" | custom-call | flops 536870912 | bytes 1179664 | tf_op jit(solution)/shard_map/pallas_call | solution.py:215
  126.9 4.1 %shard_map.76 = f32[4,64,384]{2,1,0:T(8,128)S(1)} custom-call(s32[4]{0:T(128)S(1)} %pad_add_fusion.meta, bf16[64,256]{1,0:T(8,128)(2,1)S(1)} %get-tuple-element.7.q0, bf16[64,256]{1,0:T(8,128)(2,1)S(1)} %collective-permute-done.1.q1, bf16[64,256]{1,0:T(8,128)(2,1)S(1)} %collective-permute-done.2.q2, bf16[64,256]{1,0:T(8,128)(2,1)S(1)} %collective-permute-done.3.q3, ...), custom_call_target="tpu_custom_call" | custom-call | flops 134217728 | bytes 786448 | tf_op jit(solution)/shard_map/pallas_call | solution.py:215
  131.1 10.1 %all_to_all.30.state_ref = f32[4,64,384]{2,1,0:T(8,128)S(1)} all-to-all(f32[4,64,384]{2,1,0:T(8,128)S(1)} %shard_map.76), channel_id=1, replica_groups=mesh['z'=4,'y'=4,'c'=2,'w'=4,'x'=4] {'y'}, dimensions={0} | all-to-all | bytes 786432 | tf_op jit(solution)/shard_map/all_to_all | solution.py:21
  141.5 18.3 %all_to_all.31.att_ref = bf16[4,64,256]{2,1,0:T(8,128)(2,1)S(1)} all-to-all(bf16[4,64,256]{2,1,0:T(8,128)(2,1)S(1)} %shard_map.77), channel_id=1, replica_groups=mesh['z'=4,'y'=4,'c'=2,'w'=4,'x'=4] {'w'}, dimensions={0} | all-to-all | bytes 262144 | tf_op jit(solution)/shard_map/all_to_all | solution.py:21
  159.8 2.3 %shard_map.78 = f32[4,64,288]{2,1,0:T(8,128)} custom-call(s32[4]{0:T(128)S(1)} %pad_add_fusion.meta, bf16[4,64,256]{2,1,0:T(8,128)(2,1)S(1)} %all_to_all.31.att_ref, bf16[4,4,144,256]{3,2,1,0:T(8,128)(2,1)S(1)} %bitcast.17, bf16[4,4,144,256]{3,2,1,0:T(8,128)(2,1)S(1)} %collective-permute-done.7.other_ref), custom_call_target="tpu_custom_call" | custom-call | flops 150994944 | bytes 2490384 | tf_op jit(solution)/shard_map/pallas_call | solution.py:215
  162.1 4.3 %all-to-all-start.5 = ((f32[4,64,288]{2,1,0:T(8,128)}), f32[4,64,288]{2,1,0:T(8,128)S(1)}, u32[]{:S(2)}, u32[]{:S(2)}) async-start(f32[4,64,288]{2,1,0:T(8,128)} %shard_map.78), calls=%async_computation.5 | async-start | bytes 786432 | tf_op jit(solution)/shard_map/all_to_all | solution.py:21
  167.3 6.5 %all-to-all-done.5.part_ref = f32[4,64,288]{2,1,0:T(8,128)S(1)} async-done(((f32[4,64,288]{2,1,0:T(8,128)}), f32[4,64,288]{2,1,0:T(8,128)S(1)}, u32[]{:S(2)}, u32[]{:S(2)}) %all-to-all-start.5) | async-done | bytes 294944 | tf_op jit(solution)/shard_map/all_to_all | solution.py:21
  (36 shorter events, 8.8 us)
Async XLA Ops:
  6.5 16.3 %collective-permute-start.6 = (bf16[144,256]{1,0:T(8,128)(2,1)}, bf16[144,256]{1,0:T(8,128)(2,1)S(1)}, u32[]{:S(2)}, u32[]{:S(2)}) collective-permute-start(bf16[144,256]{1,0:T(8,128)(2,1)} %bitcast.23), channel_id=1, source_target_pairs={{0,0},{4,128},{8,256},{12,384},{128,4},{132,132},{136,260},{140,38... | collective-permute-start | bytes 221192 | tf_op jit(solution)/shard_map/ppermute | solution.py:244
  9.5 1.1 copy-start.1
  13.7 32.4 %copy-start.2 = (bf16[144,512]{1,0:T(8,128)(2,1)S(1)}, bf16[144,512]{1,0:T(8,128)(2,1)}, u32[]{:S(2)}) copy-start(bf16[144,512]{1,0:T(8,128)(2,1)} %param.9) | copy-start | bytes 442372
  13.7 49.3 %copy-start.3 = (bf16[256,128]{1,0:T(8,128)(2,1)S(1)}, bf16[256,128]{1,0:T(8,128)(2,1)}, u32[]{:S(2)}) copy-start(bf16[256,128]{1,0:T(8,128)(2,1)} %param.12) | copy-start | bytes 196612
  13.7 49.3 %copy-start.4 = (bf16[256,128]{1,0:T(8,128)(2,1)S(1)}, bf16[256,128]{1,0:T(8,128)(2,1)}, u32[]{:S(2)}) copy-start(bf16[256,128]{1,0:T(8,128)(2,1)} %param.11) | copy-start | bytes 196612
  13.7 67.4 %all-to-all-start = ((bf16[4,2,64,576]{3,2,1,0:T(8,128)(2,1)}), bf16[4,2,64,576]{3,2,1,0:T(8,128)(2,1)S(1)}, u32[]{:S(2)}, u32[]{:S(2)}) async-start(bf16[4,2,64,576]{3,2,1,0:T(8,128)(2,1)} %shard_map.73), calls=%async_computation | async-start | bytes 1310720 | tf_op jit(solution)/shard_map/all_to_all | solution.py:21
  22.9 79.7 %all-gather.5.cloned.1.call-start = ((), (), s32[]{:S(2)}) async-start(), calls=%async_computation.6 | async-start | bytes 1474560 | tf_op jit(solution)/shard_map/all_gather | solution.py:246
  61.0 20.5 %collective-permute-start = (bf16[576,512]{1,0:T(8,128)(2,1)S(1)}, bf16[576,512]{1,0:T(8,128)(2,1)}, u32[]{:S(2)}, u32[]{:S(2)}) collective-permute-start(bf16[576,512]{1,0:T(8,128)(2,1)S(1)} %all_gather.21), channel_id=1, source_target_pairs={{0,16},{16,0},{1,17},{17,1},{2,18},{18,2},{3,19},{19,3},{4,20},{20... | collective-permute-start | bytes 1769480 | tf_op jit(solution)/shard_map/ppermute | solution.py:25
  79.1 38.6 %collective-permute-start.5 = (bf16[4,256,256]{2,1,0:T(8,128)(2,1)S(1)}, bf16[4,256,256]{2,1,0:T(8,128)(2,1)S(1)}, u32[]{:S(2)}, u32[]{:S(2)}) collective-permute-start(bf16[4,256,256]{2,1,0:T(8,128)(2,1)S(1)} %bitcast.18), channel_id=1, source_target_pairs={{0,16},{16,0},{1,17},{17,1},{2,18},{18,2},{3,19},{19,3},{4,20},{20... | collective-permute-start | bytes 1572872 | tf_op jit(solution)/shard_map/ppermute | solution.py:25
  83.8 13.3 %all-to-all-start.1 = ((f32[4,64,512]{2,1,0:T(8,128)}), f32[4,64,512]{2,1,0:T(8,128)S(1)}, u32[]{:S(2)}, u32[]{:S(2)}) async-start(f32[4,64,512]{2,1,0:T(8,128)} %bitcast.5), calls=%async_computation.1 | async-start | bytes 1048576 | tf_op jit(solution)/shard_map/all_to_all | solution.py:21
  97.8 10.6 %all-to-all-start.2 = ((bf16[4,64,256]{2,1,0:T(8,128)(2,1)}), bf16[4,64,256]{2,1,0:T(8,128)(2,1)S(1)}, u32[]{:S(2)}, u32[]{:S(2)}) async-start(bf16[4,64,256]{2,1,0:T(8,128)(2,1)} %get-tuple-element.8), calls=%async_computation.2 | async-start | bytes 262144 | tf_op jit(solution)/shard_map/all_to_all | solution.py:21
  102.6 57.3 %collective-permute-start.7 = (bf16[4,4,144,256]{3,2,1,0:T(8,128)(2,1)}, bf16[4,4,144,256]{3,2,1,0:T(8,128)(2,1)S(1)}, u32[]{:S(2)}, u32[]{:S(2)}) collective-permute-start(bf16[4,4,144,256]{3,2,1,0:T(8,128)(2,1)} %bitcast.16), channel_id=1, source_target_pairs={{0,16},{16,0},{1,17},{17,1},{2,18},{18,2},{3,19},{19,3},{4,20},{20... | collective-permute-start | bytes 3538952 | tf_op jit(solution)/shard_map/ppermute | solution.py:25
  108.5 18.5 %collective-permute-start.4 = (bf16[4,64,256]{2,1,0:T(8,128)(2,1)S(1)}, bf16[4,64,256]{2,1,0:T(8,128)(2,1)S(1)}, u32[]{:S(2)}, u32[]{:S(2)}) collective-permute-start(bf16[4,64,256]{2,1,0:T(8,128)(2,1)S(1)} %all-to-all-done.2.own_ref), channel_id=1, source_target_pairs={{0,16},{16,0},{1,17},{17,1},{2,18},{18,2},{3,19},{19,3},{4,20},{20... | collective-permute-start | bytes 393224 | tf_op jit(solution)/shard_map/ppermute | solution.py:25
  110.4 10.5 %collective-permute-start.1 = (bf16[64,256]{1,0:T(8,128)(2,1)S(1)}, bf16[64,256]{1,0:T(8,128)(2,1)S(1)}, u32[]{:S(2)}, u32[]{:S(2)}) collective-permute-start(bf16[64,256]{1,0:T(8,128)(2,1)S(1)} %get-tuple-element.7.q0), channel_id=1, source_target_pairs={{32,0},{64,32},{96,64},{0,96},{33,1},{65,33},{97,65},{1,97},{34,2}... | collective-permute-start | bytes 98312 | tf_op jit(solution)/shard_map/ppermute | solution.py:279
  112.3 8.5 %collective-permute-start.2 = (bf16[64,256]{1,0:T(8,128)(2,1)S(1)}, bf16[64,256]{1,0:T(8,128)(2,1)S(1)}, u32[]{:S(2)}, u32[]{:S(2)}) collective-permute-start(bf16[64,256]{1,0:T(8,128)(2,1)S(1)} %get-tuple-element.7.q0), channel_id=1, source_target_pairs={{64,0},{96,32},{0,64},{32,96},{65,1},{97,33},{1,65},{33,97},{66,2}... | collective-permute-start | bytes 98312 | tf_op jit(solution)/shard_map/ppermute | solution.py:279
  117.8 5.8 %collective-permute-start.3 = (bf16[64,256]{1,0:T(8,128)(2,1)S(1)}, bf16[64,256]{1,0:T(8,128)(2,1)S(1)}, u32[]{:S(2)}, u32[]{:S(2)}) collective-permute-start(bf16[64,256]{1,0:T(8,128)(2,1)S(1)} %get-tuple-element.7.q0), channel_id=1, source_target_pairs={{96,0},{0,32},{32,64},{64,96},{97,1},{1,33},{33,65},{65,97},{98,2}... | collective-permute-start | bytes 98312 | tf_op jit(solution)/shard_map/ppermute | solution.py:279
  126.9 32.9 %copy-start = (bf16[16,144,256]{2,1,0:T(8,128)(2,1)S(1)}, bf16[16,144,256]{2,1,0:T(8,128)(2,1)}, u32[]{:S(2)}) copy-start(bf16[16,144,256]{2,1,0:T(8,128)(2,1)} %all-gather.5.cloned.1.call-done) | copy-start | bytes 3538948
  162.1 11.7 %all-to-all-start.5 = ((f32[4,64,288]{2,1,0:T(8,128)}), f32[4,64,288]{2,1,0:T(8,128)S(1)}, u32[]{:S(2)}, u32[]{:S(2)}) async-start(f32[4,64,288]{2,1,0:T(8,128)} %shard_map.78), calls=%async_computation.5 | async-start | bytes 786432 | tf_op jit(solution)/shard_map/all_to_all | solution.py:21
Sparse Core Ops, SparseCore 0:
  46.2 25.9 all-gather.4

commit v3 on v2

--- a/solution.py
+++ b/solution.py
@@ -19,6 +19,27 @@
 
 def exchange(x, axis):
     return lax.all_to_all(x, axis, 0, 0, tiled=True)
+
+
+def from_next(x, axis, step, size):
+    return lax.ppermute(x, axis, [((i + step) % size, i) for i in range(size)])
+
+
+def from_pair(x, axis, bit, size):
+    return lax.ppermute(x, axis, [(i ^ bit, i) for i in range(size)])
+
+
+def gather_z(x):
+    pair = jnp.stack([x, from_pair(x, "z", 1, NZ)])
+    return jnp.concatenate([pair, from_pair(pair, "z", 2, NZ)])
+
+
+def gather_y(x):
+    after, before = from_next(x, "y", 1, NY), from_next(x, "y", NY - 1, NY)
+    half = x.shape[0] // 2
+    low = from_next(after[:half], "y", 1, NY)
+    high = from_next(before[half:], "y", NY - 1, NY)
+    return jnp.stack([x, after, jnp.concatenate([low, high]), before])
 
 
 def swap_core(x):
@@ -61,18 +82,21 @@
     return out
 
 
-def norm_kernel(meta, tokens_ref, gain_ref, out_ref):
+def norm_kernel(meta, tokens_ref, gain_ref, out_ref, normed_ref):
     hidden = tokens_ref[...].astype(jnp.float32)
     mean = jnp.mean(hidden * hidden, axis=-1, keepdims=True)
-    normed = (hidden * lax.rsqrt(mean + epsilon) * gain_ref[...]).astype(jnp.bfloat16)
+    normed_ref[...] = (hidden * lax.rsqrt(mean + epsilon) * gain_ref[...]).astype(jnp.bfloat16)
     first = meta[3] == 0
-    k_rows = normed.shape[1] // (NZ * NY * NC)
-    for y in range(NY):
-        for z in range(NZ):
-            at = (z * NY + y) * NC * k_rows
-            low, high = normed[:, at : at + k_rows], normed[:, at + k_rows : at + 2 * k_rows]
-            out_ref[y, 0, :, z * k_rows : (z + 1) * k_rows] = jnp.where(first, low, high)
-            out_ref[y, 1, :, z * k_rows : (z + 1) * k_rows] = jnp.where(first, high, low)
+    span = normed_ref.shape[1] // NZ
+    k_rows = span // (NY * NC)
+    for k in range(NZ):
+        block = meta[1] ^ k
+        part = normed_ref[:, pl.ds(pl.multiple_of(block * span, span), span)]
+        for y in range(NY):
+            at = y * NC * k_rows
+            low, high = part[:, at : at + k_rows], part[:, at + k_rows : at + 2 * k_rows]
+            out_ref[y, 0, :, k * k_rows : (k + 1) * k_rows] = jnp.where(first, low, high)
+            out_ref[y, 1, :, k * k_rows : (k + 1) * k_rows] = jnp.where(first, high, low)
 
 
 def rotary_kernel(part_ref, cos_ref, sin_ref, q_ref, new_ref):
@@ -88,13 +112,13 @@
     q_ref[:, HEAD:] = (rotated(1) * scale).astype(jnp.bfloat16)
     keys = rotated(2).astype(jnp.bfloat16)
     values = total[:, 3 * HEAD :].astype(jnp.bfloat16)
-    for i in range(NZ):
+    for i in range(NZ * NC):
         new_ref[i, :, :HEAD] = keys
         new_ref[i, :, HEAD:] = values
 
 
 def prefix_kernel(meta, q0, q1, q2, q3, own_ref, other_ref, out_ref):
-    length, y, c = meta[0], meta[2], meta[3]
+    length, my_z, y, c = meta[0], meta[1], meta[2], meta[3]
     slots = own_ref.shape[1]
     rows = q0.shape[0]
     lane = lax.broadcasted_iota(jnp.int32, (2 * rows, slots), 1)
@@ -106,11 +130,11 @@
             query = jnp.concatenate([qa[:, lanes], qb[:, lanes]], axis=0)
             parts = []
             for source, core in ((own_ref, c), (other_ref, 1 - c)):
-                for z in range(NZ):
-                    start = ((z * NY + y) * NC + core) * slots
+                for k in range(NZ):
+                    start = (((my_z ^ k) * NY + y) * NC + core) * slots
                     parts.append(
                         block_result(
-                            query, source[z, :, :HEAD], source[z, :, HEAD:], lane < length - start
+                            query, source[k, :, :HEAD], source[k, :, HEAD:], lane < length - start
                         )
                     )
             highest, denom, accum = combine(parts)
@@ -122,9 +146,9 @@
             out_ref[place, :, 2 * HEAD :] = stats[i * rows : (i + 1) * rows]
 
 
-def new_kernel(meta, q0, q1, q2, q3, own_ref, other_ref, state_ref, out_ref):
+def new_kernel(meta, q0, q1, q2, q3, new_ref, state_ref, out_ref):
     my_z, y, c = meta[1], meta[2], meta[3]
-    slots = own_ref.shape[1]
+    slots = new_ref.shape[1]
     rows = q0.shape[0]
     lane = lax.broadcasted_iota(jnp.int32, (2 * rows, slots), 1)
     row = lax.broadcasted_iota(jnp.int32, (2 * rows, slots), 0)
@@ -138,14 +162,13 @@
             lanes = slice(head * HEAD, (head + 1) * HEAD)
             query = jnp.concatenate([qa[:, lanes], qb[:, lanes]], axis=0)
             parts = []
-            for source, core in ((own_ref, c), (other_ref, 1 - c)):
-                for z in range(NZ):
-                    start = ((z * NY + y) * NC + core) * slots
-                    parts.append(
-                        block_result(
-                            query, source[z, :, :HEAD], source[z, :, HEAD:], offset >= start
-                        )
+            for k in range(NZ * NC):
+                start = ((k // NC * NY + y) * NC + k % NC) * slots
+                parts.append(
+                    block_result(
+                        query, new_ref[k, :, :HEAD], new_ref[k, :, HEAD:], offset >= start
                     )
+                )
             highest, denom, accum = combine(parts)
             old_highest = old_stats[:, 2 * head : 2 * head + 1]
             old_denom = old_stats[:, 2 * head + 1 : 2 * head + 2]
@@ -187,19 +210,20 @@
     first = meta[3] == 0
     half = own_ref.shape[2]
     for x in range(NX):
+        place = lax.rem(meta[2] + x, NX)
         sums = []
         for source in (own_ref, other_ref):
             total = 0.0
-            for w in range(NW):
+            for k in range(NW):
                 total = total + lax.dot_general(
-                    att_ref[w],
-                    source[x, w],
+                    att_ref[meta[1] ^ k],
+                    source[x, k],
                     (((1,), (1,)), ((), ())),
                     preferred_element_type=jnp.float32,
                 )
             sums.append(total)
-        out_ref[x, :, :half] = jnp.where(first, sums[0], sums[1])
-        out_ref[x, :, half:] = jnp.where(first, sums[1], sums[0])
+        out_ref[place, :, :half] = jnp.where(first, sums[0], sums[1])
+        out_ref[place, :, half:] = jnp.where(first, sums[1], sums[0])
 
 
 def last_kernel(part_ref, residual_ref, out_ref):
@@ -207,7 +231,7 @@
     out_ref[...] = (residual_ref[...].astype(jnp.float32) + total).astype(jnp.bfloat16)
 
 
-def call(kernel, out, operands, scalars=0, flops=0):
+def call(kernel, out, operands, scalars=0, flops=0, scratch=()):
     specs = [pl.BlockSpec(memory_space=pltpu.SMEM)] * scalars
     specs += [pl.BlockSpec(memory_space=pltpu.VMEM)] * (len(operands) - scalars)
     moved = sum(o.size * o.dtype.itemsize for o in operands)
@@ -217,6 +241,7 @@
         out_shape=shapes,
         in_specs=specs,
         out_specs=[pl.BlockSpec(memory_space=pltpu.VMEM)] * len(out),
+        scratch_shapes=list(scratch),
         compiler_params=pltpu.CompilerParams(vmem_limit_bytes=VMEM_BYTES),
         cost_estimate=pl.CostEstimate(
             flops=flops, bytes_accessed=moved, transcendentals=flops // 512
@@ -235,15 +260,14 @@
     length = cache_len[0]
     meta = jnp.stack([length, z, y, c]).astype(jnp.int32)
 
-    w_own = lax.all_gather(w_qkv, "z", axis=0, tiled=True)
+    w_own = gather_z(w_qkv)
     w_other = swap_core(w_own)
-    cache = jnp.concatenate([cache_keys, cache_values], axis=1)
-    cache_own = lax.all_gather(cache, "z", axis=0)
+    cache_own = gather_z(jnp.concatenate([cache_keys, cache_values], axis=1))
     cache_other = swap_core(cache_own)
     trade = [(a * NW + b, b * NW + a) for a in range(NZ) for b in range(NW)]
     out_block = lax.ppermute(w_out.T, ("z", "w"), trade)
-    out_block = lax.all_gather(out_block, "z", axis=0)
-    out_own = lax.all_gather(out_block, "y", axis=0)
+    out_block = gather_z(out_block)
+    out_own = gather_y(out_block)
     out_other = swap_core(out_own)
 
     rows_out = call(
@@ -252,8 +276,10 @@
         (meta, tokens, pre_gain.reshape(1, -1)),
         scalars=1,
         flops=tokens.size * 6,
+        scratch=[pltpu.VMEM(tokens.shape, bf16)],
     )
     rows_in = exchange(rows_out, "y")
+    w_own, w_other = (w.reshape(NZ * k_rows, -1) for w in (w_own, w_other))
     rows_own = rows_in[:, 0].reshape(NY * tok_rows, -1)
     rows_other = rows_in[:, 1].reshape(NY * tok_rows, -1)
     partial = jnp.dot(rows_own, w_own, preferred_element_type=f32) + jnp.dot(
@@ -270,14 +296,11 @@
     sine_part = jnp.concatenate([-sine_part, sine_part], axis=1)
     queries, new = call(
         rotary_kernel,
-        [((tok_rows, 2 * HEAD), bf16), ((NZ, tok_rows, 2 * HEAD), bf16)],
+        [((tok_rows, 2 * HEAD), bf16), ((NZ * NC, tok_rows, 2 * HEAD), bf16)],
         (partial, cosine, sine_part),
     )
-    new_own = exchange(new, "z")
-    new_other = swap_core(new_own)
-    all_queries = [queries] + [
-        lax.ppermute(queries, "y", [((i + k) % NY, i) for i in range(NY)]) for k in range(1, NY)
-    ]
+    all_new = exchange(new, ("z", "c"))
+    all_queries = [queries] + [from_next(queries, "y", k, NY) for k in range(1, NY)]
 
     state_shape = [((NY, tok_rows, 3 * HEAD), f32)]
     state = call(
@@ -290,7 +313,7 @@
     state = call(
         new_kernel,
         state_shape,
-        (meta, *all_queries, new_own, new_other, state),
+        (meta, *all_queries, all_new, state),
         scalars=1,
         flops=4 * 512 * 512 * 128,
     )

time: 184 us -> 166 us (0.902)
  blocking collectives: 82.7 us -> 9.62 us
  starting transfers between devices: 43 us -> 87.1 us
  waiting for transfers between devices: 21 us -> 41.8 us
  between operations: 14.3 us -> 1.06 us
  other arithmetic: 0.39 us -> 4 us
    all_gather x3 -> x0, blocking collectives: 54.3 us -> none  [the longest x1 23.2 us: on_device(): out_block = lax.all_gather(out_block, 'z', axis=0)]
    ppermute x3 -> x13, starting transfers between devices: 10.4 us -> 48.8 us  [the longest x7 25 us: from_next(): return lax.ppermute(x, axis, [((i + step) % size, i) for i in range(size)])]
    all_to_all x2 -> x1, blocking collectives: 28.4 us -> 9.62 us  [exchange(): return lax.all_to_all(x, axis, 0, 0, tiled=True)]
    ppermute x3 -> x13, waiting for transfers between devices: 2.71 us -> 20.1 us  [the longest x6 15.7 us: from_pair(): return lax.ppermute(x, axis, [(i ^ bit, i) for i in range(size)])]
    all_to_all x4 -> x5, starting transfers between devices: 23.4 us -> 31.9 us  [exchange(): return lax.all_to_all(x, axis, 0, 0, tiled=True)]
    all_to_all x4 -> x5, waiting for transfers between devices: 18.2 us -> 21.8 us  [exchange(): return lax.all_to_all(x, axis, 0, 0, tiled=True)]
    another operation x0 -> x6, other arithmetic: none -> 2.57 us  [the longest x3 1.44 us: gather_z(): pair = jnp.stack([x, from_pair(x, 'z', 1, NZ)])]
    ppermute x4 -> x3, starting transfers between devices: 7.64 us -> 5.76 us  [swap_core(): return lax.ppermute(x, 'c', [(0, 1), (1, 0)])]
  transfers between devices with their start and end apart: 13 -> 22, of which waited for: 4 -> 6; matrix products, arithmetic and copies ran while one was open for 3% -> 4% of each run, Pallas kernels for 6% -> 8%
where the time goes in v3:
time: 166 us; the launch traced here: 164 us
  starting transfers between devices  87.1 us (52%)
  waiting for transfers between devices  41.8 us (25%)
  Pallas kernels  15.6 us (9%)
  blocking collectives  9.62 us (6%)
  other arithmetic  4 us (2%)
  local copies, waits for them, and re-layouts  2.86 us (2%)
    all_to_all x5, starting transfers between devices, exchange(): return lax.all_to_all(x, axis, 0, 0, tiled=True)  31.9 us
    ppermute x7, starting transfers between devices, from_next(): return lax.ppermute(x, axis, [((i + step) % size, i) for i in range(size)])  25 us
    ppermute x6, starting transfers between devices, from_pair(): return lax.ppermute(x, axis, [(i ^ bit, i) for i in range(size)])  23.8 us
    all_to_all x5, waiting for transfers between devices, exchange(): return lax.all_to_all(x, axis, 0, 0, tiled=True)  21.8 us
    ppermute x6, waiting for transfers between devices, from_pair(): return lax.ppermute(x, axis, [(i ^ bit, i) for i in range(size)])  15.7 us
    pallas_call x7, Pallas kernels, call(): pl.pallas_call(kernel, out_shape=shapes, in_specs=specs, out_specs=[pl.Bl...  15.6 us
    all_to_all x1, blocking collectives, exchange(): return lax.all_to_all(x, axis, 0, 0, tiled=True)  9.62 us
    ppermute x3, starting transfers between devices, swap_core(): return lax.ppermute(x, 'c', [(0, 1), (1, 0)])  5.76 us
  transfers between devices with their start and end apart: 22, of which 6 were waited for; matrix products, arithmetic and copies ran while one was open for 4% of the time, Pallas kernels for 8%

profile of v3, /device:TPU:24, one launch (start us, length us, event | category | flops | bytes accessed | tf_op | source)
XLA Modules:
  0.0 163.6 jit_solution(12431999153794966322)
XLA Ops:
  0.0 3.8 %collective-permute-start = (bf16[144,512]{1,0:T(8,128)(2,1)}, bf16[144,512]{1,0:T(8,128)(2,1)S(1)}, u32[]{:S(2)}, u32[]{:S(2)}) collective-permute-start(bf16[144,512]{1,0:T(8,128)(2,1)} %param.9), channel_id=1, source_target_pairs={{128,0},{0,128},{384,256},{256,384},{129,1},{1,129},{385,257},{257... | collective-permute-start | bytes 442376 | tf_op jit(solution)/shard_map/ppermute | solution.py:29
  6.4 3.5 %shard_map.73 = bf16[4,2,64,576]{3,2,1,0:T(8,128)(2,1)} custom-call(s32[4]{0:T(128)S(1)} %pad_add_fusion.meta, bf16[64,4608]{1,0:T(8,128)(2,1)S(1)} %copy-done, f32[1,4608]{1,0:T(1,128)S(1)} %reshape.23.gain_ref), custom_call_target="tpu_custom_call" | custom-call | flops 1769472 | bytes 608272 | tf_op jit(solution)/shard_map/pallas_call | solution.py:239
  9.9 7.3 %all-to-all-start = ((bf16[4,2,64,576]{3,2,1,0:T(8,128)(2,1)}), bf16[4,2,64,576]{3,2,1,0:T(8,128)(2,1)S(1)}, u32[]{:S(2)}, u32[]{:S(2)}) async-start(bf16[4,2,64,576]{3,2,1,0:T(8,128)(2,1)} %shard_map.73), calls=%async_computation | async-start | bytes 1310720 | tf_op jit(solution)/shard_map/all_to_all | solution.py:21
  17.2 2.7 %collective-permute-start.1 = (bf16[2,144,512]{2,1,0:T(8,128)(2,1)S(1)}, bf16[2,144,512]{2,1,0:T(8,128)(2,1)S(1)}, u32[]{:S(2)}, u32[]{:S(2)}) collective-permute-start(bf16[2,144,512]{2,1,0:T(8,128)(2,1)S(1)} %pad_maximum_fusion.3), channel_id=1, source_target_pairs={{256,0},{384,128},{0,256},{128,384},{257,1},{385,129},{1,257},{129... | collective-permute-start | bytes 884744 | tf_op jit(solution)/shard_map/ppermute | solution.py:29
  20.0 3.1 %collective-permute-start.6 = (bf16[256,256]{1,0:T(8,128)(2,1)S(1)}, bf16[256,256]{1,0:T(8,128)(2,1)S(1)}, u32[]{:S(2)}, u32[]{:S(2)}) collective-permute-start(bf16[256,256]{1,0:T(8,128)(2,1)S(1)} %constant_dynamic-update-slice_fusion), channel_id=1, source_target_pairs={{128,0},{0,128},{384,256},{256,384},{129,1},{1,129},{385,257},{257... | collective-permute-start | bytes 393224 | tf_op jit(solution)/shard_map/ppermute | solution.py:29
  23.8 9.9 %collective-permute-done.1 = bf16[2,144,512]{2,1,0:T(8,128)(2,1)S(1)} collective-permute-done((bf16[2,144,512]{2,1,0:T(8,128)(2,1)S(1)}, bf16[2,144,512]{2,1,0:T(8,128)(2,1)S(1)}, u32[]{:S(2)}, u32[]{:S(2)}) %collective-permute-start.1) | collective-permute-done | bytes 294944 | tf_op jit(solution)/shard_map/ppermute | solution.py:29
  38.4 9.9 %collective-permute-start.7 = (bf16[2,256,256]{2,1,0:T(8,128)(2,1)}, bf16[2,256,256]{2,1,0:T(8,128)(2,1)}, u32[]{:S(2)}, u32[]{:S(2)}) collective-permute-start(bf16[2,256,256]{2,1,0:T(8,128)(2,1)} %pad_maximum_fusion.5), channel_id=1, source_target_pairs={{256,0},{384,128},{0,256},{128,384},{257,1},{385,129},{1,257},{129... | collective-permute-start | bytes 786440 | tf_op jit(solution)/shard_map/ppermute | solution.py:29
  49.0 2.3 %collective-permute-start.11 = (bf16[2,144,256]{2,1,0:T(8,128)(2,1)}, bf16[2,144,256]{2,1,0:T(8,128)(2,1)}, u32[]{:S(2)}, u32[]{:S(2)}) collective-permute-start(bf16[2,144,256]{2,1,0:T(8,128)(2,1)} %pad_maximum_fusion.6), channel_id=1, source_target_pairs={{256,0},{384,128},{0,256},{128,384},{257,1},{385,129},{1,257},{129... | collective-permute-start | bytes 442376 | tf_op jit(solution)/shard_map/ppermute | solution.py:29
  53.0 4.8 %all-to-all-start.1 = ((f32[4,64,512]{2,1,0:T(8,128)}), f32[4,64,512]{2,1,0:T(8,128)S(1)}, u32[]{:S(2)}, u32[]{:S(2)}) async-start(f32[4,64,512]{2,1,0:T(8,128)} %bitcast.9), calls=%async_computation.1 | async-start | bytes 1048576 | tf_op jit(solution)/shard_map/all_to_all | solution.py:21
  57.8 5.8 %collective-permute-done.11 = bf16[2,144,256]{2,1,0:T(8,128)(2,1)} collective-permute-done((bf16[2,144,256]{2,1,0:T(8,128)(2,1)}, bf16[2,144,256]{2,1,0:T(8,128)(2,1)}, u32[]{:S(2)}, u32[]{:S(2)}) %collective-permute-start.11) | collective-permute-done | bytes 147488 | tf_op jit(solution)/shard_map/ppermute | solution.py:29
  64.5 2.8 %collective-permute-start.12 = (bf16[4,144,256]{2,1,0:T(8,128)(2,1)S(1)}, bf16[4,144,256]{2,1,0:T(8,128)(2,1)S(1)}, u32[]{:S(2)}, u32[]{:S(2)}) collective-permute-start(bf16[4,144,256]{2,1,0:T(8,128)(2,1)S(1)} %get-tuple-element.12), channel_id=1, source_target_pairs={{32,0},{64,32},{96,64},{0,96},{33,1},{65,33},{97,65},{1,97},{34,2}... | collective-permute-start | bytes 884744 | tf_op jit(solution)/shard_map/ppermute | solution.py:25
  67.3 4.3 %collective-permute-start.14 = (bf16[4,144,256]{2,1,0:T(8,128)(2,1)S(1)}, bf16[4,144,256]{2,1,0:T(8,128)(2,1)S(1)}, u32[]{:S(2)}, u32[]{:S(2)}) collective-permute-start(bf16[4,144,256]{2,1,0:T(8,128)(2,1)S(1)} %get-tuple-element.12), channel_id=1, source_target_pairs={{96,0},{0,32},{32,64},{64,96},{97,1},{1,33},{33,65},{65,97},{98,2}... | collective-permute-start | bytes 884744 | tf_op jit(solution)/shard_map/ppermute | solution.py:25
  72.7 3.9 %all-to-all-start.2 = ((bf16[8,64,256]{2,1,0:T(8,128)(2,1)}), bf16[8,64,256]{2,1,0:T(8,128)(2,1)S(1)}, u32[]{:S(2)}, u32[]{:S(2)}) async-start(bf16[8,64,256]{2,1,0:T(8,128)(2,1)} %get-tuple-element.8), calls=%async_computation.2 | async-start | bytes 524288 | tf_op jit(solution)/shard_map/all_to_all | solution.py:21
  78.6 5.1 %collective-permute-start.15 = (bf16[2,144,256]{2,1,0:T(8,128)(2,1)S(1)}, bf16[2,144,256]{2,1,0:T(8,128)(2,1)S(1)}, u32[]{:S(2)}, u32[]{:S(2)}) collective-permute-start(bf16[2,144,256]{2,1,0:T(8,128)(2,1)S(1)} %slice.19), channel_id=1, source_target_pairs={{96,0},{0,32},{32,64},{64,96},{97,1},{1,33},{33,65},{65,97},{98,2}... | collective-permute-start | bytes 442376 | tf_op jit(solution)/shard_map/ppermute | solution.py:25
  91.2 7.1 %collective-permute-start.4 = (bf16[64,256]{1,0:T(8,128)(2,1)S(1)}, bf16[64,256]{1,0:T(8,128)(2,1)S(1)}, u32[]{:S(2)}, u32[]{:S(2)}) collective-permute-start(bf16[64,256]{1,0:T(8,128)(2,1)S(1)} %get-tuple-element.7.q0), channel_id=1, source_target_pairs={{64,0},{96,32},{0,64},{32,96},{65,1},{97,33},{1,65},{33,97},{66,2}... | collective-permute-start | bytes 98312 | tf_op jit(solution)/shard_map/ppermute | solution.py:25
  100.3 3.8 %collective-permute-done.5.q3 = bf16[64,256]{1,0:T(8,128)(2,1)S(1)} collective-permute-done((bf16[64,256]{1,0:T(8,128)(2,1)S(1)}, bf16[64,256]{1,0:T(8,128)(2,1)S(1)}, u32[]{:S(2)}, u32[]{:S(2)}) %collective-permute-start.5) | collective-permute-done | bytes 32800 | tf_op jit(solution)/shard_map/ppermute | solution.py:25
  104.1 3.3 %shard_map.75.state_ref = f32[4,64,384]{2,1,0:T(8,128)S(1)} custom-call(s32[4]{0:T(128)S(1)} %pad_add_fusion.meta, bf16[64,256]{1,0:T(8,128)(2,1)S(1)} %get-tuple-element.7.q0, bf16[64,256]{1,0:T(8,128)(2,1)S(1)} %collective-permute-done.3.q1, bf16[64,256]{1,0:T(8,128)(2,1)S(1)} %collective-permute-done.4.q2, bf16[64,256]{1,0:T(8,128)(2,1)S(1)} %collective-permute-done.5.q3, ...), custom_call_target="tpu_custom_call" | custom-call | flops 536870912 | bytes 1179664 | tf_op jit(solution)/shard_map/pallas_call | solution.py:239
  107.4 4.1 %shard_map.76 = f32[4,64,384]{2,1,0:T(8,128)S(1)} custom-call(s32[4]{0:T(128)S(1)} %pad_add_fusion.meta, bf16[64,256]{1,0:T(8,128)(2,1)S(1)} %get-tuple-element.7.q0, bf16[64,256]{1,0:T(8,128)(2,1)S(1)} %collective-permute-done.3.q1, bf16[64,256]{1,0:T(8,128)(2,1)S(1)} %collective-permute-done.4.q2, bf16[64,256]{1,0:T(8,128)(2,1)S(1)} %collective-permute-done.5.q3, ...), custom_call_target="tpu_custom_call" | custom-call | flops 134217728 | bytes 786448 | tf_op jit(solution)/shard_map/pallas_call | solution.py:239
  111.5 9.6 %all_to_all.30.state_ref = f32[4,64,384]{2,1,0:T(8,128)S(1)} all-to-all(f32[4,64,384]{2,1,0:T(8,128)S(1)} %shard_map.76), channel_id=1, replica_groups=mesh['z'=4,'y'=4,'c'=2,'w'=4,'x'=4] {'y'}, dimensions={0} | all-to-all | bytes 786432 | tf_op jit(solution)/shard_map/all_to_all | solution.py:21
  122.1 11.6 %all-to-all-start.4 = ((bf16[4,64,256]{2,1,0:T(8,128)(2,1)}), bf16[4,64,256]{2,1,0:T(8,128)(2,1)S(1)}, u32[]{:S(2)}, u32[]{:S(2)}) async-start(bf16[4,64,256]{2,1,0:T(8,128)(2,1)} %shard_map.77), calls=%async_computation.4 | async-start | bytes 262144 | tf_op jit(solution)/shard_map/all_to_all | solution.py:21
  133.8 15.3 %all-to-all-done.4.att_ref = bf16[4,64,256]{2,1,0:T(8,128)(2,1)S(1)} async-done(((bf16[4,64,256]{2,1,0:T(8,128)(2,1)}), bf16[4,64,256]{2,1,0:T(8,128)(2,1)S(1)}, u32[]{:S(2)}, u32[]{:S(2)}) %all-to-all-start.4) | async-done | bytes 131104 | tf_op jit(solution)/shard_map/all_to_all | solution.py:21
  149.0 2.2 %shard_map.78 = f32[4,64,288]{2,1,0:T(8,128)} custom-call(s32[4]{0:T(128)S(1)} %pad_add_fusion.meta, bf16[4,64,256]{2,1,0:T(8,128)(2,1)S(1)} %all-to-all-done.4.att_ref, bf16[4,4,144,256]{3,2,1,0:T(8,128)(2,1)S(1)} %pad_maximum_fusion.own_ref, bf16[4,4,144,256]{3,2,1,0:T(8,128)(2,1)S(1)} %collective-permute-done.16.other_ref), custom_call_target="tpu_custom_call" | custom-call | flops 150994944 | bytes 2490384 | tf_op jit(solution)/shard_map/pallas_call | solution.py:239
  151.3 4.3 %all-to-all-start.5 = ((f32[4,64,288]{2,1,0:T(8,128)}), f32[4,64,288]{2,1,0:T(8,128)S(1)}, u32[]{:S(2)}, u32[]{:S(2)}) async-start(f32[4,64,288]{2,1,0:T(8,128)} %shard_map.78), calls=%async_computation.5 | async-start | bytes 786432 | tf_op jit(solution)/shard_map/all_to_all | solution.py:21
  156.5 6.5 %all-to-all-done.5.part_ref = f32[4,64,288]{2,1,0:T(8,128)S(1)} async-done(((f32[4,64,288]{2,1,0:T(8,128)}), f32[4,64,288]{2,1,0:T(8,128)S(1)}, u32[]{:S(2)}, u32[]{:S(2)}) %all-to-all-start.5) | async-done | bytes 294944 | tf_op jit(solution)/shard_map/all_to_all | solution.py:21
  (60 shorter events, 25.5 us)
Async XLA Ops:
  0.0 17.2 %collective-permute-start = (bf16[144,512]{1,0:T(8,128)(2,1)}, bf16[144,512]{1,0:T(8,128)(2,1)S(1)}, u32[]{:S(2)}, u32[]{:S(2)}) collective-permute-start(bf16[144,512]{1,0:T(8,128)(2,1)} %param.9), channel_id=1, source_target_pairs={{128,0},{0,128},{384,256},{256,384},{129,1},{1,129},{385,257},{257... | collective-permute-start | bytes 442376 | tf_op jit(solution)/shard_map/ppermute | solution.py:29
  6.4 10.8 %copy-start.1 = (bf16[144,512]{1,0:T(8,128)(2,1)S(1)}, bf16[144,512]{1,0:T(8,128)(2,1)}, u32[]{:S(2)}) copy-start(bf16[144,512]{1,0:T(8,128)(2,1)} %param.9) | copy-start | bytes 442372
  9.9 13.2 %copy-start.4 = (bf16[256,144]{0,1:T(8,128)(2,1)S(1)}, bf16[256,144]{0,1:T(8,128)(2,1)}, u32[]{:S(2)}) copy-start(bf16[256,144]{0,1:T(8,128)(2,1)} %param.10) | copy-start | bytes 221188
  9.9 41.5 %all-to-all-start = ((bf16[4,2,64,576]{3,2,1,0:T(8,128)(2,1)}), bf16[4,2,64,576]{3,2,1,0:T(8,128)(2,1)S(1)}, u32[]{:S(2)}, u32[]{:S(2)}) async-start(bf16[4,2,64,576]{3,2,1,0:T(8,128)(2,1)} %shard_map.73), calls=%async_computation | async-start | bytes 1310720 | tf_op jit(solution)/shard_map/all_to_all | solution.py:21
  17.2 16.5 %collective-permute-start.1 = (bf16[2,144,512]{2,1,0:T(8,128)(2,1)S(1)}, bf16[2,144,512]{2,1,0:T(8,128)(2,1)S(1)}, u32[]{:S(2)}, u32[]{:S(2)}) collective-permute-start(bf16[2,144,512]{2,1,0:T(8,128)(2,1)S(1)} %pad_maximum_fusion.3), channel_id=1, source_target_pairs={{256,0},{384,128},{0,256},{128,384},{257,1},{385,129},{1,257},{129... | collective-permute-start | bytes 884744 | tf_op jit(solution)/shard_map/ppermute | solution.py:29
  20.0 17.7 %collective-permute-start.6 = (bf16[256,256]{1,0:T(8,128)(2,1)S(1)}, bf16[256,256]{1,0:T(8,128)(2,1)S(1)}, u32[]{:S(2)}, u32[]{:S(2)}) collective-permute-start(bf16[256,256]{1,0:T(8,128)(2,1)S(1)} %constant_dynamic-update-slice_fusion), channel_id=1, source_target_pairs={{128,0},{0,128},{384,256},{256,384},{129,1},{1,129},{385,257},{257... | collective-permute-start | bytes 393224 | tf_op jit(solution)/shard_map/ppermute | solution.py:29
  23.1 12.6 %collective-permute-start.9 = (bf16[144,256]{1,0:T(8,128)(2,1)S(1)}, bf16[144,256]{1,0:T(8,128)(2,1)S(1)}, u32[]{:S(2)}, u32[]{:S(2)}) collective-permute-start(bf16[144,256]{1,0:T(8,128)(2,1)S(1)} %bitcast.45), channel_id=1, source_target_pairs={{0,0},{4,128},{8,256},{12,384},{128,4},{132,132},{136,260},{140,38... | collective-permute-start | bytes 221192 | tf_op jit(solution)/shard_map/ppermute | solution.py:268
  33.8 17.6 %collective-permute-start.2 = (bf16[4,144,512]{2,1,0:T(8,128)(2,1)S(1)}, bf16[4,144,512]{2,1,0:T(8,128)(2,1)S(1)}, u32[]{:S(2)}, u32[]{:S(2)}) collective-permute-start(bf16[4,144,512]{2,1,0:T(8,128)(2,1)S(1)} %pad_maximum_fusion.1), channel_id=1, source_target_pairs={{0,16},{16,0},{1,17},{17,1},{2,18},{18,2},{3,19},{19,3},{4,20},{20... | collective-permute-start | bytes 1769480 | tf_op jit(solution)/shard_map/ppermute | solution.py:46
  35.7 12.6 %collective-permute-start.10 = (bf16[144,256]{1,0:T(8,128)(2,1)S(1)}, bf16[144,256]{1,0:T(8,128)(2,1)S(1)}, u32[]{:S(2)}, u32[]{:S(2)}) collective-permute-start(bf16[144,256]{1,0:T(8,128)(2,1)S(1)} %collective-permute-done.9), channel_id=1, source_target_pairs={{128,0},{0,128},{384,256},{256,384},{129,1},{1,129},{385,257},{257... | collective-permute-start | bytes 221192 | tf_op jit(solution)/shard_map/ppermute | solution.py:29
  38.4 45.3 %collective-permute-start.7 = (bf16[2,256,256]{2,1,0:T(8,128)(2,1)}, bf16[2,256,256]{2,1,0:T(8,128)(2,1)}, u32[]{:S(2)}, u32[]{:S(2)}) collective-permute-start(bf16[2,256,256]{2,1,0:T(8,128)(2,1)} %pad_maximum_fusion.5), channel_id=1, source_target_pairs={{256,0},{384,128},{0,256},{128,384},{257,1},{385,129},{1,257},{129... | collective-permute-start | bytes 786440 | tf_op jit(solution)/shard_map/ppermute | solution.py:29
  49.0 14.5 %collective-permute-start.11 = (bf16[2,144,256]{2,1,0:T(8,128)(2,1)}, bf16[2,144,256]{2,1,0:T(8,128)(2,1)}, u32[]{:S(2)}, u32[]{:S(2)}) collective-permute-start(bf16[2,144,256]{2,1,0:T(8,128)(2,1)} %pad_maximum_fusion.6), channel_id=1, source_target_pairs={{256,0},{384,128},{0,256},{128,384},{257,1},{385,129},{1,257},{129... | collective-permute-start | bytes 442376 | tf_op jit(solution)/shard_map/ppermute | solution.py:29
  53.0 18.9 %all-to-all-start.1 = ((f32[4,64,512]{2,1,0:T(8,128)}), f32[4,64,512]{2,1,0:T(8,128)S(1)}, u32[]{:S(2)}, u32[]{:S(2)}) async-start(f32[4,64,512]{2,1,0:T(8,128)} %bitcast.9), calls=%async_computation.1 | async-start | bytes 1048576 | tf_op jit(solution)/shard_map/all_to_all | solution.py:21
  64.5 12.1 %collective-permute-start.12 = (bf16[4,144,256]{2,1,0:T(8,128)(2,1)S(1)}, bf16[4,144,256]{2,1,0:T(8,128)(2,1)S(1)}, u32[]{:S(2)}, u32[]{:S(2)}) collective-permute-start(bf16[4,144,256]{2,1,0:T(8,128)(2,1)S(1)} %get-tuple-element.12), channel_id=1, source_target_pairs={{32,0},{64,32},{96,64},{0,96},{33,1},{65,33},{97,65},{1,97},{34,2}... | collective-permute-start | bytes 884744 | tf_op jit(solution)/shard_map/ppermute | solution.py:25
  67.3 11.3 %collective-permute-start.14 = (bf16[4,144,256]{2,1,0:T(8,128)(2,1)S(1)}, bf16[4,144,256]{2,1,0:T(8,128)(2,1)S(1)}, u32[]{:S(2)}, u32[]{:S(2)}) collective-permute-start(bf16[4,144,256]{2,1,0:T(8,128)(2,1)S(1)} %get-tuple-element.12), channel_id=1, source_target_pairs={{96,0},{0,32},{32,64},{64,96},{97,1},{1,33},{33,65},{65,97},{98,2}... | collective-permute-start | bytes 884744 | tf_op jit(solution)/shard_map/ppermute | solution.py:25
  72.7 34.7 %all-to-all-start.2 = ((bf16[8,64,256]{2,1,0:T(8,128)(2,1)}), bf16[8,64,256]{2,1,0:T(8,128)(2,1)S(1)}, u32[]{:S(2)}, u32[]{:S(2)}) async-start(bf16[8,64,256]{2,1,0:T(8,128)(2,1)} %get-tuple-element.8), calls=%async_computation.2 | async-start | bytes 524288 | tf_op jit(solution)/shard_map/all_to_all | solution.py:21
  76.6 10.0 %collective-permute-start.13 = (bf16[2,144,256]{2,1,0:T(8,128)(2,1)S(1)}, bf16[2,144,256]{2,1,0:T(8,128)(2,1)S(1)}, u32[]{:S(2)}, u32[]{:S(2)}) collective-permute-start(bf16[2,144,256]{2,1,0:T(8,128)(2,1)S(1)} %slice.18), channel_id=1, source_target_pairs={{32,0},{64,32},{96,64},{0,96},{33,1},{65,33},{97,65},{1,97},{34,2}... | collective-permute-start | bytes 442376 | tf_op jit(solution)/shard_map/ppermute | solution.py:25
  78.6 8.6 %collective-permute-start.15 = (bf16[2,144,256]{2,1,0:T(8,128)(2,1)S(1)}, bf16[2,144,256]{2,1,0:T(8,128)(2,1)S(1)}, u32[]{:S(2)}, u32[]{:S(2)}) collective-permute-start(bf16[2,144,256]{2,1,0:T(8,128)(2,1)S(1)} %slice.19), channel_id=1, source_target_pairs={{96,0},{0,32},{32,64},{64,96},{97,1},{1,33},{33,65},{65,97},{98,2}... | collective-permute-start | bytes 442376 | tf_op jit(solution)/shard_map/ppermute | solution.py:25
  84.7 15.5 %collective-permute-start.8 = (bf16[4,256,256]{2,1,0:T(8,128)(2,1)S(1)}, bf16[4,256,256]{2,1,0:T(8,128)(2,1)S(1)}, u32[]{:S(2)}, u32[]{:S(2)}) collective-permute-start(bf16[4,256,256]{2,1,0:T(8,128)(2,1)S(1)} %pad_maximum_fusion.2.own_ref), channel_id=1, source_target_pairs={{0,16},{16,0},{1,17},{17,1},{2,18},{18,2},{3,19},{19,3},{4,20},{20... | collective-permute-start | bytes 1572872 | tf_op jit(solution)/shard_map/ppermute | solution.py:46
  87.4 46.4 %collective-permute-start.16 = (bf16[4,4,144,256]{3,2,1,0:T(8,128)(2,1)S(1)}, bf16[4,4,144,256]{3,2,1,0:T(8,128)(2,1)S(1)}, u32[]{:S(2)}, u32[]{:S(2)}) collective-permute-start(bf16[4,4,144,256]{3,2,1,0:T(8,128)(2,1)S(1)} %pad_maximum_fusion.own_ref), channel_id=1, source_target_pairs={{0,16},{16,0},{1,17},{17,1},{2,18},{18,2},{3,19},{19,3},{4,20},{20... | collective-permute-start | bytes 3538952 | tf_op jit(solution)/shard_map/ppermute | solution.py:46
  89.3 10.9 %collective-permute-start.3 = (bf16[64,256]{1,0:T(8,128)(2,1)S(1)}, bf16[64,256]{1,0:T(8,128)(2,1)S(1)}, u32[]{:S(2)}, u32[]{:S(2)}) collective-permute-start(bf16[64,256]{1,0:T(8,128)(2,1)S(1)} %get-tuple-element.7.q0), channel_id=1, source_target_pairs={{32,0},{64,32},{96,64},{0,96},{33,1},{65,33},{97,65},{1,97},{34,2}... | collective-permute-start | bytes 98312 | tf_op jit(solution)/shard_map/ppermute | solution.py:25
  91.2 9.0 %collective-permute-start.4 = (bf16[64,256]{1,0:T(8,128)(2,1)S(1)}, bf16[64,256]{1,0:T(8,128)(2,1)S(1)}, u32[]{:S(2)}, u32[]{:S(2)}) collective-permute-start(bf16[64,256]{1,0:T(8,128)(2,1)S(1)} %get-tuple-element.7.q0), channel_id=1, source_target_pairs={{64,0},{96,32},{0,64},{32,96},{65,1},{97,33},{1,65},{33,97},{66,2}... | collective-permute-start | bytes 98312 | tf_op jit(solution)/shard_map/ppermute | solution.py:25
  98.3 5.8 %collective-permute-start.5 = (bf16[64,256]{1,0:T(8,128)(2,1)S(1)}, bf16[64,256]{1,0:T(8,128)(2,1)S(1)}, u32[]{:S(2)}, u32[]{:S(2)}) collective-permute-start(bf16[64,256]{1,0:T(8,128)(2,1)S(1)} %get-tuple-element.7.q0), channel_id=1, source_target_pairs={{96,0},{0,32},{32,64},{64,96},{97,1},{1,33},{33,65},{65,97},{98,2}... | collective-permute-start | bytes 98312 | tf_op jit(solution)/shard_map/ppermute | solution.py:25
  122.1 26.9 %all-to-all-start.4 = ((bf16[4,64,256]{2,1,0:T(8,128)(2,1)}), bf16[4,64,256]{2,1,0:T(8,128)(2,1)S(1)}, u32[]{:S(2)}, u32[]{:S(2)}) async-start(bf16[4,64,256]{2,1,0:T(8,128)(2,1)} %shard_map.77), calls=%async_computation.4 | async-start | bytes 262144 | tf_op jit(solution)/shard_map/all_to_all | solution.py:21
  151.3 11.7 %all-to-all-start.5 = ((f32[4,64,288]{2,1,0:T(8,128)}), f32[4,64,288]{2,1,0:T(8,128)S(1)}, u32[]{:S(2)}, u32[]{:S(2)}) async-start(f32[4,64,288]{2,1,0:T(8,128)} %shard_map.78), calls=%async_computation.5 | async-start | bytes 786432 | tf_op jit(solution)/shard_map/all_to_all | solution.py:21
  (3 other events, 21.2 us)

commit v4 on v3

v4 whole, which is shorter than its diff:
```python
import jax
import jax.numpy as jnp
from jax import lax
from jax.experimental import pallas as pl
from jax.experimental.pallas import tpu as pltpu
from jax.sharding import Mesh, PartitionSpec as P

D = 4608
HEAD = 128
HEADS = 32
NZ, NY, NC, NW, NX = 4, 4, 2, 4, 4
SEQ = ("z", "y", "c")
FSDP = ("w", "x")

masked_score = -1e30
epsilon = 1e-06
VMEM_BYTES = 40 * 1024 * 1024


def exchange(x, axis):
    return lax.all_to_all(x, axis, 0, 0, tiled=True)


def from_next(x, axis, step, size):
    return lax.ppermute(x, axis, [((i + step) % size, i) for i in range(size)])


def from_pair(x, axis, bit, size):
    return lax.ppermute(x, axis, [(i ^ bit, i) for i in range(size)])


def gather_y(x):
    after, before = from_next(x, "y", 1, NY), from_next(x, "y", NY - 1, NY)
    half = x.shape[0] // 2
    low = from_next(after[:half], "y", 1, NY)
    high = from_next(before[half:], "y", NY - 1, NY)
    return jnp.stack([x, after, jnp.concatenate([low, high]), before])


def swap_core(x):
    return lax.ppermute(x, "c", [(0, 1), (1, 0)])


def block_result(query, keys, values, allowed):
    scores = lax.dot_general(
        keys, query, (((1,), (1,)), ((), ())), preferred_element_type=jnp.float32
    )
    scores = jnp.where(allowed, scores, masked_score)
    best = jnp.max(scores, axis=0, keepdims=True)
    weights = jnp.exp(scores - best)
    total = jnp.where(best > 0.5 * masked_score, jnp.sum(weights, axis=0, keepdims=True), 0.0)
    numer = lax.dot_general(
        values,
        weights.astype(jnp.bfloat16),
        (((0,), (0,)), ((), ())),
        preferred_element_type=jnp.float32,
    )
    inverse = 1.0 / jnp.where(total > 0.0, total, 1.0)
    share = (numer * inverse).astype(jnp.bfloat16)
    return best, total, share


def combine(parts):
    highest = parts[0][0]
    for best, _, _ in parts[1:]:
        highest = jnp.maximum(highest, best)
    denom = 0.0
    accum = 0.0
    for best, total, share in parts:
        weight = total * jnp.exp(best - highest)
        denom = denom + weight
        accum = accum + weight * share.astype(jnp.float32)
    return highest, denom, accum


def norm_kernel(meta, tokens_ref, gain_ref, out_ref, normed_ref):
    hidden = tokens_ref[...].astype(jnp.float32)
    mean = jnp.mean(hidden * hidden, axis=-1, keepdims=True)
    normed_ref[...] = (hidden * lax.rsqrt(mean + epsilon) * gain_ref[...]).astype(jnp.bfloat16)
    first = meta[3] == 0
    span = normed_ref.shape[1] // NZ
    k_rows = span // (NY * NC)
    for k in range(NZ):
        block = meta[1] ^ k
        part = normed_ref[:, pl.ds(pl.multiple_of(block * span, span), span)]
        for y in range(NY):
            at = y * NC * k_rows
            low, high = part[:, at : at + k_rows], part[:, at + k_rows : at + 2 * k_rows]
            out_ref[y, 0, :, k * k_rows : (k + 1) * k_rows] = jnp.where(first, low, high)
            out_ref[y, 1, :, k * k_rows : (k + 1) * k_rows] = jnp.where(first, high, low)


def project_kernel(rows_ref, own_ref, other_ref, out_ref):
    own = own_ref[...].reshape(-1, own_ref.shape[2])
    other = other_ref[...].reshape(-1, other_ref.shape[2])
    peers, _, rows, depth = rows_ref.shape
    total = jnp.dot(
        rows_ref[:, 0].reshape(peers * rows, depth), own, preferred_element_type=jnp.float32
    ) + jnp.dot(
        rows_ref[:, 1].reshape(peers * rows, depth), other, preferred_element_type=jnp.float32
    )
    out_ref[...] = total.reshape(out_ref.shape)


def rotary_kernel(part_ref, cos_ref, sin_ref, q_ref, new_ref):
    total = (part_ref[0] + part_ref[1]) + (part_ref[2] + part_ref[3])
    cosine, sine_part = cos_ref[...], sin_ref[...]

    def rotated(i):
        u = total[:, i * HEAD : (i + 1) * HEAD]
        return u * cosine + pltpu.roll(u, HEAD // 2, 1) * sine_part

    scale = (D // HEADS) ** (-0.5)
    q_ref[:, :HEAD] = (rotated(0) * scale).astype(jnp.bfloat16)
    q_ref[:, HEAD:] = (rotated(1) * scale).astype(jnp.bfloat16)
    keys = rotated(2).astype(jnp.bfloat16)
    values = total[:, 3 * HEAD :].astype(jnp.bfloat16)
    for i in range(NZ * NC):
        new_ref[i, :, :HEAD] = keys
        new_ref[i, :, HEAD:] = values


def attention_kernel(meta, q0, q1, q2, q3, own_ref, other_ref, new_ref, out_ref):
    length, my_z, y, c = meta[0], meta[1], meta[2], meta[3]
    slots, new_slots = own_ref.shape[1], new_ref.shape[1]
    rows = q0.shape[0]
    lanes = 4 * rows
    slot = lax.broadcasted_iota(jnp.int32, (slots, lanes), 0)
    key = lax.broadcasted_iota(jnp.int32, (new_slots, lanes), 0)
    lane = lax.broadcasted_iota(jnp.int32, (new_slots, lanes), 1)
    for chunk, pair in enumerate(((q0, q1), (q2, q3))):
        query = jnp.concatenate(
            [q[:, h * HEAD : (h + 1) * HEAD] for q in pair for h in range(2)], axis=0
        )
        places = [lax.rem(y + 2 * chunk + i, NY) for i in range(2)]
        bases = [((my_z * NY + place) * NC + c) * rows for place in places]
        token = jnp.where(lane < 2 * rows, bases[0], bases[1]) + lane % rows
        offset = token - key
        parts = []
        for source, core in ((own_ref, c), (other_ref, 1 - c)):
            for k in range(NZ):
                start = (((my_z ^ k) * NY + y) * NC + core) * slots
                parts.append(
                    block_result(
                        query, source[k, :, :HEAD], source[k, :, HEAD:], slot < length - start
                    )
                )
        for k in range(NZ * NC):
            start = ((k // NC * NY + y) * NC + k % NC) * new_slots
            parts.append(
                block_result(query, new_ref[k, :, :HEAD], new_ref[k, :, HEAD:], offset >= start)
            )
        highest, denom, accum = combine(parts)
        row = lax.broadcasted_iota(jnp.int32, (8, 2 * rows), 0)
        for i, place in enumerate(places):
            part = slice(i * 2 * rows, (i + 1) * 2 * rows)
            out_ref[place, :HEAD, :] = accum[:, part]
            out_ref[place, HEAD:, :] = jnp.where(row == 0, highest[:, part], denom[:, part])


def merge_kernel(state_ref, out_ref):
    rows = out_ref.shape[1]
    bests = [state_ref[i, HEAD : HEAD + 1, :] for i in range(NY)]
    highest = bests[0]
    for best in bests[1:]:
        highest = jnp.maximum(highest, best)
    denom = 0.0
    accum = 0.0
    for i in range(NY):
        scale = jnp.exp(bests[i] - highest)
        denom = denom + state_ref[i, HEAD + 1 : HEAD + 2, :] * scale
        accum = accum + state_ref[i, :HEAD, :] * scale
    attention = jnp.transpose(accum / denom).astype(jnp.bfloat16)
    for i in range(NW):
        out_ref[i, :, :HEAD] = attention[:rows]
        out_ref[i, :, HEAD:] = attention[rows:]


def output_kernel(meta, att_ref, own_ref, other_ref, out_ref):
    first = meta[3] == 0
    half = own_ref.shape[2]
    for x in range(NX):
        place = lax.rem(meta[2] + x, NX)
        sums = []
        for source in (own_ref, other_ref):
            total = 0.0
            for k in range(NW):
                total = total + lax.dot_general(
                    att_ref[meta[1] ^ k],
                    source[x, k],
                    (((1,), (1,)), ((), ())),
                    preferred_element_type=jnp.float32,
                )
            sums.append(total)
        out_ref[place, :, :half] = jnp.where(first, sums[0], sums[1])
        out_ref[place, :, half:] = jnp.where(first, sums[1], sums[0])


def last_kernel(part_ref, residual_ref, out_ref):
    total = (part_ref[0] + part_ref[1]) + (part_ref[2] + part_ref[3])
    out_ref[...] = (residual_ref[...].astype(jnp.float32) + total).astype(jnp.bfloat16)


def call(kernel, out, operands, scalars=0, flops=0, scratch=(), held=()):
    count, extra = len(operands), len(held)

    def body(*refs):
        after = count + extra
        kernel(*refs[:count], *refs[after : after + len(out)], *refs[after + len(out) + extra :])

    specs = [pl.BlockSpec(memory_space=pltpu.SMEM)] * scalars
    specs += [pl.BlockSpec(memory_space=pltpu.VMEM)] * (count - scalars)
    moved = sum(o.size * o.dtype.itemsize for o in operands)
    shapes = [jax.ShapeDtypeStruct(shape, dtype) for shape, dtype in out]
    shapes += [jax.ShapeDtypeStruct(h.shape, h.dtype) for h in held]
    results = pl.pallas_call(
        body,
        out_shape=shapes,
        in_specs=specs + [pl.BlockSpec(memory_space=pl.ANY)] * extra,
        out_specs=[pl.BlockSpec(memory_space=pltpu.VMEM)] * len(out)
        + [pl.BlockSpec(memory_space=pl.ANY)] * extra,
        scratch_shapes=list(scratch),
        input_output_aliases={count + i: len(out) + i for i in range(extra)},
        compiler_params=pltpu.CompilerParams(vmem_limit_bytes=VMEM_BYTES),
        cost_estimate=pl.CostEstimate(
            flops=flops, bytes_accessed=moved, transcendentals=flops // 512
        ),
    )(*operands, *held)
    return results if len(results) > 1 else results[0]


def on_device(tokens, pre_gain, w_qkv, w_out, cache_keys, cache_values, cache_len):
    tok_rows = tokens.shape[0]
    k_rows = w_qkv.shape[0]
    bf16, f32 = jnp.bfloat16, jnp.float32
    z, y, c = (lax.axis_index(name) for name in SEQ)
    seq_index = (z * NY + y) * NC + c
    fsdp_index = lax.axis_index("w") * NX + lax.axis_index("x")
    length = cache_len[0]
    meta = jnp.stack([length, z, y, c]).astype(jnp.int32)

    w_own = jnp.stack([w_qkv] + [from_pair(w_qkv, "z", k, NZ) for k in range(1, NZ)])
    w_other = swap_core(w_own)
    cache = jnp.concatenate([cache_keys, cache_values], axis=1)
    rows_out, cache, out_block = call(
        norm_kernel,
        [((NY, NC, tok_rows, NZ * k_rows), bf16)],
        (meta, tokens, pre_gain.reshape(1, -1)),
        scalars=1,
        flops=tokens.size * 6,
        scratch=[pltpu.VMEM(tokens.shape, bf16)],
        held=(cache, w_out.T),
    )
    rows_in = exchange(rows_out, "y")
    trade = [(a * NW + b, b * NW + a) for a in range(NZ) for b in range(NW)]
    out_block = lax.ppermute(out_block, ("z", "w"), trade)
    cache = jnp.stack([cache, from_pair(cache, "z", 1, NZ)])
    partial, cache, out_block = call(
        project_kernel,
        [((NY, tok_rows, w_qkv.shape[1]), f32)],
        (rows_in, w_own, w_other),
        flops=2 * 256 * 1152 * 512,
        held=(cache, out_block),
    )
    partial = exchange(partial, "y")
    cache_own = jnp.concatenate([cache, from_pair(cache, "z", 2, NZ)])
    cache_other = swap_core(cache_own)
    out_pair = jnp.stack([out_block, from_pair(out_block, "z", 1, NZ)])

    half_dim = HEAD // 2
    inverse_freq = 10000.0 ** (-jnp.arange(half_dim, dtype=f32) / half_dim)
    positions = length + seq_index * tok_rows + jnp.arange(tok_rows, dtype=jnp.int32)
    angles = positions.astype(f32)[:, None] * inverse_freq[None, :]
    cosine, sine_part = jnp.cos(angles), jnp.sin(angles)
    cosine = jnp.concatenate([cosine, cosine], axis=1)
    sine_part = jnp.concatenate([-sine_part, sine_part], axis=1)
    queries, new, out_pair = call(
        rotary_kernel,
        [((tok_rows, 2 * HEAD), bf16), ((NZ * NC, tok_rows, 2 * HEAD), bf16)],
        (partial, cosine, sine_part),
        held=(out_pair,),
    )
    all_new = exchange(new, ("z", "c"))
    all_queries = [queries] + [from_next(queries, "y", k, NY) for k in range(1, NY)]
    out_own = gather_y(jnp.concatenate([out_pair, from_pair(out_pair, "z", 2, NZ)]))
    out_other = swap_core(out_own)

    state = call(
        attention_kernel,
        [((NY, HEAD + 8, 2 * tok_rows), f32)],
        (meta, *all_queries, cache_own, cache_other, all_new),
        scalars=1,
        flops=4 * 512 * 2560 * 128,
    )
    states = exchange(state, "y")
    attention = call(merge_kernel, [((NW, tok_rows, 2 * HEAD), bf16)], (states,))
    attention = exchange(attention, "w")
    width = D // (NW * NX)
    terms = call(
        output_kernel,
        [((NX, tok_rows, width), f32)],
        (meta, attention, out_own, out_other),
        scalars=1,
        flops=2 * 64 * 4096 * 288,
    )
    terms = exchange(terms, "x")
    residual = lax.dynamic_slice_in_dim(tokens, fsdp_index * width, width, 1)
    return call(last_kernel, [((tok_rows, width), bf16)], (terms, residual))


def solution(mesh):
    fine = Mesh(mesh.devices.reshape(NZ, NY, NC, NW, NX), SEQ + FSDP)
    return jax.shard_map(
        on_device,
        mesh=fine,
        in_specs=(
            P(SEQ, None),
            P(),
            P(SEQ, FSDP),
            P(FSDP, SEQ),
            P(SEQ, FSDP),
            P(SEQ, FSDP),
            P(),
        ),
        out_specs=P(SEQ, FSDP),
        check_vma=False,
    )
```

time: 166 us -> 175 us (1.054)
  blocking collectives: 9.62 us -> 33 us
  starting transfers between devices: 87.1 us -> 80.2 us
  waiting for transfers between devices: 41.8 us -> 37.9 us
  other arithmetic: 4 us -> 1.59 us
    all_to_all x1 -> x2, blocking collectives: 9.62 us -> 33 us  [exchange(): return lax.all_to_all(x, axis, 0, 0, tiled=True)]
    all_to_all x5 -> x4, starting transfers between devices: 31.9 us -> 19 us  [exchange(): return lax.all_to_all(x, axis, 0, 0, tiled=True)]
    all_to_all x5 -> x4, waiting for transfers between devices: 21.8 us -> 9.51 us  [exchange(): return lax.all_to_all(x, axis, 0, 0, tiled=True)]
    ppermute x6 -> x7, waiting for transfers between devices: 15.7 us -> 24.1 us  [from_pair(): return lax.ppermute(x, axis, [(i ^ bit, i) for i in range(size)])]
    ppermute x6 -> x7, starting transfers between devices: 23.8 us -> 31.5 us  [from_pair(): return lax.ppermute(x, axis, [(i ^ bit, i) for i in range(size)])]
    unnamed x11 -> x19, local copies, waits for them, and re-layouts: 1.09 us -> 3.89 us
    ppermute x7, starting transfers between devices: 25 us -> 23.1 us  [from_next(): return lax.ppermute(x, axis, [((i + step) % size, i) for i in range(size)])]
  transfers between devices with their start and end apart: 22 -> 22, of which waited for: 6 -> 10; matrix products, arithmetic and copies ran while one was open for 4% -> 0% of each run, Pallas kernels for 8% -> 6%
where the time goes in v4:
time: 175 us; the launch traced here: 173 us
  starting transfers between devices  80.2 us (46%)
  waiting for transfers between devices  37.9 us (22%)
  blocking collectives  33 us (19%)
  Pallas kernels  15.1 us (9%)
  local copies, waits for them, and re-layouts  4.04 us (2%)
    all_to_all x2, blocking collectives, exchange(): return lax.all_to_all(x, axis, 0, 0, tiled=True)  33 us
    ppermute x7, starting transfers between devices, from_pair(): return lax.ppermute(x, axis, [(i ^ bit, i) for i in range(size)])  31.5 us
    ppermute x7, waiting for transfers between devices, from_pair(): return lax.ppermute(x, axis, [(i ^ bit, i) for i in range(size)])  24.1 us
    ppermute x7, starting transfers between devices, from_next(): return lax.ppermute(x, axis, [((i + step) % size, i) for i in range(size)])  23.1 us
    all_to_all x4, starting transfers between devices, exchange(): return lax.all_to_all(x, axis, 0, 0, tiled=True)  19 us
    pallas_call x7, Pallas kernels, call(): pl.pallas_call(body, out_shape=shapes, in_specs=specs + [pl.BlockSpec(mem...  15.1 us
    all_to_all x4, waiting for transfers between devices, exchange(): return lax.all_to_all(x, axis, 0, 0, tiled=True)  9.51 us
    ppermute x3, starting transfers between devices, swap_core(): return lax.ppermute(x, 'c', [(0, 1), (1, 0)])  5.93 us
  transfers between devices with their start and end apart: 22, of which 10 were waited for; matrix products, arithmetic and copies ran while one was open for 0% of the time, Pallas kernels for 6%

profile of v4, /device:TPU:24, one launch (start us, length us, event | category | flops | bytes accessed | tf_op | source)
XLA Modules:
  0.0 172.9 jit_solution(12756138578013451983)
XLA Ops:
  1.0 6.5 %collective-permute-start.2 = (bf16[144,512]{1,0:T(8,128)(2,1)}, bf16[144,512]{1,0:T(8,128)(2,1)S(1)}, u32[]{:S(2)}, u32[]{:S(2)}) collective-permute-start(bf16[144,512]{1,0:T(8,128)(2,1)} %param.9), channel_id=1, source_target_pairs={{384,0},{256,128},{128,256},{0,384},{385,1},{257,129},{129,257},{1... | collective-permute-start | bytes 442376 | tf_op jit(solution)/shard_map/ppermute | solution.py:29
  9.4 2.5 %collective-permute-start = (bf16[144,512]{1,0:T(8,128)(2,1)}, bf16[144,512]{1,0:T(8,128)(2,1)S(1)}, u32[]{:S(2)}, u32[]{:S(2)}) collective-permute-start(bf16[144,512]{1,0:T(8,128)(2,1)} %param.9), channel_id=1, source_target_pairs={{128,0},{0,128},{384,256},{256,384},{129,1},{1,129},{385,257},{257... | collective-permute-start | bytes 442376 | tf_op jit(solution)/shard_map/ppermute | solution.py:29
  12.6 7.2 %collective-permute-done.1 = bf16[144,512]{1,0:T(8,128)(2,1)S(1)} collective-permute-done((bf16[144,512]{1,0:T(8,128)(2,1)}, bf16[144,512]{1,0:T(8,128)(2,1)S(1)}, u32[]{:S(2)}, u32[]{:S(2)}) %collective-permute-start.1) | collective-permute-done | bytes 147488 | tf_op jit(solution)/shard_map/ppermute | solution.py:29
  23.1 3.5 %shard_map.73 = (bf16[4,2,64,576]{3,2,1,0:T(8,128)(2,1)}, bf16[256,256]{1,0:T(8,128)(2,1)S(1)}, bf16[144,256]{1,0:T(8,128)(2,1)S(1)}) custom-call(s32[4]{0:T(128)S(1)} %pad_add_fusion.refs_0_, bf16[64,4608]{1,0:T(8,128)(2,1)S(1)} %copy-done, f32[1,4608]{1,0:T(1,128)S(1)} %reshape.14.refs_2_, ...), custom_call_target="tpu_custom_call", output_to_operand_aliasing={{1}: (3, {}), {2}: (4, {})} | custom-call | flops 1769472 | bytes 608272 | tf_op jit(solution)/shard_map/pallas_call | solution.py:216
  26.6 4.9 %all-to-all-start = ((bf16[4,2,64,576]{3,2,1,0:T(8,128)(2,1)}), bf16[4,2,64,576]{3,2,1,0:T(8,128)(2,1)S(1)}, u32[]{:S(2)}, u32[]{:S(2)}) async-start(bf16[4,2,64,576]{3,2,1,0:T(8,128)(2,1)} %get-tuple-element.14), calls=%async_computation | async-start | bytes 1310720 | tf_op jit(solution)/shard_map/all_to_all | solution.py:21
  31.5 2.4 %collective-permute-start.4 = (bf16[256,256]{1,0:T(8,128)(2,1)S(1)}, bf16[256,256]{1,0:T(8,128)(2,1)S(1)}, u32[]{:S(2)}, u32[]{:S(2)}) collective-permute-start(bf16[256,256]{1,0:T(8,128)(2,1)S(1)} %get-tuple-element.15), channel_id=1, source_target_pairs={{128,0},{0,128},{384,256},{256,384},{129,1},{1,129},{385,257},{257... | collective-permute-start | bytes 393224 | tf_op jit(solution)/shard_map/ppermute | solution.py:29
  34.7 4.3 %collective-permute-done.4 = bf16[256,256]{1,0:T(8,128)(2,1)S(1)} collective-permute-done((bf16[256,256]{1,0:T(8,128)(2,1)S(1)}, bf16[256,256]{1,0:T(8,128)(2,1)S(1)}, u32[]{:S(2)}, u32[]{:S(2)}) %collective-permute-start.4) | collective-permute-done | bytes 131104 | tf_op jit(solution)/shard_map/ppermute | solution.py:29
  42.6 5.5 %all-to-all-start.1 = ((f32[4,64,512]{2,1,0:T(8,128)}), f32[4,64,512]{2,1,0:T(8,128)S(1)}, u32[]{:S(2)}, u32[]{:S(2)}) async-start(f32[4,64,512]{2,1,0:T(8,128)} %get-tuple-element.17), calls=%async_computation.1 | async-start | bytes 1048576 | tf_op jit(solution)/shard_map/all_to_all | solution.py:21
  48.3 5.1 %collective-permute-start.6 = (bf16[144,256]{1,0:T(8,128)(2,1)S(1)}, bf16[144,256]{1,0:T(8,128)(2,1)S(1)}, u32[]{:S(2)}, u32[]{:S(2)}) collective-permute-start(bf16[144,256]{1,0:T(8,128)(2,1)S(1)} %get-tuple-element.18), channel_id=1, source_target_pairs={{128,0},{0,128},{384,256},{256,384},{129,1},{1,129},{385,257},{257... | collective-permute-start | bytes 221192 | tf_op jit(solution)/shard_map/ppermute | solution.py:29
  56.7 10.3 %collective-permute-start.12 = (bf16[2,144,256]{2,1,0:T(8,128)(2,1)S(1)}, bf16[2,144,256]{2,1,0:T(8,128)(2,1)S(1)}, u32[]{:S(2)}, u32[]{:S(2)}) collective-permute-start(bf16[2,144,256]{2,1,0:T(8,128)(2,1)S(1)} %get-tuple-element.22), channel_id=1, source_target_pairs={{256,0},{384,128},{0,256},{128,384},{257,1},{385,129},{1,257},{129... | collective-permute-start | bytes 442376 | tf_op jit(solution)/shard_map/ppermute | solution.py:29
  67.0 5.3 %collective-permute-done.12 = bf16[2,144,256]{2,1,0:T(8,128)(2,1)S(1)} collective-permute-done((bf16[2,144,256]{2,1,0:T(8,128)(2,1)S(1)}, bf16[2,144,256]{2,1,0:T(8,128)(2,1)S(1)}, u32[]{:S(2)}, u32[]{:S(2)}) %collective-permute-start.12) | collective-permute-done | bytes 147488 | tf_op jit(solution)/shard_map/ppermute | solution.py:29
  72.4 4.0 %collective-permute-start.15 = (bf16[4,144,256]{2,1,0:T(8,128)(2,1)S(1)}, bf16[4,144,256]{2,1,0:T(8,128)(2,1)S(1)}, u32[]{:S(2)}, u32[]{:S(2)}) collective-permute-start(bf16[4,144,256]{2,1,0:T(8,128)(2,1)S(1)} %constant_dynamic-update-slice_fusion.2), channel_id=1, source_target_pairs={{96,0},{0,32},{32,64},{64,96},{97,1},{1,33},{33,65},{65,97},{98,2}... | collective-permute-start | bytes 884744 | tf_op jit(solution)/shard_map/ppermute | solution.py:25
  78.3 2.7 %collective-permute-start.10 = (bf16[2,256,256]{2,1,0:T(8,128)(2,1)S(1)}, bf16[2,256,256]{2,1,0:T(8,128)(2,1)S(1)}, u32[]{:S(2)}, u32[]{:S(2)}) collective-permute-start(bf16[2,256,256]{2,1,0:T(8,128)(2,1)S(1)} %get-tuple-element.20), channel_id=1, source_target_pairs={{256,0},{384,128},{0,256},{128,384},{257,1},{385,129},{1,257},{129... | collective-permute-start | bytes 786440 | tf_op jit(solution)/shard_map/ppermute | solution.py:29
  81.0 4.3 %all-to-all-start.2 = ((bf16[8,64,256]{2,1,0:T(8,128)(2,1)}), bf16[8,64,256]{2,1,0:T(8,128)(2,1)S(1)}, u32[]{:S(2)}, u32[]{:S(2)}) async-start(bf16[8,64,256]{2,1,0:T(8,128)(2,1)} %get-tuple-element.21), calls=%async_computation.2 | async-start | bytes 524288 | tf_op jit(solution)/shard_map/all_to_all | solution.py:21
  85.3 5.1 %collective-permute-start.16 = (bf16[2,144,256]{2,1,0:T(8,128)(2,1)S(1)}, bf16[2,144,256]{2,1,0:T(8,128)(2,1)S(1)}, u32[]{:S(2)}, u32[]{:S(2)}) collective-permute-start(bf16[2,144,256]{2,1,0:T(8,128)(2,1)S(1)} %slice.9), channel_id=1, source_target_pairs={{96,0},{0,32},{32,64},{64,96},{97,1},{1,33},{33,65},{65,97},{98,2}... | collective-permute-start | bytes 442376 | tf_op jit(solution)/shard_map/ppermute | solution.py:25
  92.4 4.8 %collective-permute-done.10 = bf16[2,256,256]{2,1,0:T(8,128)(2,1)S(1)} collective-permute-done((bf16[2,256,256]{2,1,0:T(8,128)(2,1)S(1)}, bf16[2,256,256]{2,1,0:T(8,128)(2,1)S(1)}, u32[]{:S(2)}, u32[]{:S(2)}) %collective-permute-start.10) | collective-permute-done | bytes 262176 | tf_op jit(solution)/shard_map/ppermute | solution.py:29
  104.0 6.0 %collective-permute-start.8 = (bf16[64,256]{1,0:T(8,128)(2,1)S(1)}, bf16[64,256]{1,0:T(8,128)(2,1)S(1)}, u32[]{:S(2)}, u32[]{:S(2)}) collective-permute-start(bf16[64,256]{1,0:T(8,128)(2,1)S(1)} %get-tuple-element.19.refs_1_), channel_id=1, source_target_pairs={{64,0},{96,32},{0,64},{32,96},{65,1},{97,33},{1,65},{33,97},{66,2}... | collective-permute-start | bytes 98312 | tf_op jit(solution)/shard_map/ppermute | solution.py:25
  112.0 3.9 %collective-permute-done.9.refs_4_ = bf16[64,256]{1,0:T(8,128)(2,1)S(1)} collective-permute-done((bf16[64,256]{1,0:T(8,128)(2,1)S(1)}, bf16[64,256]{1,0:T(8,128)(2,1)S(1)}, u32[]{:S(2)}, u32[]{:S(2)}) %collective-permute-start.9) | collective-permute-done | bytes 32800 | tf_op jit(solution)/shard_map/ppermute | solution.py:25
  118.8 6.4 %shard_map.76 = f32[4,136,128]{2,1,0:T(8,128)S(1)} custom-call(s32[4]{0:T(128)S(1)} %pad_add_fusion.refs_0_, bf16[64,256]{1,0:T(8,128)(2,1)S(1)} %get-tuple-element.19.refs_1_, bf16[64,256]{1,0:T(8,128)(2,1)S(1)} %collective-permute-done.7.refs_2_, bf16[64,256]{1,0:T(8,128)(2,1)S(1)} %collective-permute-done.8.refs_3_, ...), custom_call_target="tpu_custom_call" | custom-call | flops 671088640 | bytes 1441808 | tf_op jit(solution)/shard_map/pallas_call | solution.py:216
  125.1 9.0 %all_to_all.30.refs_0_ = f32[4,136,128]{2,1,0:T(8,128)S(1)} all-to-all(f32[4,136,128]{2,1,0:T(8,128)S(1)} %shard_map.76), channel_id=1, replica_groups=mesh['z'=4,'y'=4,'c'=2,'w'=4,'x'=4] {'y'}, dimensions={0} | all-to-all | bytes 557056 | tf_op jit(solution)/shard_map/all_to_all | solution.py:21
  134.3 24.0 %all_to_all.31.refs_1_ = bf16[4,64,256]{2,1,0:T(8,128)(2,1)S(1)} all-to-all(bf16[4,64,256]{2,1,0:T(8,128)(2,1)S(1)} %shard_map.77), channel_id=1, replica_groups=mesh['z'=4,'y'=4,'c'=2,'w'=4,'x'=4] {'w'}, dimensions={0} | all-to-all | bytes 262144 | tf_op jit(solution)/shard_map/all_to_all | solution.py:21
  158.3 2.3 %shard_map.78 = f32[4,64,288]{2,1,0:T(8,128)} custom-call(s32[4]{0:T(128)S(1)} %pad_add_fusion.refs_0_, bf16[4,64,256]{2,1,0:T(8,128)(2,1)S(1)} %all_to_all.31.refs_1_, bf16[4,4,144,256]{3,2,1,0:T(8,128)(2,1)S(1)} %pad_maximum_fusion.refs_2_, bf16[4,4,144,256]{3,2,1,0:T(8,128)(2,1)S(1)} %collective-permute-done.17.refs_3_), custom_call_target="tpu_custom_call" | custom-call | flops 150994944 | bytes 2490384 | tf_op jit(solution)/shard_map/pallas_call | solution.py:216
  160.5 4.3 %all-to-all-start.5 = ((f32[4,64,288]{2,1,0:T(8,128)}), f32[4,64,288]{2,1,0:T(8,128)S(1)}, u32[]{:S(2)}, u32[]{:S(2)}) async-start(f32[4,64,288]{2,1,0:T(8,128)} %shard_map.78), calls=%async_computation.5 | async-start | bytes 786432 | tf_op jit(solution)/shard_map/all_to_all | solution.py:21
  164.9 7.3 %all-to-all-done.5.refs_0_ = f32[4,64,288]{2,1,0:T(8,128)S(1)} async-done(((f32[4,64,288]{2,1,0:T(8,128)}), f32[4,64,288]{2,1,0:T(8,128)S(1)}, u32[]{:S(2)}, u32[]{:S(2)}) %all-to-all-start.5) | async-done | bytes 294944 | tf_op jit(solution)/shard_map/all_to_all | solution.py:21
  (65 shorter events, 30.1 us)
Async XLA Ops:
  0.0 23.1 %copy-start = (bf16[64,4608]{1,0:T(8,128)(2,1)S(1)}, bf16[64,4608]{1,0:T(8,128)(2,1)}, u32[]{:S(2)}) copy-start(bf16[64,4608]{1,0:T(8,128)(2,1)} %refs_1_.1) | copy-start | bytes 1769476
  0.0 23.0 %copy-start.5 = (bf16[256,128]{1,0:T(8,128)(2,1)S(1)}, bf16[256,128]{1,0:T(8,128)(2,1)}, u32[]{:S(2)}) copy-start(bf16[256,128]{1,0:T(8,128)(2,1)} %param.12) | copy-start | bytes 196612
  1.0 11.6 %collective-permute-start.2 = (bf16[144,512]{1,0:T(8,128)(2,1)}, bf16[144,512]{1,0:T(8,128)(2,1)S(1)}, u32[]{:S(2)}, u32[]{:S(2)}) collective-permute-start(bf16[144,512]{1,0:T(8,128)(2,1)} %param.9), channel_id=1, source_target_pairs={{384,0},{256,128},{128,256},{0,384},{385,1},{257,129},{129,257},{1... | collective-permute-start | bytes 442376 | tf_op jit(solution)/shard_map/ppermute | solution.py:29
  7.5 12.3 %collective-permute-start.1 = (bf16[144,512]{1,0:T(8,128)(2,1)}, bf16[144,512]{1,0:T(8,128)(2,1)S(1)}, u32[]{:S(2)}, u32[]{:S(2)}) collective-permute-start(bf16[144,512]{1,0:T(8,128)(2,1)} %param.9), channel_id=1, source_target_pairs={{256,0},{384,128},{0,256},{128,384},{257,1},{385,129},{1,257},{129... | collective-permute-start | bytes 442376 | tf_op jit(solution)/shard_map/ppermute | solution.py:29
  9.4 10.6 %collective-permute-start = (bf16[144,512]{1,0:T(8,128)(2,1)}, bf16[144,512]{1,0:T(8,128)(2,1)S(1)}, u32[]{:S(2)}, u32[]{:S(2)}) collective-permute-start(bf16[144,512]{1,0:T(8,128)(2,1)} %param.9), channel_id=1, source_target_pairs={{128,0},{0,128},{384,256},{256,384},{129,1},{1,129},{385,257},{257... | collective-permute-start | bytes 442376 | tf_op jit(solution)/shard_map/ppermute | solution.py:29
  21.0 20.3 %collective-permute-start.3 = (bf16[4,144,512]{2,1,0:T(8,128)(2,1)S(1)}, bf16[4,144,512]{2,1,0:T(8,128)(2,1)S(1)}, u32[]{:S(2)}, u32[]{:S(2)}) collective-permute-start(bf16[4,144,512]{2,1,0:T(8,128)(2,1)S(1)} %pad_maximum_fusion.1.refs_1_), channel_id=1, source_target_pairs={{0,16},{16,0},{1,17},{17,1},{2,18},{18,2},{3,19},{19,3},{4,20},{20... | collective-permute-start | bytes 1769480 | tf_op jit(solution)/shard_map/ppermute | solution.py:41
  26.6 14.7 %all-to-all-start = ((bf16[4,2,64,576]{3,2,1,0:T(8,128)(2,1)}), bf16[4,2,64,576]{3,2,1,0:T(8,128)(2,1)S(1)}, u32[]{:S(2)}, u32[]{:S(2)}) async-start(bf16[4,2,64,576]{3,2,1,0:T(8,128)(2,1)} %get-tuple-element.14), calls=%async_computation | async-start | bytes 1310720 | tf_op jit(solution)/shard_map/all_to_all | solution.py:21
  31.5 7.5 %collective-permute-start.4 = (bf16[256,256]{1,0:T(8,128)(2,1)S(1)}, bf16[256,256]{1,0:T(8,128)(2,1)S(1)}, u32[]{:S(2)}, u32[]{:S(2)}) collective-permute-start(bf16[256,256]{1,0:T(8,128)(2,1)S(1)} %get-tuple-element.15), channel_id=1, source_target_pairs={{128,0},{0,128},{384,256},{256,384},{129,1},{1,129},{385,257},{257... | collective-permute-start | bytes 393224 | tf_op jit(solution)/shard_map/ppermute | solution.py:29
  34.0 5.1 %collective-permute-start.5 = (bf16[144,256]{1,0:T(8,128)(2,1)S(1)}, bf16[144,256]{1,0:T(8,128)(2,1)S(1)}, u32[]{:S(2)}, u32[]{:S(2)}) collective-permute-start(bf16[144,256]{1,0:T(8,128)(2,1)S(1)} %get-tuple-element.16), channel_id=1, source_target_pairs={{0,0},{4,128},{8,256},{12,384},{128,4},{132,132},{136,260},{140,38... | collective-permute-start | bytes 221192 | tf_op jit(solution)/shard_map/ppermute | solution.py:256
  42.6 13.2 %all-to-all-start.1 = ((f32[4,64,512]{2,1,0:T(8,128)}), f32[4,64,512]{2,1,0:T(8,128)S(1)}, u32[]{:S(2)}, u32[]{:S(2)}) async-start(f32[4,64,512]{2,1,0:T(8,128)} %get-tuple-element.17), calls=%async_computation.1 | async-start | bytes 1048576 | tf_op jit(solution)/shard_map/all_to_all | solution.py:21
  48.3 7.5 %collective-permute-start.6 = (bf16[144,256]{1,0:T(8,128)(2,1)S(1)}, bf16[144,256]{1,0:T(8,128)(2,1)S(1)}, u32[]{:S(2)}, u32[]{:S(2)}) collective-permute-start(bf16[144,256]{1,0:T(8,128)(2,1)S(1)} %get-tuple-element.18), channel_id=1, source_target_pairs={{128,0},{0,128},{384,256},{256,384},{129,1},{1,129},{385,257},{257... | collective-permute-start | bytes 221192 | tf_op jit(solution)/shard_map/ppermute | solution.py:29
  56.7 15.7 %collective-permute-start.12 = (bf16[2,144,256]{2,1,0:T(8,128)(2,1)S(1)}, bf16[2,144,256]{2,1,0:T(8,128)(2,1)S(1)}, u32[]{:S(2)}, u32[]{:S(2)}) collective-permute-start(bf16[2,144,256]{2,1,0:T(8,128)(2,1)S(1)} %get-tuple-element.22), channel_id=1, source_target_pairs={{256,0},{384,128},{0,256},{128,384},{257,1},{385,129},{1,257},{129... | collective-permute-start | bytes 442376 | tf_op jit(solution)/shard_map/ppermute | solution.py:29
  72.4 12.9 %collective-permute-start.15 = (bf16[4,144,256]{2,1,0:T(8,128)(2,1)S(1)}, bf16[4,144,256]{2,1,0:T(8,128)(2,1)S(1)}, u32[]{:S(2)}, u32[]{:S(2)}) collective-permute-start(bf16[4,144,256]{2,1,0:T(8,128)(2,1)S(1)} %constant_dynamic-update-slice_fusion.2), channel_id=1, source_target_pairs={{96,0},{0,32},{32,64},{64,96},{97,1},{1,33},{33,65},{65,97},{98,2}... | collective-permute-start | bytes 884744 | tf_op jit(solution)/shard_map/ppermute | solution.py:25
  76.4 14.1 %collective-permute-start.13 = (bf16[4,144,256]{2,1,0:T(8,128)(2,1)S(1)}, bf16[4,144,256]{2,1,0:T(8,128)(2,1)S(1)}, u32[]{:S(2)}, u32[]{:S(2)}) collective-permute-start(bf16[4,144,256]{2,1,0:T(8,128)(2,1)S(1)} %constant_dynamic-update-slice_fusion.2), channel_id=1, source_target_pairs={{32,0},{64,32},{96,64},{0,96},{33,1},{65,33},{97,65},{1,97},{34,2}... | collective-permute-start | bytes 884744 | tf_op jit(solution)/shard_map/ppermute | solution.py:25
  78.3 18.9 %collective-permute-start.10 = (bf16[2,256,256]{2,1,0:T(8,128)(2,1)S(1)}, bf16[2,256,256]{2,1,0:T(8,128)(2,1)S(1)}, u32[]{:S(2)}, u32[]{:S(2)}) collective-permute-start(bf16[2,256,256]{2,1,0:T(8,128)(2,1)S(1)} %get-tuple-element.20), channel_id=1, source_target_pairs={{256,0},{384,128},{0,256},{128,384},{257,1},{385,129},{1,257},{129... | collective-permute-start | bytes 786440 | tf_op jit(solution)/shard_map/ppermute | solution.py:29
  81.0 35.7 %all-to-all-start.2 = ((bf16[8,64,256]{2,1,0:T(8,128)(2,1)}), bf16[8,64,256]{2,1,0:T(8,128)(2,1)S(1)}, u32[]{:S(2)}, u32[]{:S(2)}) async-start(bf16[8,64,256]{2,1,0:T(8,128)(2,1)} %get-tuple-element.21), calls=%async_computation.2 | async-start | bytes 524288 | tf_op jit(solution)/shard_map/all_to_all | solution.py:21
  85.3 13.9 %collective-permute-start.16 = (bf16[2,144,256]{2,1,0:T(8,128)(2,1)S(1)}, bf16[2,144,256]{2,1,0:T(8,128)(2,1)S(1)}, u32[]{:S(2)}, u32[]{:S(2)}) collective-permute-start(bf16[2,144,256]{2,1,0:T(8,128)(2,1)S(1)} %slice.9), channel_id=1, source_target_pairs={{96,0},{0,32},{32,64},{64,96},{97,1},{1,33},{33,65},{65,97},{98,2}... | collective-permute-start | bytes 442376 | tf_op jit(solution)/shard_map/ppermute | solution.py:25
  90.5 9.1 %collective-permute-start.14 = (bf16[2,144,256]{2,1,0:T(8,128)(2,1)S(1)}, bf16[2,144,256]{2,1,0:T(8,128)(2,1)S(1)}, u32[]{:S(2)}, u32[]{:S(2)}) collective-permute-start(bf16[2,144,256]{2,1,0:T(8,128)(2,1)S(1)} %slice.8), channel_id=1, source_target_pairs={{32,0},{64,32},{96,64},{0,96},{33,1},{65,33},{97,65},{1,97},{34,2}... | collective-permute-start | bytes 442376 | tf_op jit(solution)/shard_map/ppermute | solution.py:25
  97.3 18.6 %collective-permute-start.11 = (bf16[4,256,256]{2,1,0:T(8,128)(2,1)S(1)}, bf16[4,256,256]{2,1,0:T(8,128)(2,1)S(1)}, u32[]{:S(2)}, u32[]{:S(2)}) collective-permute-start(bf16[4,256,256]{2,1,0:T(8,128)(2,1)S(1)} %constant_dynamic-update-slice_fusion.refs_5_), channel_id=1, source_target_pairs={{0,16},{16,0},{1,17},{17,1},{2,18},{18,2},{3,19},{19,3},{4,20},{20... | collective-permute-start | bytes 1572872 | tf_op jit(solution)/shard_map/ppermute | solution.py:41
  99.7 58.5 %collective-permute-start.17 = (bf16[4,4,144,256]{3,2,1,0:T(8,128)(2,1)S(1)}, bf16[4,4,144,256]{3,2,1,0:T(8,128)(2,1)S(1)}, u32[]{:S(2)}, u32[]{:S(2)}) collective-permute-start(bf16[4,4,144,256]{3,2,1,0:T(8,128)(2,1)S(1)} %pad_maximum_fusion.refs_2_), channel_id=1, source_target_pairs={{0,16},{16,0},{1,17},{17,1},{2,18},{18,2},{3,19},{19,3},{4,20},{20... | collective-permute-start | bytes 3538952 | tf_op jit(solution)/shard_map/ppermute | solution.py:41
  101.8 10.2 %collective-permute-start.7 = (bf16[64,256]{1,0:T(8,128)(2,1)S(1)}, bf16[64,256]{1,0:T(8,128)(2,1)S(1)}, u32[]{:S(2)}, u32[]{:S(2)}) collective-permute-start(bf16[64,256]{1,0:T(8,128)(2,1)S(1)} %get-tuple-element.19.refs_1_), channel_id=1, source_target_pairs={{32,0},{64,32},{96,64},{0,96},{33,1},{65,33},{97,65},{1,97},{34,2}... | collective-permute-start | bytes 98312 | tf_op jit(solution)/shard_map/ppermute | solution.py:25
  104.0 8.0 %collective-permute-start.8 = (bf16[64,256]{1,0:T(8,128)(2,1)S(1)}, bf16[64,256]{1,0:T(8,128)(2,1)S(1)}, u32[]{:S(2)}, u32[]{:S(2)}) collective-permute-start(bf16[64,256]{1,0:T(8,128)(2,1)S(1)} %get-tuple-element.19.refs_1_), channel_id=1, source_target_pairs={{64,0},{96,32},{0,64},{32,96},{65,1},{97,33},{1,65},{33,97},{66,2}... | collective-permute-start | bytes 98312 | tf_op jit(solution)/shard_map/ppermute | solution.py:25
  110.1 5.8 %collective-permute-start.9 = (bf16[64,256]{1,0:T(8,128)(2,1)S(1)}, bf16[64,256]{1,0:T(8,128)(2,1)S(1)}, u32[]{:S(2)}, u32[]{:S(2)}) collective-permute-start(bf16[64,256]{1,0:T(8,128)(2,1)S(1)} %get-tuple-element.19.refs_1_), channel_id=1, source_target_pairs={{96,0},{0,32},{32,64},{64,96},{97,1},{1,33},{33,65},{65,97},{98,2}... | collective-permute-start | bytes 98312 | tf_op jit(solution)/shard_map/ppermute | solution.py:25
  160.5 11.7 %all-to-all-start.5 = ((f32[4,64,288]{2,1,0:T(8,128)}), f32[4,64,288]{2,1,0:T(8,128)S(1)}, u32[]{:S(2)}, u32[]{:S(2)}) async-start(f32[4,64,288]{2,1,0:T(8,128)} %shard_map.78), calls=%async_computation.5 | async-start | bytes 786432 | tf_op jit(solution)/shard_map/all_to_all | solution.py:21
  (6 other events, 51.4 us)

commit v5 on v4

v5 whole, which is shorter than its diff:
```python
import jax
import jax.numpy as jnp
from jax import lax
from jax.experimental import pallas as pl
from jax.experimental.pallas import tpu as pltpu
from jax.sharding import Mesh, PartitionSpec as P

D = 4608
HEAD = 128
HEADS = 32
NZ, NY, NC, NW, NX = 4, 4, 2, 4, 4
SEQ = ("z", "y", "c")
FSDP = ("w", "x")

masked_score = -1e30
epsilon = 1e-06
VMEM_BYTES = 40 * 1024 * 1024


def exchange(x, axis):
    return lax.all_to_all(x, axis, 0, 0, tiled=True)


def from_next(x, axis, step, size):
    return lax.ppermute(x, axis, [((i + step) % size, i) for i in range(size)])


def from_pair(x, axis, bit, size):
    return lax.ppermute(x, axis, [(i ^ bit, i) for i in range(size)])


def stack_z(x):
    return jnp.stack([x] + [from_pair(x, "z", k, NZ) for k in range(1, NZ)])


def block_result(query, keys, values, allowed):
    scores = lax.dot_general(
        keys, query, (((1,), (1,)), ((), ())), preferred_element_type=jnp.float32
    )
    scores = jnp.where(allowed, scores, masked_score)
    best = jnp.max(scores, axis=0, keepdims=True)
    weights = jnp.exp(scores - best)
    total = jnp.where(best > 0.5 * masked_score, jnp.sum(weights, axis=0, keepdims=True), 0.0)
    numer = lax.dot_general(
        values,
        weights.astype(jnp.bfloat16),
        (((0,), (0,)), ((), ())),
        preferred_element_type=jnp.float32,
    )
    inverse = 1.0 / jnp.where(total > 0.0, total, 1.0)
    share = (numer * inverse).astype(jnp.bfloat16)
    return best, total, share


def combine(parts):
    highest = parts[0][0]
    for best, _, _ in parts[1:]:
        highest = jnp.maximum(highest, best)
    denom = 0.0
    accum = 0.0
    for best, total, share in parts:
        weight = total * jnp.exp(best - highest)
        denom = denom + weight
        accum = accum + weight * share.astype(jnp.float32)
    return highest, denom, accum


def norm_kernel(meta, tokens_ref, gain_ref, out_ref, normed_ref):
    hidden = tokens_ref[...].astype(jnp.float32)
    mean = jnp.mean(hidden * hidden, axis=-1, keepdims=True)
    normed_ref[...] = (hidden * lax.rsqrt(mean + epsilon) * gain_ref[...]).astype(jnp.bfloat16)
    span = normed_ref.shape[1] // NZ
    k_rows = span // (NY * NC)
    for k in range(NZ):
        block = meta[1] ^ k
        part = normed_ref[:, pl.ds(pl.multiple_of(block * span, span), span)]
        for i in range(NY * NC):
            piece = part[:, i * k_rows : (i + 1) * k_rows]
            out_ref[i, :, k * k_rows : (k + 1) * k_rows] = piece


def project_kernel(rows_ref, w0, w1, w2, w3, out_ref):
    weights = jnp.concatenate([w[...] for w in (w0, w1, w2, w3)], axis=0)
    peers, rows, depth = rows_ref.shape
    total = jnp.dot(
        rows_ref[...].reshape(peers * rows, depth), weights, preferred_element_type=jnp.float32
    )
    out_ref[...] = total.reshape(out_ref.shape)


def rotary_kernel(part_ref, cos_ref, sin_ref, q_ref, new_ref):
    total = part_ref[0]
    for i in range(1, part_ref.shape[0]):
        total = total + part_ref[i]
    cosine, sine_part = cos_ref[...], sin_ref[...]

    def rotated(i):
        u = total[:, i * HEAD : (i + 1) * HEAD]
        return u * cosine + pltpu.roll(u, HEAD // 2, 1) * sine_part

    scale = (D // HEADS) ** (-0.5)
    first = (rotated(0) * scale).astype(jnp.bfloat16)
    second = (rotated(1) * scale).astype(jnp.bfloat16)
    for i in range(NY * NC):
        q_ref[i, :, :HEAD] = first
        q_ref[i, :, HEAD:] = second
    new_ref[:, :HEAD] = rotated(2).astype(jnp.bfloat16)
    new_ref[:, HEAD:] = total[:, 3 * HEAD :].astype(jnp.bfloat16)


def attention_kernel(meta, q_ref, cache_ref, n0, n1, n2, n3, out_ref):
    length, my_z, y, c = meta[0], meta[1], meta[2], meta[3]
    slots, new_slots = cache_ref.shape[1], n0.shape[0]
    rows = q_ref.shape[1]
    lanes = 4 * rows
    slot = lax.broadcasted_iota(jnp.int32, (slots, lanes), 0)
    key = lax.broadcasted_iota(jnp.int32, (new_slots, lanes), 0)
    lane = lax.broadcasted_iota(jnp.int32, (new_slots, lanes), 1)
    row = lax.broadcasted_iota(jnp.int32, (8, 2 * rows), 0)
    blocks = [((my_z ^ k) * NY + y) * NC + c for k in range(NZ)]
    for pair in range(NY):
        query = jnp.concatenate(
            [
                q_ref[2 * pair + i, :, h * HEAD : (h + 1) * HEAD]
                for i in range(NC)
                for h in range(2)
            ],
            axis=0,
        )
        base = (my_z * NY + pair) * NC * rows
        offset = base + jnp.where(lane < 2 * rows, 0, rows) + lane % rows - key
        parts = []
        for k in range(NZ):
            parts.append(
                block_result(
                    query,
                    cache_ref[k, :, :HEAD],
                    cache_ref[k, :, HEAD:],
                    slot < length - blocks[k] * slots,
                )
            )
        for k, new in enumerate((n0, n1, n2, n3)):
            parts.append(
                block_result(
                    query, new[:, :HEAD], new[:, HEAD:], offset >= blocks[k] * new_slots
                )
            )
        highest, denom, accum = combine(parts)
        for i in range(NC):
            part = slice(i * 2 * rows, (i + 1) * 2 * rows)
            out_ref[2 * pair + i, :HEAD, :] = accum[:, part]
            out_ref[2 * pair + i, HEAD:, :] = jnp.where(row == 0, highest[:, part], denom[:, part])


def merge_kernel(state_ref, out_ref):
    rows = out_ref.shape[1]
    bests = [state_ref[i, HEAD : HEAD + 1, :] for i in range(NY * NC)]
    highest = bests[0]
    for best in bests[1:]:
        highest = jnp.maximum(highest, best)
    denom = 0.0
    accum = 0.0
    for i in range(NY * NC):
        scale = jnp.exp(bests[i] - highest)
        denom = denom + state_ref[i, HEAD + 1 : HEAD + 2, :] * scale
        accum = accum + state_ref[i, :HEAD, :] * scale
    attention = jnp.transpose(accum / denom).astype(jnp.bfloat16)
    for i in range(NW * NC):
        out_ref[i, :, :HEAD] = attention[:rows]
        out_ref[i, :, HEAD:] = attention[rows:]


def output_kernel(meta, att_ref, b0, b1, b2, b3, out_ref):
    rows = att_ref.shape[1]
    att = [
        att_ref[pl.ds((meta[1] ^ k) * NC, NC)].reshape(NC * rows, att_ref.shape[2])
        for k in range(NW)
    ]
    for step, block in enumerate((b0, b1, b2, b3)):
        place = lax.rem(meta[2] + step, NX)
        total = 0.0
        for k in range(NW):
            total = total + lax.dot_general(
                att[k], block[k], (((1,), (1,)), ((), ())), preferred_element_type=jnp.float32
            )
        for i in range(NC):
            out_ref[place * NC + i] = total[i * rows : (i + 1) * rows]


def last_kernel(part_ref, residual_ref, out_ref):
    half = part_ref.shape[2]
    for j in range(NC):
        total = (part_ref[j] + part_ref[NC + j]) + (part_ref[2 * NC + j] + part_ref[3 * NC + j])
        at = slice(j * half, (j + 1) * half)
        out_ref[:, at] = (residual_ref[:, at].astype(jnp.float32) + total).astype(jnp.bfloat16)


def call(kernel, out, operands, scalars=0, flops=0, scratch=(), held=()):
    count, extra = len(operands), len(held)

    def body(*refs):
        after = count + extra
        kernel(*refs[:count], *refs[after : after + len(out)], *refs[after + len(out) + extra :])

    specs = [pl.BlockSpec(memory_space=pltpu.SMEM)] * scalars
    specs += [pl.BlockSpec(memory_space=pltpu.VMEM)] * (count - scalars)
    moved = sum(o.size * o.dtype.itemsize for o in operands)
    shapes = [jax.ShapeDtypeStruct(shape, dtype) for shape, dtype in out]
    shapes += [jax.ShapeDtypeStruct(h.shape, h.dtype) for h in held]
    results = pl.pallas_call(
        body,
        out_shape=shapes,
        in_specs=specs + [pl.BlockSpec(memory_space=pl.ANY)] * extra,
        out_specs=[pl.BlockSpec(memory_space=pltpu.VMEM)] * len(out)
        + [pl.BlockSpec(memory_space=pl.ANY)] * extra,
        scratch_shapes=list(scratch),
        input_output_aliases={count + i: len(out) + i for i in range(extra)},
        compiler_params=pltpu.CompilerParams(vmem_limit_bytes=VMEM_BYTES),
        cost_estimate=pl.CostEstimate(
            flops=flops, bytes_accessed=moved, transcendentals=flops // 512
        ),
    )(*operands, *held)
    return results if len(results) > 1 else results[0]


def on_device(tokens, pre_gain, w_qkv, w_out, cache_keys, cache_values, cache_len):
    tok_rows = tokens.shape[0]
    k_rows = w_qkv.shape[0]
    bf16, f32 = jnp.bfloat16, jnp.float32
    z, y, c = (lax.axis_index(name) for name in SEQ)
    seq_index = (z * NY + y) * NC + c
    fsdp_index = lax.axis_index("w") * NX + lax.axis_index("x")
    length = cache_len[0]
    meta = jnp.stack([length, z, y, c]).astype(jnp.int32)

    rows_out = call(
        norm_kernel,
        [((NY * NC, tok_rows, NZ * k_rows), bf16)],
        (meta, tokens, pre_gain.reshape(1, -1)),
        scalars=1,
        flops=tokens.size * 6,
        scratch=[pltpu.VMEM(tokens.shape, bf16)],
    )
    rows_in = exchange(rows_out, ("y", "c"))
    weights = [w_qkv] + [from_pair(w_qkv, "z", k, NZ) for k in range(1, NZ)]
    trade = [(a * NW + b, b * NW + a) for a in range(NZ) for b in range(NW)]
    out_block = lax.ppermute(w_out.T, ("z", "w"), trade)
    cache = jnp.concatenate([cache_keys, cache_values], axis=1)
    cache = jnp.stack([cache, from_pair(cache, "z", 1, NZ)])
    partial, cache, out_block = call(
        project_kernel,
        [((NY * NC, tok_rows, w_qkv.shape[1]), f32)],
        (rows_in, *weights),
        flops=2 * 256 * 1152 * 512,
        held=(cache, out_block),
    )
    partial = exchange(partial, ("y", "c"))
    cache = jnp.concatenate([cache, from_pair(cache, "z", 2, NZ)])
    out_pair = jnp.stack([out_block, from_pair(out_block, "z", 1, NZ)])

    half_dim = HEAD // 2
    inverse_freq = 10000.0 ** (-jnp.arange(half_dim, dtype=f32) / half_dim)
    positions = length + seq_index * tok_rows + jnp.arange(tok_rows, dtype=jnp.int32)
    angles = positions.astype(f32)[:, None] * inverse_freq[None, :]
    cosine, sine_part = jnp.cos(angles), jnp.sin(angles)
    cosine = jnp.concatenate([cosine, cosine], axis=1)
    sine_part = jnp.concatenate([-sine_part, sine_part], axis=1)
    queries, new, out_pair = call(
        rotary_kernel,
        [((NY * NC, tok_rows, 2 * HEAD), bf16), ((tok_rows, 2 * HEAD), bf16)],
        (partial, cosine, sine_part),
        held=(out_pair,),
    )
    all_queries = exchange(queries, ("y", "c"))
    all_new = [new] + [from_pair(new, "z", k, NZ) for k in range(1, NZ)]
    out_z = jnp.concatenate([out_pair, from_pair(out_pair, "z", 2, NZ)])

    state, out_z = call(
        attention_kernel,
        [((NY * NC, HEAD + 8, 2 * tok_rows), f32)],
        (meta, all_queries, cache, *all_new),
        scalars=1,
        flops=4 * 512 * 2560 * 128,
        held=(out_z,),
    )
    states = exchange(state, ("y", "c"))
    out_weights = [out_z] + [from_next(out_z, "y", k, NY) for k in range(1, NY)]
    attention = call(merge_kernel, [((NW * NC, tok_rows, 2 * HEAD), bf16)], (states,))
    attention = exchange(attention, ("w", "c"))
    width = D // (NW * NX)
    terms = call(
        output_kernel,
        [((NX * NC, tok_rows, width // NC), f32)],
        (meta, attention, *out_weights),
        scalars=1,
        flops=2 * 64 * 4096 * 288,
    )
    terms = exchange(terms, ("x", "c"))
    residual = lax.dynamic_slice_in_dim(tokens, fsdp_index * width, width, 1)
    return call(last_kernel, [((tok_rows, width), bf16)], (terms, residual))


def solution(mesh):
    fine = Mesh(mesh.devices.reshape(NZ, NY, NC, NW, NX), SEQ + FSDP)
    return jax.shard_map(
        on_device,
        mesh=fine,
        in_specs=(
            P(SEQ, None),
            P(),
            P(SEQ, FSDP),
            P(FSDP, SEQ),
            P(SEQ, FSDP),
            P(SEQ, FSDP),
            P(),
        ),
        out_specs=P(SEQ, FSDP),
        check_vma=False,
    )
```

time: 175 us -> 157 us (0.90)
  the two profiles are of different devices: /device:TPU:24 before, /device:TPU:1 now
where the time goes in v5:
time: 157 us; the launch traced here: 156 us
  starting transfers between devices  84.7 us (54%)
  waiting for transfers between devices  37.1 us (24%)
  blocking collectives  16.1 us (10%)
  Pallas kernels  14.7 us (9%)
  local copies, waits for them, and re-layouts  2.13 us (1%)
    ppermute x10, starting transfers between devices, from_pair(): return lax.ppermute(x, axis, [(i ^ bit, i) for i in range(size)])  39.5 us
    all_to_all x5, starting transfers between devices, exchange(): return lax.all_to_all(x, axis, 0, 0, tiled=True)  36.8 us
    all_to_all x1, blocking collectives, exchange(): return lax.all_to_all(x, axis, 0, 0, tiled=True)  16.1 us
    ppermute x10, waiting for transfers between devices, from_pair(): return lax.ppermute(x, axis, [(i ^ bit, i) for i in range(size)])  14.9 us
    pallas_call x7, Pallas kernels, call(): pl.pallas_call(body, out_shape=shapes, in_specs=specs + [pl.BlockSpec(mem...  14.7 us
    ppermute x3, waiting for transfers between devices, from_next(): return lax.ppermute(x, axis, [((i + step) % size, i) for i in range(size)])  13.6 us
    all_to_all x5, waiting for transfers between devices, exchange(): return lax.all_to_all(x, axis, 0, 0, tiled=True)  8.57 us
    ppermute x3, starting transfers between devices, from_next(): return lax.ppermute(x, axis, [((i + step) % size, i) for i in range(size)])  7.8 us
  transfers between devices with their start and end apart: 19, of which 7 were waited for; matrix products, arithmetic and copies ran while one was open for 1% of the time, Pallas kernels for 1%

profile of v5, /device:TPU:1, one launch (start us, length us, event | category | flops | bytes accessed | tf_op | source)
XLA Modules:
  0.0 156.2 jit_solution(16205791685098204729)
XLA Ops:
  1.9 2.7 %shard_map.73 = bf16[8,64,576]{2,1,0:T(8,128)(2,1)} custom-call(s32[4]{0:T(128)S(1)} %pad_add_fusion.refs_0_, bf16[64,4608]{1,0:T(8,128)(2,1)S(1)} %copy-done, f32[1,4608]{1,0:T(1,128)S(1)} %reshape.14.refs_2_), custom_call_target="tpu_custom_call" | custom-call | flops 1769472 | bytes 608272 | tf_op jit(solution)/shard_map/pallas_call | solution.py:210
  4.6 10.5 %all-to-all-start = ((bf16[8,64,576]{2,1,0:T(8,128)(2,1)}), bf16[8,64,576]{2,1,0:T(8,128)(2,1)S(1)}, u32[]{:S(2)}, u32[]{:S(2)}) async-start(bf16[8,64,576]{2,1,0:T(8,128)(2,1)} %shard_map.73), calls=%async_computation | async-start | bytes 1310720 | tf_op jit(solution)/shard_map/all_to_all | solution.py:21
  17.2 3.4 %collective-permute-start = (bf16[144,512]{1,0:T(8,128)(2,1)S(1)}, bf16[144,512]{1,0:T(8,128)(2,1)S(1)}, u32[]{:S(2)}, u32[]{:S(2)}) collective-permute-start(bf16[144,512]{1,0:T(8,128)(2,1)S(1)} %copy-done.1), channel_id=1, source_target_pairs={{128,0},{0,128},{384,256},{256,384},{129,1},{1,129},{385,257},{257... | collective-permute-start | bytes 442376 | tf_op jit(solution)/shard_map/ppermute | solution.py:29
  22.5 4.0 %collective-permute-start.2 = (bf16[144,512]{1,0:T(8,128)(2,1)S(1)}, bf16[144,512]{1,0:T(8,128)(2,1)S(1)}, u32[]{:S(2)}, u32[]{:S(2)}) collective-permute-start(bf16[144,512]{1,0:T(8,128)(2,1)S(1)} %copy-done.1), channel_id=1, source_target_pairs={{384,0},{256,128},{128,256},{0,384},{385,1},{257,129},{129,257},{1... | collective-permute-start | bytes 442376 | tf_op jit(solution)/shard_map/ppermute | solution.py:29
  27.2 8.7 %collective-permute-done.1.refs_3_ = bf16[144,512]{1,0:T(8,128)(2,1)S(1)} collective-permute-done((bf16[144,512]{1,0:T(8,128)(2,1)S(1)}, bf16[144,512]{1,0:T(8,128)(2,1)S(1)}, u32[]{:S(2)}, u32[]{:S(2)}) %collective-permute-start.1) | collective-permute-done | bytes 147488 | tf_op jit(solution)/shard_map/ppermute | solution.py:29
  37.5 5.1 %all-to-all-start.1 = ((f32[8,64,512]{2,1,0:T(8,128)}), f32[8,64,512]{2,1,0:T(8,128)S(1)}, u32[]{:S(2)}, u32[]{:S(2)}) async-start(f32[8,64,512]{2,1,0:T(8,128)} %get-tuple-element.13), calls=%async_computation.1 | async-start | bytes 2097152 | tf_op jit(solution)/shard_map/all_to_all | solution.py:21
  42.6 8.2 %collective-permute-start.6 = (bf16[2,256,256]{2,1,0:T(8,128)(2,1)S(1)}, bf16[2,256,256]{2,1,0:T(8,128)(2,1)S(1)}, u32[]{:S(2)}, u32[]{:S(2)}) collective-permute-start(bf16[2,256,256]{2,1,0:T(8,128)(2,1)S(1)} %get-tuple-element.16), channel_id=1, source_target_pairs={{256,0},{384,128},{0,256},{128,384},{257,1},{385,129},{1,257},{129... | collective-permute-start | bytes 786440 | tf_op jit(solution)/shard_map/ppermute | solution.py:29
  51.0 3.0 %collective-permute-start.5 = (bf16[144,256]{1,0:T(8,128)(2,1)S(1)}, bf16[144,256]{1,0:T(8,128)(2,1)S(1)}, u32[]{:S(2)}, u32[]{:S(2)}) collective-permute-start(bf16[144,256]{1,0:T(8,128)(2,1)S(1)} %get-tuple-element.14), channel_id=1, source_target_pairs={{128,0},{0,128},{384,256},{256,384},{129,1},{1,129},{385,257},{257... | collective-permute-start | bytes 221192 | tf_op jit(solution)/shard_map/ppermute | solution.py:29
  54.1 4.0 %collective-permute-done.5 = bf16[144,256]{1,0:T(8,128)(2,1)S(1)} collective-permute-done((bf16[144,256]{1,0:T(8,128)(2,1)S(1)}, bf16[144,256]{1,0:T(8,128)(2,1)S(1)}, u32[]{:S(2)}, u32[]{:S(2)}) %collective-permute-start.5) | collective-permute-done | bytes 73760 | tf_op jit(solution)/shard_map/ppermute | solution.py:29
  59.0 7.7 %collective-permute-start.10 = (bf16[2,144,256]{2,1,0:T(8,128)(2,1)S(1)}, bf16[2,144,256]{2,1,0:T(8,128)(2,1)S(1)}, u32[]{:S(2)}, u32[]{:S(2)}) collective-permute-start(bf16[2,144,256]{2,1,0:T(8,128)(2,1)S(1)} %get-tuple-element.18), channel_id=1, source_target_pairs={{256,0},{384,128},{0,256},{128,384},{257,1},{385,129},{1,257},{129... | collective-permute-start | bytes 442376 | tf_op jit(solution)/shard_map/ppermute | solution.py:29
  66.7 4.5 %all-to-all-start.2 = ((bf16[8,64,256]{2,1,0:T(8,128)(2,1)}), bf16[8,64,256]{2,1,0:T(8,128)(2,1)S(1)}, u32[]{:S(2)}, u32[]{:S(2)}) async-start(bf16[8,64,256]{2,1,0:T(8,128)(2,1)} %get-tuple-element.15), calls=%async_computation.2 | async-start | bytes 524288 | tf_op jit(solution)/shard_map/all_to_all | solution.py:21
  71.2 3.0 %collective-permute-start.7 = (bf16[64,256]{1,0:T(8,128)(2,1)S(1)}, bf16[64,256]{1,0:T(8,128)(2,1)S(1)}, u32[]{:S(2)}, u32[]{:S(2)}) collective-permute-start(bf16[64,256]{1,0:T(8,128)(2,1)S(1)} %get-tuple-element.17.refs_3_), channel_id=1, source_target_pairs={{128,0},{0,128},{384,256},{256,384},{129,1},{1,129},{385,257},{257... | collective-permute-start | bytes 98312 | tf_op jit(solution)/shard_map/ppermute | solution.py:29
  76.2 4.4 %collective-permute-start.9 = (bf16[64,256]{1,0:T(8,128)(2,1)S(1)}, bf16[64,256]{1,0:T(8,128)(2,1)S(1)}, u32[]{:S(2)}, u32[]{:S(2)}) collective-permute-start(bf16[64,256]{1,0:T(8,128)(2,1)S(1)} %get-tuple-element.17.refs_3_), channel_id=1, source_target_pairs={{384,0},{256,128},{128,256},{0,384},{385,1},{257,129},{129,257},{1... | collective-permute-start | bytes 98312 | tf_op jit(solution)/shard_map/ppermute | solution.py:29
  80.6 2.1 %collective-permute-done.9.refs_6_ = bf16[64,256]{1,0:T(8,128)(2,1)S(1)} collective-permute-done((bf16[64,256]{1,0:T(8,128)(2,1)S(1)}, bf16[64,256]{1,0:T(8,128)(2,1)S(1)}, u32[]{:S(2)}, u32[]{:S(2)}) %collective-permute-start.9) | collective-permute-done | bytes 32800 | tf_op jit(solution)/shard_map/ppermute | solution.py:29
  82.7 6.2 %shard_map.76 = (f32[8,136,128]{2,1,0:T(8,128)S(1)}, bf16[4,144,256]{2,1,0:T(8,128)(2,1)S(1)}) custom-call(s32[4]{0:T(128)S(1)} %pad_add_fusion.refs_0_, bf16[8,64,256]{2,1,0:T(8,128)(2,1)S(1)} %all-to-all-done.2.refs_1_, bf16[4,256,256]{2,1,0:T(8,128)(2,1)S(1)} %pad_maximum_fusion.refs_2_, ...), custom_call_target="tpu_custom_call", output_to_operand_aliasing={{1}: (7, {})} | custom-call | flops 671088640 | bytes 917520 | tf_op jit(solution)/shard_map/pallas_call | solution.py:210
  89.0 16.1 %all_to_all.30.refs_0_ = f32[8,136,128]{2,1,0:T(8,128)S(1)} all-to-all(f32[8,136,128]{2,1,0:T(8,128)S(1)} %get-tuple-element.19), channel_id=1, replica_groups=mesh['z'=4,'y'=4,'c'=2,'w'=4,'x'=4] {'y','c'}, dimensions={0} | all-to-all | bytes 1114112 | tf_op jit(solution)/shard_map/all_to_all | solution.py:21
  105.9 12.0 %all-to-all-start.4 = ((bf16[8,64,256]{2,1,0:T(8,128)(2,1)}), bf16[8,64,256]{2,1,0:T(8,128)(2,1)S(1)}, u32[]{:S(2)}, u32[]{:S(2)}) async-start(bf16[8,64,256]{2,1,0:T(8,128)(2,1)} %shard_map.77), calls=%async_computation.4 | async-start | bytes 524288 | tf_op jit(solution)/shard_map/all_to_all | solution.py:21
  117.9 2.8 %collective-permute-start.11 = (bf16[4,144,256]{2,1,0:T(8,128)(2,1)S(1)}, bf16[4,144,256]{2,1,0:T(8,128)(2,1)S(1)}, u32[]{:S(2)}, u32[]{:S(2)}) collective-permute-start(bf16[4,144,256]{2,1,0:T(8,128)(2,1)S(1)} %get-tuple-element.20.refs_2_), channel_id=1, source_target_pairs={{32,0},{64,32},{96,64},{0,96},{33,1},{65,33},{97,65},{1,97},{34,2}... | collective-permute-start | bytes 884744 | tf_op jit(solution)/shard_map/ppermute | solution.py:25
  120.7 3.1 %collective-permute-start.12 = (bf16[4,144,256]{2,1,0:T(8,128)(2,1)S(1)}, bf16[4,144,256]{2,1,0:T(8,128)(2,1)S(1)}, u32[]{:S(2)}, u32[]{:S(2)}) collective-permute-start(bf16[4,144,256]{2,1,0:T(8,128)(2,1)S(1)} %get-tuple-element.20.refs_2_), channel_id=1, source_target_pairs={{64,0},{96,32},{0,64},{32,96},{65,1},{97,33},{1,65},{33,97},{66,2}... | collective-permute-start | bytes 884744 | tf_op jit(solution)/shard_map/ppermute | solution.py:25
  125.8 2.7 %collective-permute-done.11.refs_3_ = bf16[4,144,256]{2,1,0:T(8,128)(2,1)S(1)} collective-permute-done((bf16[4,144,256]{2,1,0:T(8,128)(2,1)S(1)}, bf16[4,144,256]{2,1,0:T(8,128)(2,1)S(1)}, u32[]{:S(2)}, u32[]{:S(2)}) %collective-permute-start.11) | collective-permute-done | bytes 294944 | tf_op jit(solution)/shard_map/ppermute | solution.py:25
  128.5 4.0 %collective-permute-done.12.refs_4_ = bf16[4,144,256]{2,1,0:T(8,128)(2,1)S(1)} collective-permute-done((bf16[4,144,256]{2,1,0:T(8,128)(2,1)S(1)}, bf16[4,144,256]{2,1,0:T(8,128)(2,1)S(1)}, u32[]{:S(2)}, u32[]{:S(2)}) %collective-permute-start.12) | collective-permute-done | bytes 294944 | tf_op jit(solution)/shard_map/ppermute | solution.py:25
  132.5 6.9 %collective-permute-done.13.refs_5_ = bf16[4,144,256]{2,1,0:T(8,128)(2,1)S(1)} collective-permute-done((bf16[4,144,256]{2,1,0:T(8,128)(2,1)S(1)}, bf16[4,144,256]{2,1,0:T(8,128)(2,1)S(1)}, u32[]{:S(2)}, u32[]{:S(2)}) %collective-permute-start.13) | collective-permute-done | bytes 294944 | tf_op jit(solution)/shard_map/ppermute | solution.py:25
  141.2 4.8 %all-to-all-start.5 = ((f32[8,64,144]{2,1,0:T(8,128)}), f32[8,64,144]{2,1,0:T(8,128)S(1)}, u32[]{:S(2)}, u32[]{:S(2)}) async-start(f32[8,64,144]{2,1,0:T(8,128)} %shard_map.78), calls=%async_computation.5 | async-start | bytes 1048576 | tf_op jit(solution)/shard_map/all_to_all | solution.py:21
  146.9 8.6 %all-to-all-done.5.refs_0_ = f32[8,64,144]{2,1,0:T(8,128)S(1)} async-done(((f32[8,64,144]{2,1,0:T(8,128)}), f32[8,64,144]{2,1,0:T(8,128)S(1)}, u32[]{:S(2)}, u32[]{:S(2)}) %all-to-all-start.5) | async-done | bytes 294944 | tf_op jit(solution)/shard_map/all_to_all | solution.py:21
  (47 shorter events, 16.9 us)
Async XLA Ops:
  0.8 1.1 copy-start
  4.6 10.5 %copy-start.2 = (bf16[256,128]{1,0:T(8,128)(2,1)S(1)}, bf16[256,128]{1,0:T(8,128)(2,1)}, u32[]{:S(2)}) copy-start(bf16[256,128]{1,0:T(8,128)(2,1)} %param.11) | copy-start | bytes 196612
  4.6 10.5 %copy-start.3 = (bf16[256,128]{1,0:T(8,128)(2,1)S(1)}, bf16[256,128]{1,0:T(8,128)(2,1)}, u32[]{:S(2)}) copy-start(bf16[256,128]{1,0:T(8,128)(2,1)} %param.12) | copy-start | bytes 196612
  4.6 31.4 %all-to-all-start = ((bf16[8,64,576]{2,1,0:T(8,128)(2,1)}), bf16[8,64,576]{2,1,0:T(8,128)(2,1)S(1)}, u32[]{:S(2)}, u32[]{:S(2)}) async-start(bf16[8,64,576]{2,1,0:T(8,128)(2,1)} %shard_map.73), calls=%async_computation | async-start | bytes 1310720 | tf_op jit(solution)/shard_map/all_to_all | solution.py:21
  15.0 2.1 %copy-start.1 = (bf16[144,512]{1,0:T(8,128)(2,1)S(1)}, bf16[144,512]{1,0:T(8,128)(2,1)}, u32[]{:S(2)}) copy-start(bf16[144,512]{1,0:T(8,128)(2,1)} %refs_1_.3) | copy-start | bytes 442372
  15.1 11.4 %copy-start.5 = (bf16[256,144]{0,1:T(8,128)(2,1)S(1)}, bf16[256,144]{0,1:T(8,128)(2,1)}, u32[]{:S(2)}) copy-start(bf16[256,144]{0,1:T(8,128)(2,1)} %param.10) | copy-start | bytes 221188
  15.1 12.1 %collective-permute-start.3 = (bf16[256,256]{1,0:T(8,128)(2,1)S(1)}, bf16[256,256]{1,0:T(8,128)(2,1)S(1)}, u32[]{:S(2)}, u32[]{:S(2)}) collective-permute-start(bf16[256,256]{1,0:T(8,128)(2,1)S(1)} %constant_dynamic-update-slice_fusion), channel_id=1, source_target_pairs={{128,0},{0,128},{384,256},{256,384},{129,1},{1,129},{385,257},{257... | collective-permute-start | bytes 393224 | tf_op jit(solution)/shard_map/ppermute | solution.py:29
  17.2 10.0 %collective-permute-start = (bf16[144,512]{1,0:T(8,128)(2,1)S(1)}, bf16[144,512]{1,0:T(8,128)(2,1)S(1)}, u32[]{:S(2)}, u32[]{:S(2)}) collective-permute-start(bf16[144,512]{1,0:T(8,128)(2,1)S(1)} %copy-done.1), channel_id=1, source_target_pairs={{128,0},{0,128},{384,256},{256,384},{129,1},{1,129},{385,257},{257... | collective-permute-start | bytes 442376 | tf_op jit(solution)/shard_map/ppermute | solution.py:29
  20.5 15.4 %collective-permute-start.1 = (bf16[144,512]{1,0:T(8,128)(2,1)S(1)}, bf16[144,512]{1,0:T(8,128)(2,1)S(1)}, u32[]{:S(2)}, u32[]{:S(2)}) collective-permute-start(bf16[144,512]{1,0:T(8,128)(2,1)S(1)} %copy-done.1), channel_id=1, source_target_pairs={{256,0},{384,128},{0,256},{128,384},{257,1},{385,129},{1,257},{129... | collective-permute-start | bytes 442376 | tf_op jit(solution)/shard_map/ppermute | solution.py:29
  22.5 13.5 %collective-permute-start.2 = (bf16[144,512]{1,0:T(8,128)(2,1)S(1)}, bf16[144,512]{1,0:T(8,128)(2,1)S(1)}, u32[]{:S(2)}, u32[]{:S(2)}) collective-permute-start(bf16[144,512]{1,0:T(8,128)(2,1)S(1)} %copy-done.1), channel_id=1, source_target_pairs={{384,0},{256,128},{128,256},{0,384},{385,1},{257,129},{129,257},{1... | collective-permute-start | bytes 442376 | tf_op jit(solution)/shard_map/ppermute | solution.py:29
  26.5 0.7 collective-permute-start.4
  37.5 20.6 %all-to-all-start.1 = ((f32[8,64,512]{2,1,0:T(8,128)}), f32[8,64,512]{2,1,0:T(8,128)S(1)}, u32[]{:S(2)}, u32[]{:S(2)}) async-start(f32[8,64,512]{2,1,0:T(8,128)} %get-tuple-element.13), calls=%async_computation.1 | async-start | bytes 2097152 | tf_op jit(solution)/shard_map/all_to_all | solution.py:21
  42.6 28.6 %collective-permute-start.6 = (bf16[2,256,256]{2,1,0:T(8,128)(2,1)S(1)}, bf16[2,256,256]{2,1,0:T(8,128)(2,1)S(1)}, u32[]{:S(2)}, u32[]{:S(2)}) collective-permute-start(bf16[2,256,256]{2,1,0:T(8,128)(2,1)S(1)} %get-tuple-element.16), channel_id=1, source_target_pairs={{256,0},{384,128},{0,256},{128,384},{257,1},{385,129},{1,257},{129... | collective-permute-start | bytes 786440 | tf_op jit(solution)/shard_map/ppermute | solution.py:29
  51.0 7.1 %collective-permute-start.5 = (bf16[144,256]{1,0:T(8,128)(2,1)S(1)}, bf16[144,256]{1,0:T(8,128)(2,1)S(1)}, u32[]{:S(2)}, u32[]{:S(2)}) collective-permute-start(bf16[144,256]{1,0:T(8,128)(2,1)S(1)} %get-tuple-element.14), channel_id=1, source_target_pairs={{128,0},{0,128},{384,256},{256,384},{129,1},{1,129},{385,257},{257... | collective-permute-start | bytes 221192 | tf_op jit(solution)/shard_map/ppermute | solution.py:29
  59.0 21.5 %collective-permute-start.10 = (bf16[2,144,256]{2,1,0:T(8,128)(2,1)S(1)}, bf16[2,144,256]{2,1,0:T(8,128)(2,1)S(1)}, u32[]{:S(2)}, u32[]{:S(2)}) collective-permute-start(bf16[2,144,256]{2,1,0:T(8,128)(2,1)S(1)} %get-tuple-element.18), channel_id=1, source_target_pairs={{256,0},{384,128},{0,256},{128,384},{257,1},{385,129},{1,257},{129... | collective-permute-start | bytes 442376 | tf_op jit(solution)/shard_map/ppermute | solution.py:29
  66.7 16.0 %all-to-all-start.2 = ((bf16[8,64,256]{2,1,0:T(8,128)(2,1)}), bf16[8,64,256]{2,1,0:T(8,128)(2,1)S(1)}, u32[]{:S(2)}, u32[]{:S(2)}) async-start(bf16[8,64,256]{2,1,0:T(8,128)(2,1)} %get-tuple-element.15), calls=%async_computation.2 | async-start | bytes 524288 | tf_op jit(solution)/shard_map/all_to_all | solution.py:21
  71.2 9.3 %collective-permute-start.7 = (bf16[64,256]{1,0:T(8,128)(2,1)S(1)}, bf16[64,256]{1,0:T(8,128)(2,1)S(1)}, u32[]{:S(2)}, u32[]{:S(2)}) collective-permute-start(bf16[64,256]{1,0:T(8,128)(2,1)S(1)} %get-tuple-element.17.refs_3_), channel_id=1, source_target_pairs={{128,0},{0,128},{384,256},{256,384},{129,1},{1,129},{385,257},{257... | collective-permute-start | bytes 98312 | tf_op jit(solution)/shard_map/ppermute | solution.py:29
  74.2 6.4 %collective-permute-start.8 = (bf16[64,256]{1,0:T(8,128)(2,1)S(1)}, bf16[64,256]{1,0:T(8,128)(2,1)S(1)}, u32[]{:S(2)}, u32[]{:S(2)}) collective-permute-start(bf16[64,256]{1,0:T(8,128)(2,1)S(1)} %get-tuple-element.17.refs_3_), channel_id=1, source_target_pairs={{256,0},{384,128},{0,256},{128,384},{257,1},{385,129},{1,257},{129... | collective-permute-start | bytes 98312 | tf_op jit(solution)/shard_map/ppermute | solution.py:29
  76.2 6.6 %collective-permute-start.9 = (bf16[64,256]{1,0:T(8,128)(2,1)S(1)}, bf16[64,256]{1,0:T(8,128)(2,1)S(1)}, u32[]{:S(2)}, u32[]{:S(2)}) collective-permute-start(bf16[64,256]{1,0:T(8,128)(2,1)S(1)} %get-tuple-element.17.refs_3_), channel_id=1, source_target_pairs={{384,0},{256,128},{128,256},{0,384},{385,1},{257,129},{129,257},{1... | collective-permute-start | bytes 98312 | tf_op jit(solution)/shard_map/ppermute | solution.py:29
  105.9 33.5 %all-to-all-start.4 = ((bf16[8,64,256]{2,1,0:T(8,128)(2,1)}), bf16[8,64,256]{2,1,0:T(8,128)(2,1)S(1)}, u32[]{:S(2)}, u32[]{:S(2)}) async-start(bf16[8,64,256]{2,1,0:T(8,128)(2,1)} %shard_map.77), calls=%async_computation.4 | async-start | bytes 524288 | tf_op jit(solution)/shard_map/all_to_all | solution.py:21
  117.9 10.5 %collective-permute-start.11 = (bf16[4,144,256]{2,1,0:T(8,128)(2,1)S(1)}, bf16[4,144,256]{2,1,0:T(8,128)(2,1)S(1)}, u32[]{:S(2)}, u32[]{:S(2)}) collective-permute-start(bf16[4,144,256]{2,1,0:T(8,128)(2,1)S(1)} %get-tuple-element.20.refs_2_), channel_id=1, source_target_pairs={{32,0},{64,32},{96,64},{0,96},{33,1},{65,33},{97,65},{1,97},{34,2}... | collective-permute-start | bytes 884744 | tf_op jit(solution)/shard_map/ppermute | solution.py:25
  120.7 11.8 %collective-permute-start.12 = (bf16[4,144,256]{2,1,0:T(8,128)(2,1)S(1)}, bf16[4,144,256]{2,1,0:T(8,128)(2,1)S(1)}, u32[]{:S(2)}, u32[]{:S(2)}) collective-permute-start(bf16[4,144,256]{2,1,0:T(8,128)(2,1)S(1)} %get-tuple-element.20.refs_2_), channel_id=1, source_target_pairs={{64,0},{96,32},{0,64},{32,96},{65,1},{97,33},{1,65},{33,97},{66,2}... | collective-permute-start | bytes 884744 | tf_op jit(solution)/shard_map/ppermute | solution.py:25
  123.8 15.5 %collective-permute-start.13 = (bf16[4,144,256]{2,1,0:T(8,128)(2,1)S(1)}, bf16[4,144,256]{2,1,0:T(8,128)(2,1)S(1)}, u32[]{:S(2)}, u32[]{:S(2)}) collective-permute-start(bf16[4,144,256]{2,1,0:T(8,128)(2,1)S(1)} %get-tuple-element.20.refs_2_), channel_id=1, source_target_pairs={{96,0},{0,32},{32,64},{64,96},{97,1},{1,33},{33,65},{65,97},{98,2}... | collective-permute-start | bytes 884744 | tf_op jit(solution)/shard_map/ppermute | solution.py:25
  141.2 14.3 %all-to-all-start.5 = ((f32[8,64,144]{2,1,0:T(8,128)}), f32[8,64,144]{2,1,0:T(8,128)S(1)}, u32[]{:S(2)}, u32[]{:S(2)}) async-start(f32[8,64,144]{2,1,0:T(8,128)} %shard_map.78), calls=%async_computation.5 | async-start | bytes 1048576 | tf_op jit(solution)/shard_map/all_to_all | solution.py:21
  (1 other events, 0.7 us)

commit v6 on v5

--- a/solution.py
+++ b/solution.py
@@ -17,20 +17,27 @@
 VMEM_BYTES = 40 * 1024 * 1024
 
 
+def swap_core(x):
+    return lax.ppermute(x, "c", [(0, 1), (1, 0)])
+
+
+PAIRS = (0, 2, 1, 3)
+
+
 def exchange(x, axis):
     return lax.all_to_all(x, axis, 0, 0, tiled=True)
 
 
+def copies(x, count):
+    return jnp.broadcast_to(x[None], (count,) + x.shape)
+
+
 def from_next(x, axis, step, size):
     return lax.ppermute(x, axis, [((i + step) % size, i) for i in range(size)])
 
 
 def from_pair(x, axis, bit, size):
     return lax.ppermute(x, axis, [(i ^ bit, i) for i in range(size)])
-
-
-def stack_z(x):
-    return jnp.stack([x] + [from_pair(x, "z", k, NZ) for k in range(1, NZ)])
 
 
 def block_result(query, keys, values, allowed):
@@ -65,6 +72,49 @@
     return highest, denom, accum
 
 
+def joint_results(query, keys, values, alloweds):
+    count, slots, _ = keys.shape
+    scores = lax.dot_general(
+        keys.reshape(count * slots, HEAD),
+        query,
+        (((1,), (1,)), ((), ())),
+        preferred_element_type=jnp.float32,
+    )
+    turned = jnp.concatenate([values[k].T for k in range(count)], axis=1)
+    owner = lax.broadcasted_iota(jnp.int32, turned.shape, 1) // slots
+    spread = jnp.concatenate(
+        [jnp.where(owner == k, turned, 0.0).astype(jnp.bfloat16) for k in range(count)], axis=0
+    )
+    stats, rounded = [], []
+    for k in range(count):
+        part = jnp.where(alloweds[k], scores[k * slots : (k + 1) * slots], masked_score)
+        best = jnp.max(part, axis=0, keepdims=True)
+        weights = jnp.exp(part - best)
+        total = jnp.where(best > 0.5 * masked_score, jnp.sum(weights, axis=0, keepdims=True), 0.0)
+        stats.append((best, total))
+        rounded.append(weights.astype(jnp.bfloat16))
+    numer = jnp.dot(spread, jnp.concatenate(rounded, axis=0), preferred_element_type=jnp.float32)
+    parts = []
+    for k, (best, total) in enumerate(stats):
+        inverse = 1.0 / jnp.where(total > 0.0, total, 1.0)
+        share = (numer[k * HEAD : (k + 1) * HEAD] * inverse).astype(jnp.bfloat16)
+        parts.append((best, total, share))
+    return parts
+
+
+def combine(parts):
+    highest = parts[0][0]
+    for best, _, _ in parts[1:]:
+        highest = jnp.maximum(highest, best)
+    denom = 0.0
+    accum = 0.0
+    for best, total, share in parts:
+        weight = total * jnp.exp(best - highest)
+        denom = denom + weight
+        accum = accum + weight * share.astype(jnp.float32)
+    return highest, denom, accum
+
+
 def norm_kernel(meta, tokens_ref, gain_ref, out_ref, normed_ref):
     hidden = tokens_ref[...].astype(jnp.float32)
     mean = jnp.mean(hidden * hidden, axis=-1, keepdims=True)
@@ -74,13 +124,14 @@
     for k in range(NZ):
         block = meta[1] ^ k
         part = normed_ref[:, pl.ds(pl.multiple_of(block * span, span), span)]
-        for i in range(NY * NC):
-            piece = part[:, i * k_rows : (i + 1) * k_rows]
-            out_ref[i, :, k * k_rows : (k + 1) * k_rows] = piece
+        for y in range(NY):
+            piece = part[:, y * NC * k_rows : (y + 1) * NC * k_rows]
+            for i in range(NC):
+                out_ref[y * NC + i, :, k * NC * k_rows : (k + 1) * NC * k_rows] = piece
 
 
 def project_kernel(rows_ref, w0, w1, w2, w3, out_ref):
-    weights = jnp.concatenate([w[...] for w in (w0, w1, w2, w3)], axis=0)
+    weights = jnp.concatenate([w[i] for w in (w0, w1, w2, w3) for i in range(NC)], axis=0)
     peers, rows, depth = rows_ref.shape
     total = jnp.dot(
         rows_ref[...].reshape(peers * rows, depth), weights, preferred_element_type=jnp.float32
@@ -89,9 +140,10 @@
 
 
 def rotary_kernel(part_ref, cos_ref, sin_ref, q_ref, new_ref):
-    total = part_ref[0]
-    for i in range(1, part_ref.shape[0]):
-        total = total + part_ref[i]
+    halves = []
+    for c in range(NC):
+        halves.append((part_ref[c] + part_ref[NC + c]) + (part_ref[2 * NC + c] + part_ref[3 * NC + c]))
+    total = jnp.concatenate(halves, axis=1)
     cosine, sine_part = cos_ref[...], sin_ref[...]
 
     def rotated(i):
@@ -112,23 +164,26 @@
     length, my_z, y, c = meta[0], meta[1], meta[2], meta[3]
     slots, new_slots = cache_ref.shape[1], n0.shape[0]
     rows = q_ref.shape[1]
-    lanes = 4 * rows
+    count = 4
+    lanes = count * 2 * rows
     slot = lax.broadcasted_iota(jnp.int32, (slots, lanes), 0)
     key = lax.broadcasted_iota(jnp.int32, (new_slots, lanes), 0)
     lane = lax.broadcasted_iota(jnp.int32, (new_slots, lanes), 1)
     row = lax.broadcasted_iota(jnp.int32, (8, 2 * rows), 0)
-    blocks = [((my_z ^ k) * NY + y) * NC + c for k in range(NZ)]
-    for pair in range(NY):
+    cached = [((my_z ^ k) * NY + y) * NC + c for k in PAIRS]
+    fresh = [((my_z ^ k) * NY + y) * NC + c for k in range(NZ)]
+    new = jnp.stack([n[...] for n in (n0, n1, n2, n3)])
+    for first in range(0, NY * NC, count):
         query = jnp.concatenate(
             [
-                q_ref[2 * pair + i, :, h * HEAD : (h + 1) * HEAD]
-                for i in range(NC)
+                q_ref[first + i, :, h * HEAD : (h + 1) * HEAD]
+                for i in range(count)
                 for h in range(2)
             ],
             axis=0,
         )
-        base = (my_z * NY + pair) * NC * rows
-        offset = base + jnp.where(lane < 2 * rows, 0, rows) + lane % rows - key
+        base = (my_z * NY * NC + first) * rows
+        offset = base + lane // (2 * rows) * rows + lane % rows - key
         parts = []
         for k in range(NZ):
             parts.append(
@@ -136,24 +191,24 @@
                     query,
                     cache_ref[k, :, :HEAD],
                     cache_ref[k, :, HEAD:],
-                    slot < length - blocks[k] * slots,
+                    slot < length - cached[k] * slots,
                 )
             )
-        for k, new in enumerate((n0, n1, n2, n3)):
-            parts.append(
-                block_result(
-                    query, new[:, :HEAD], new[:, HEAD:], offset >= blocks[k] * new_slots
-                )
-            )
+        parts += joint_results(
+            query,
+            new[:, :, :HEAD],
+            new[:, :, HEAD:],
+            [offset >= at * new_slots for at in fresh],
+        )
         highest, denom, accum = combine(parts)
-        for i in range(NC):
+        for i in range(count):
             part = slice(i * 2 * rows, (i + 1) * 2 * rows)
-            out_ref[2 * pair + i, :HEAD, :] = accum[:, part]
-            out_ref[2 * pair + i, HEAD:, :] = jnp.where(row == 0, highest[:, part], denom[:, part])
+            out_ref[first + i, :HEAD, :] = accum[:, part]
+            out_ref[first + i, HEAD:, :] = jnp.where(row == 0, highest[:, part], denom[:, part])
 
 
 def merge_kernel(state_ref, out_ref):
-    rows = out_ref.shape[1]
+    rows = out_ref.shape[0]
     bests = [state_ref[i, HEAD : HEAD + 1, :] for i in range(NY * NC)]
     highest = bests[0]
     for best in bests[1:]:
@@ -165,32 +220,44 @@
         denom = denom + state_ref[i, HEAD + 1 : HEAD + 2, :] * scale
         accum = accum + state_ref[i, :HEAD, :] * scale
     attention = jnp.transpose(accum / denom).astype(jnp.bfloat16)
-    for i in range(NW * NC):
-        out_ref[i, :, :HEAD] = attention[:rows]
-        out_ref[i, :, HEAD:] = attention[rows:]
-
-
-def output_kernel(meta, att_ref, b0, b1, b2, b3, out_ref):
+    out_ref[:, :HEAD] = attention[:rows]
+    out_ref[:, HEAD:] = attention[rows:]
+
+
+def output_kernel(meta, att_ref, other_ref, weight_ref, out_ref):
     rows = att_ref.shape[1]
-    att = [
-        att_ref[pl.ds((meta[1] ^ k) * NC, NC)].reshape(NC * rows, att_ref.shape[2])
-        for k in range(NW)
-    ]
-    for step, block in enumerate((b0, b1, b2, b3)):
-        place = lax.rem(meta[2] + step, NX)
+    z, c, w = meta[1], meta[3], meta[4]
+    places = [lax.rem((z ^ k) + NW - w, NW) for k in range(NZ)]
+    att = [jnp.concatenate([att_ref[at], other_ref[at]], axis=0) for at in places]
+    for x in range(NX):
+        place = x * NC
         total = 0.0
         for k in range(NW):
             total = total + lax.dot_general(
-                att[k], block[k], (((1,), (1,)), ((), ())), preferred_element_type=jnp.float32
+                att[k],
+                weight_ref[x, k],
+                (((1,), (1,)), ((), ())),
+                preferred_element_type=jnp.float32,
             )
-        for i in range(NC):
-            out_ref[place * NC + i] = total[i * rows : (i + 1) * rows]
+        rest = total[:, HEAD:]
+        for i, core in enumerate((c, 1 - c)):
+            out_ref[place + core, :rows] = total[i * rows : (i + 1) * rows, :HEAD]
+            out_ref[place + core, rows:] = jnp.concatenate(
+                [rest[i * rows + g * 8 : i * rows + g * 8 + 8] for g in range(rows // 8)], axis=1
+            )
 
 
 def last_kernel(part_ref, residual_ref, out_ref):
-    half = part_ref.shape[2]
+    rows = out_ref.shape[0]
+    half = out_ref.shape[1] // NC
+    wide = half - HEAD
     for j in range(NC):
         total = (part_ref[j] + part_ref[NC + j]) + (part_ref[2 * NC + j] + part_ref[3 * NC + j])
+        rest = total[rows:]
+        rest = jnp.concatenate(
+            [rest[:, g * wide : (g + 1) * wide] for g in range(rows // 8)], axis=0
+        )
+        total = jnp.concatenate([total[:rows], rest], axis=1)
         at = slice(j * half, (j + 1) * half)
         out_ref[:, at] = (residual_ref[:, at].astype(jnp.float32) + total).astype(jnp.bfloat16)
 
@@ -231,33 +298,36 @@
     seq_index = (z * NY + y) * NC + c
     fsdp_index = lax.axis_index("w") * NX + lax.axis_index("x")
     length = cache_len[0]
-    meta = jnp.stack([length, z, y, c]).astype(jnp.int32)
-
+    meta = jnp.stack([length, z, y, c, lax.axis_index("w")]).astype(jnp.int32)
+
+    half = w_qkv.shape[1] // NC
+    low, high = w_qkv[:, :half], w_qkv[:, half:]
+    kept, given = jnp.where(c == 0, low, high), jnp.where(c == 0, high, low)
+    got = swap_core(given)
+    w_pair = jnp.where(c == 0, jnp.stack([kept, got]), jnp.stack([got, kept]))
     rows_out = call(
         norm_kernel,
-        [((NY * NC, tok_rows, NZ * k_rows), bf16)],
+        [((NY * NC, tok_rows, NZ * NC * k_rows), bf16)],
         (meta, tokens, pre_gain.reshape(1, -1)),
         scalars=1,
         flops=tokens.size * 6,
         scratch=[pltpu.VMEM(tokens.shape, bf16)],
     )
     rows_in = exchange(rows_out, ("y", "c"))
-    weights = [w_qkv] + [from_pair(w_qkv, "z", k, NZ) for k in range(1, NZ)]
+    weights = [w_pair] + [from_pair(w_pair, "z", k, NZ) for k in range(1, NZ)]
     trade = [(a * NW + b, b * NW + a) for a in range(NZ) for b in range(NW)]
     out_block = lax.ppermute(w_out.T, ("z", "w"), trade)
     cache = jnp.concatenate([cache_keys, cache_values], axis=1)
-    cache = jnp.stack([cache, from_pair(cache, "z", 1, NZ)])
-    partial, cache, out_block = call(
+    cache = jnp.stack([cache, from_pair(cache, "z", 2, NZ)])
+    partial, cache = call(
         project_kernel,
-        [((NY * NC, tok_rows, w_qkv.shape[1]), f32)],
+        [((NY * NC, tok_rows, half), f32)],
         (rows_in, *weights),
         flops=2 * 256 * 1152 * 512,
-        held=(cache, out_block),
+        held=(cache,),
     )
     partial = exchange(partial, ("y", "c"))
-    cache = jnp.concatenate([cache, from_pair(cache, "z", 2, NZ)])
-    out_pair = jnp.stack([out_block, from_pair(out_block, "z", 1, NZ)])
-
+    cache = jnp.concatenate([cache, from_pair(cache, "z", 1, NZ)])
     half_dim = HEAD // 2
     inverse_freq = 10000.0 ** (-jnp.arange(half_dim, dtype=f32) / half_dim)
     positions = length + seq_index * tok_rows + jnp.arange(tok_rows, dtype=jnp.int32)
@@ -265,33 +335,36 @@
     cosine, sine_part = jnp.cos(angles), jnp.sin(angles)
     cosine = jnp.concatenate([cosine, cosine], axis=1)
     sine_part = jnp.concatenate([-sine_part, sine_part], axis=1)
-    queries, new, out_pair = call(
+    queries, new, out_block = call(
         rotary_kernel,
         [((NY * NC, tok_rows, 2 * HEAD), bf16), ((tok_rows, 2 * HEAD), bf16)],
         (partial, cosine, sine_part),
-        held=(out_pair,),
+        held=(out_block,),
     )
     all_queries = exchange(queries, ("y", "c"))
     all_new = [new] + [from_pair(new, "z", k, NZ) for k in range(1, NZ)]
-    out_z = jnp.concatenate([out_pair, from_pair(out_pair, "z", 2, NZ)])
-
-    state, out_z = call(
+
+    state, out_block = call(
         attention_kernel,
         [((NY * NC, HEAD + 8, 2 * tok_rows), f32)],
         (meta, all_queries, cache, *all_new),
         scalars=1,
         flops=4 * 512 * 2560 * 128,
-        held=(out_z,),
+        held=(out_block,),
     )
     states = exchange(state, ("y", "c"))
-    out_weights = [out_z] + [from_next(out_z, "y", k, NY) for k in range(1, NY)]
-    attention = call(merge_kernel, [((NW * NC, tok_rows, 2 * HEAD), bf16)], (states,))
-    attention = exchange(attention, ("w", "c"))
+    out_z = jnp.stack([out_block] + [from_pair(out_block, "z", k, NZ) for k in range(1, NZ)])
+    attention, out_z = call(
+        merge_kernel, [((tok_rows, 2 * HEAD), bf16)], (states,), held=(out_z,)
+    )
+    out_weights = exchange(copies(out_z, NY), "y")
+    attention = jnp.stack([attention] + [from_next(attention, "w", k, NW) for k in range(1, NW)])
+    att_other = swap_core(attention)
     width = D // (NW * NX)
     terms = call(
         output_kernel,
-        [((NX * NC, tok_rows, width // NC), f32)],
-        (meta, attention, *out_weights),
+        [((NX * NC, tok_rows * width // NC // HEAD, HEAD), f32)],
+        (meta, attention, att_other, out_weights),
         scalars=1,
         flops=2 * 64 * 4096 * 288,
     )

time: 157 us -> 151 us (0.962)
  the two profiles are of different devices: /device:TPU:1 before, /device:TPU:24 now
where the time goes in v6:
time: 151 us; the launch traced here: 149 us
  starting transfers between devices  101 us (67%)
  waiting for transfers between devices  30.3 us (20%)
  Pallas kernels  12.3 us (8%)
  local copies, waits for them, and re-layouts  3.98 us (3%)
    ppermute x11, starting transfers between devices, from_pair(): return lax.ppermute(x, axis, [(i ^ bit, i) for i in range(size)])  41.2 us
    all_to_all x6, starting transfers between devices, exchange(): return lax.all_to_all(x, axis, 0, 0, tiled=True)  33.4 us
    ppermute x3, starting transfers between devices, from_next(): return lax.ppermute(x, axis, [((i + step) % size, i) for i in range(size)])  22 us
    ppermute x11, waiting for transfers between devices, from_pair(): return lax.ppermute(x, axis, [(i ^ bit, i) for i in range(size)])  14.6 us
    pallas_call x7, Pallas kernels, call(): pl.pallas_call(body, out_shape=shapes, in_specs=specs + [pl.BlockSpec(mem...  12.3 us
    all_to_all x6, waiting for transfers between devices, exchange(): return lax.all_to_all(x, axis, 0, 0, tiled=True)  8.55 us
    ppermute x3, waiting for transfers between devices, from_next(): return lax.ppermute(x, axis, [((i + step) % size, i) for i in range(size)])  5.82 us
    ppermute x2, starting transfers between devices, swap_core(): return lax.ppermute(x, 'c', [(0, 1), (1, 0)])  3.98 us
  transfers between devices with their start and end apart: 23, of which 11 were waited for; matrix products, arithmetic and copies ran while one was open for 1% of the time, Pallas kernels for 1%

profile of v6, /device:TPU:24, one launch (start us, length us, event | category | flops | bytes accessed | tf_op | source)
XLA Modules:
  0.0 149.2 jit_solution(8919211219565283775)
XLA Ops:
  2.6 2.1 %shard_map.73 = bf16[8,64,1152]{2,1,0:T(8,128)(2,1)} custom-call(s32[5]{0:T(128)S(1)} %stack.72.refs_0_, bf16[64,4608]{1,0:T(8,128)(2,1)S(1)} %copy-done, f32[1,4608]{1,0:T(1,128)S(1)} %reshape.15.refs_2_), custom_call_target="tpu_custom_call" | custom-call | flops 1769472 | bytes 608276 | tf_op jit(solution)/shard_map/pallas_call | solution.py:277
  4.7 9.2 %all-to-all-start = ((bf16[8,64,1152]{2,1,0:T(8,128)(2,1)}), bf16[8,64,1152]{2,1,0:T(8,128)(2,1)S(1)}, u32[]{:S(2)}, u32[]{:S(2)}) async-start(bf16[8,64,1152]{2,1,0:T(8,128)(2,1)} %shard_map.73), calls=%async_computation | async-start | bytes 2359296 | tf_op jit(solution)/shard_map/all_to_all | solution.py:28
  18.1 2.7 %collective-permute-start.1 = (bf16[2,144,256]{2,1,0:T(8,128)(2,1)S(1)}, bf16[2,144,256]{2,1,0:T(8,128)(2,1)S(1)}, u32[]{:S(2)}, u32[]{:S(2)}) collective-permute-start(bf16[2,144,256]{2,1,0:T(8,128)(2,1)S(1)} %maximum_select_fusion.refs_1_), channel_id=1, source_target_pairs={{128,0},{0,128},{384,256},{256,384},{129,1},{1,129},{385,257},{257... | collective-permute-start | bytes 442376 | tf_op jit(solution)/shard_map/ppermute | solution.py:40
  20.8 4.1 %collective-permute-start.2 = (bf16[2,144,256]{2,1,0:T(8,128)(2,1)S(1)}, bf16[2,144,256]{2,1,0:T(8,128)(2,1)S(1)}, u32[]{:S(2)}, u32[]{:S(2)}) collective-permute-start(bf16[2,144,256]{2,1,0:T(8,128)(2,1)S(1)} %maximum_select_fusion.refs_1_), channel_id=1, source_target_pairs={{256,0},{384,128},{0,256},{128,384},{257,1},{385,129},{1,257},{129... | collective-permute-start | bytes 442376 | tf_op jit(solution)/shard_map/ppermute | solution.py:40
  24.8 3.4 %collective-permute-start.3 = (bf16[2,144,256]{2,1,0:T(8,128)(2,1)S(1)}, bf16[2,144,256]{2,1,0:T(8,128)(2,1)S(1)}, u32[]{:S(2)}, u32[]{:S(2)}) collective-permute-start(bf16[2,144,256]{2,1,0:T(8,128)(2,1)S(1)} %maximum_select_fusion.refs_1_), channel_id=1, source_target_pairs={{384,0},{256,128},{128,256},{0,384},{385,1},{257,129},{129,257},{1... | collective-permute-start | bytes 442376 | tf_op jit(solution)/shard_map/ppermute | solution.py:40
  30.5 5.8 %collective-permute-done.2.refs_3_ = bf16[2,144,256]{2,1,0:T(8,128)(2,1)S(1)} collective-permute-done((bf16[2,144,256]{2,1,0:T(8,128)(2,1)S(1)}, bf16[2,144,256]{2,1,0:T(8,128)(2,1)S(1)}, u32[]{:S(2)}, u32[]{:S(2)}) %collective-permute-start.2) | collective-permute-done | bytes 147488 | tf_op jit(solution)/shard_map/ppermute | solution.py:40
  37.6 4.8 %all-to-all-start.1 = ((f32[8,64,256]{2,1,0:T(8,128)}), f32[8,64,256]{2,1,0:T(8,128)S(1)}, u32[]{:S(2)}, u32[]{:S(2)}) async-start(f32[8,64,256]{2,1,0:T(8,128)} %get-tuple-element.14), calls=%async_computation.1 | async-start | bytes 1048576 | tf_op jit(solution)/shard_map/all_to_all | solution.py:28
  42.5 6.4 %collective-permute-start.6 = (bf16[2,256,256]{2,1,0:T(8,128)(2,1)S(1)}, bf16[2,256,256]{2,1,0:T(8,128)(2,1)S(1)}, u32[]{:S(2)}, u32[]{:S(2)}) collective-permute-start(bf16[2,256,256]{2,1,0:T(8,128)(2,1)S(1)} %get-tuple-element.16), channel_id=1, source_target_pairs={{128,0},{0,128},{384,256},{256,384},{129,1},{1,129},{385,257},{257... | collective-permute-start | bytes 786440 | tf_op jit(solution)/shard_map/ppermute | solution.py:40
  51.5 5.4 %all-to-all-start.2 = ((bf16[8,64,256]{2,1,0:T(8,128)(2,1)}), bf16[8,64,256]{2,1,0:T(8,128)(2,1)S(1)}, u32[]{:S(2)}, u32[]{:S(2)}) async-start(bf16[8,64,256]{2,1,0:T(8,128)(2,1)} %get-tuple-element.15), calls=%async_computation.2 | async-start | bytes 524288 | tf_op jit(solution)/shard_map/all_to_all | solution.py:28
  57.0 6.3 %collective-permute-start.7 = (bf16[64,256]{1,0:T(8,128)(2,1)S(1)}, bf16[64,256]{1,0:T(8,128)(2,1)S(1)}, u32[]{:S(2)}, u32[]{:S(2)}) collective-permute-start(bf16[64,256]{1,0:T(8,128)(2,1)S(1)} %get-tuple-element.17.refs_3_), channel_id=1, source_target_pairs={{128,0},{0,128},{384,256},{256,384},{129,1},{1,129},{385,257},{257... | collective-permute-start | bytes 98312 | tf_op jit(solution)/shard_map/ppermute | solution.py:40
  63.3 3.1 %collective-permute-start.8 = (bf16[64,256]{1,0:T(8,128)(2,1)S(1)}, bf16[64,256]{1,0:T(8,128)(2,1)S(1)}, u32[]{:S(2)}, u32[]{:S(2)}) collective-permute-start(bf16[64,256]{1,0:T(8,128)(2,1)S(1)} %get-tuple-element.17.refs_3_), channel_id=1, source_target_pairs={{256,0},{384,128},{0,256},{128,384},{257,1},{385,129},{1,257},{129... | collective-permute-start | bytes 98312 | tf_op jit(solution)/shard_map/ppermute | solution.py:40
  66.4 3.3 %collective-permute-start.9 = (bf16[64,256]{1,0:T(8,128)(2,1)S(1)}, bf16[64,256]{1,0:T(8,128)(2,1)S(1)}, u32[]{:S(2)}, u32[]{:S(2)}) collective-permute-start(bf16[64,256]{1,0:T(8,128)(2,1)S(1)} %get-tuple-element.17.refs_3_), channel_id=1, source_target_pairs={{384,0},{256,128},{128,256},{0,384},{385,1},{257,129},{129,257},{1... | collective-permute-start | bytes 98312 | tf_op jit(solution)/shard_map/ppermute | solution.py:40
  70.0 4.0 %collective-permute-done.9.refs_6_ = bf16[64,256]{1,0:T(8,128)(2,1)S(1)} collective-permute-done((bf16[64,256]{1,0:T(8,128)(2,1)S(1)}, bf16[64,256]{1,0:T(8,128)(2,1)S(1)}, u32[]{:S(2)}, u32[]{:S(2)}) %collective-permute-start.9) | collective-permute-done | bytes 32800 | tf_op jit(solution)/shard_map/ppermute | solution.py:40
  74.0 5.3 %shard_map.76 = (f32[8,136,128]{2,1,0:T(8,128)}, bf16[144,256]{1,0:T(8,128)(2,1)S(1)}) custom-call(s32[5]{0:T(128)S(1)} %stack.72.refs_0_, bf16[8,64,256]{2,1,0:T(8,128)(2,1)S(1)} %all-to-all-done.2.refs_1_, bf16[4,256,256]{2,1,0:T(8,128)(2,1)S(1)} %pad_maximum_fusion.refs_2_, ...), custom_call_target="tpu_custom_call", output_to_operand_aliasing={{1}: (7, {})} | custom-call | flops 671088640 | bytes 917524 | tf_op jit(solution)/shard_map/pallas_call | solution.py:277
  79.3 4.8 %all-to-all-start.3 = ((f32[8,136,128]{2,1,0:T(8,128)}), f32[8,136,128]{2,1,0:T(8,128)S(1)}, u32[]{:S(2)}, u32[]{:S(2)}) async-start(f32[8,136,128]{2,1,0:T(8,128)} %get-tuple-element.19), calls=%async_computation.3 | async-start | bytes 1114112 | tf_op jit(solution)/shard_map/all_to_all | solution.py:28
  84.1 3.3 %collective-permute-start.12 = (bf16[144,256]{1,0:T(8,128)(2,1)S(1)}, bf16[144,256]{1,0:T(8,128)(2,1)S(1)}, u32[]{:S(2)}, u32[]{:S(2)}) collective-permute-start(bf16[144,256]{1,0:T(8,128)(2,1)S(1)} %get-tuple-element.20), channel_id=1, source_target_pairs={{384,0},{256,128},{128,256},{0,384},{385,1},{257,129},{129,257},{1... | collective-permute-start | bytes 221192 | tf_op jit(solution)/shard_map/ppermute | solution.py:40
  89.5 4.7 %collective-permute-start.10 = (bf16[144,256]{1,0:T(8,128)(2,1)S(1)}, bf16[144,256]{1,0:T(8,128)(2,1)S(1)}, u32[]{:S(2)}, u32[]{:S(2)}) collective-permute-start(bf16[144,256]{1,0:T(8,128)(2,1)S(1)} %get-tuple-element.20), channel_id=1, source_target_pairs={{128,0},{0,128},{384,256},{256,384},{129,1},{1,129},{385,257},{257... | collective-permute-start | bytes 221192 | tf_op jit(solution)/shard_map/ppermute | solution.py:40
  98.5 4.8 %all-to-all-start.4 = ((bf16[4,4,144,256]{3,2,1,0:T(8,128)(2,1)}), bf16[4,4,144,256]{3,2,1,0:T(8,128)(2,1)S(1)}, u32[]{:S(2)}, u32[]{:S(2)}) async-start(bf16[4,4,144,256]{3,2,1,0:T(8,128)(2,1)} %broadcast_in_dim.2), calls=%async_computation.4 | async-start | bytes 2359296 | tf_op jit(solution)/shard_map/all_to_all | solution.py:28
  103.3 7.9 %collective-permute-start.15 = (bf16[64,256]{1,0:T(8,128)(2,1)S(1)}, bf16[64,256]{1,0:T(8,128)(2,1)S(1)}, u32[]{:S(2)}, u32[]{:S(2)}) collective-permute-start(bf16[64,256]{1,0:T(8,128)(2,1)S(1)} %get-tuple-element.21), channel_id=1, source_target_pairs={{12,0},{0,4},{4,8},{8,12},{13,1},{1,5},{5,9},{9,13},{14,2},{2,6},{... | collective-permute-start | bytes 98312 | tf_op jit(solution)/shard_map/ppermute | solution.py:36
  111.2 10.2 %collective-permute-start.14 = (bf16[64,256]{1,0:T(8,128)(2,1)S(1)}, bf16[64,256]{1,0:T(8,128)(2,1)S(1)}, u32[]{:S(2)}, u32[]{:S(2)}) collective-permute-start(bf16[64,256]{1,0:T(8,128)(2,1)S(1)} %get-tuple-element.21), channel_id=1, source_target_pairs={{8,0},{12,4},{0,8},{4,12},{9,1},{13,5},{1,9},{5,13},{10,2},{14,6},... | collective-permute-start | bytes 98312 | tf_op jit(solution)/shard_map/ppermute | solution.py:36
  121.4 3.9 %collective-permute-start.13 = (bf16[64,256]{1,0:T(8,128)(2,1)S(1)}, bf16[64,256]{1,0:T(8,128)(2,1)S(1)}, u32[]{:S(2)}, u32[]{:S(2)}) collective-permute-start(bf16[64,256]{1,0:T(8,128)(2,1)S(1)} %get-tuple-element.21), channel_id=1, source_target_pairs={{4,0},{8,4},{12,8},{0,12},{5,1},{9,5},{13,9},{1,13},{6,2},{10,6},{... | collective-permute-start | bytes 98312 | tf_op jit(solution)/shard_map/ppermute | solution.py:36
  125.8 5.3 %collective-permute-done.13 = bf16[64,256]{1,0:T(8,128)(2,1)S(1)} collective-permute-done((bf16[64,256]{1,0:T(8,128)(2,1)S(1)}, bf16[64,256]{1,0:T(8,128)(2,1)S(1)}, u32[]{:S(2)}, u32[]{:S(2)}) %collective-permute-start.13) | collective-permute-done | bytes 32800 | tf_op jit(solution)/shard_map/ppermute | solution.py:36
  136.2 4.3 %all-to-all-start.5 = ((f32[8,72,128]{2,1,0:T(8,128)}), f32[8,72,128]{2,1,0:T(8,128)S(1)}, u32[]{:S(2)}, u32[]{:S(2)}) async-start(f32[8,72,128]{2,1,0:T(8,128)} %shard_map.78), calls=%async_computation.5 | async-start | bytes 589824 | tf_op jit(solution)/shard_map/all_to_all | solution.py:28
  141.5 7.0 %all-to-all-done.5.refs_0_ = f32[8,72,128]{2,1,0:T(8,128)S(1)} async-done(((f32[8,72,128]{2,1,0:T(8,128)}), f32[8,72,128]{2,1,0:T(8,128)S(1)}, u32[]{:S(2)}, u32[]{:S(2)}) %all-to-all-start.5) | async-done | bytes 294944 | tf_op jit(solution)/shard_map/all_to_all | solution.py:28
  (55 shorter events, 26.2 us)
Async XLA Ops:
  4.7 23.5 %copy-start.4 = (bf16[256,144]{0,1:T(8,128)(2,1)S(1)}, bf16[256,144]{0,1:T(8,128)(2,1)}, u32[]{:S(2)}) copy-start(bf16[256,144]{0,1:T(8,128)(2,1)} %param.10) | copy-start | bytes 221188
  4.7 31.6 %all-to-all-start = ((bf16[8,64,1152]{2,1,0:T(8,128)(2,1)}), bf16[8,64,1152]{2,1,0:T(8,128)(2,1)S(1)}, u32[]{:S(2)}, u32[]{:S(2)}) async-start(bf16[8,64,1152]{2,1,0:T(8,128)(2,1)} %shard_map.73), calls=%async_computation | async-start | bytes 2359296 | tf_op jit(solution)/shard_map/all_to_all | solution.py:28
  14.0 4.1 %collective-permute-start = (bf16[144,256]{1,0:T(8,128)(2,1)S(1)}, bf16[144,256]{1,0:T(8,128)(2,1)S(1)}, u32[]{:S(2)}, u32[]{:S(2)}) collective-permute-start(bf16[144,256]{1,0:T(8,128)(2,1)S(1)} %get-tuple-element.24), channel_id=1, source_target_pairs={{0,16},{16,0},{1,17},{17,1},{2,18},{18,2},{3,19},{19,3},{4,20},{20... | collective-permute-start | bytes 221192 | tf_op jit(solution)/shard_map/ppermute | solution.py:21
  16.1 12.8 %collective-permute-start.4 = (bf16[256,256]{1,0:T(8,128)(2,1)S(1)}, bf16[256,256]{1,0:T(8,128)(2,1)S(1)}, u32[]{:S(2)}, u32[]{:S(2)}) collective-permute-start(bf16[256,256]{1,0:T(8,128)(2,1)S(1)} %constant_dynamic-update-slice_fusion), channel_id=1, source_target_pairs={{256,0},{384,128},{0,256},{128,384},{257,1},{385,129},{1,257},{129... | collective-permute-start | bytes 393224 | tf_op jit(solution)/shard_map/ppermute | solution.py:40
  18.1 12.4 %collective-permute-start.1 = (bf16[2,144,256]{2,1,0:T(8,128)(2,1)S(1)}, bf16[2,144,256]{2,1,0:T(8,128)(2,1)S(1)}, u32[]{:S(2)}, u32[]{:S(2)}) collective-permute-start(bf16[2,144,256]{2,1,0:T(8,128)(2,1)S(1)} %maximum_select_fusion.refs_1_), channel_id=1, source_target_pairs={{128,0},{0,128},{384,256},{256,384},{129,1},{1,129},{385,257},{257... | collective-permute-start | bytes 442376 | tf_op jit(solution)/shard_map/ppermute | solution.py:40
  20.8 15.5 %collective-permute-start.2 = (bf16[2,144,256]{2,1,0:T(8,128)(2,1)S(1)}, bf16[2,144,256]{2,1,0:T(8,128)(2,1)S(1)}, u32[]{:S(2)}, u32[]{:S(2)}) collective-permute-start(bf16[2,144,256]{2,1,0:T(8,128)(2,1)S(1)} %maximum_select_fusion.refs_1_), channel_id=1, source_target_pairs={{256,0},{384,128},{0,256},{128,384},{257,1},{385,129},{1,257},{129... | collective-permute-start | bytes 442376 | tf_op jit(solution)/shard_map/ppermute | solution.py:40
  24.8 11.5 %collective-permute-start.3 = (bf16[2,144,256]{2,1,0:T(8,128)(2,1)S(1)}, bf16[2,144,256]{2,1,0:T(8,128)(2,1)S(1)}, u32[]{:S(2)}, u32[]{:S(2)}) collective-permute-start(bf16[2,144,256]{2,1,0:T(8,128)(2,1)S(1)} %maximum_select_fusion.refs_1_), channel_id=1, source_target_pairs={{384,0},{256,128},{128,256},{0,384},{385,1},{257,129},{129,257},{1... | collective-permute-start | bytes 442376 | tf_op jit(solution)/shard_map/ppermute | solution.py:40
  28.2 20.9 %collective-permute-start.5 = (bf16[144,256]{1,0:T(8,128)(2,1)S(1)}, bf16[144,256]{1,0:T(8,128)(2,1)S(1)}, u32[]{:S(2)}, u32[]{:S(2)}) collective-permute-start(bf16[144,256]{1,0:T(8,128)(2,1)S(1)} %bitcast.31), channel_id=1, source_target_pairs={{0,0},{4,128},{8,256},{12,384},{128,4},{132,132},{136,260},{140,38... | collective-permute-start | bytes 221192 | tf_op jit(solution)/shard_map/ppermute | solution.py:319
  37.6 13.1 %all-to-all-start.1 = ((f32[8,64,256]{2,1,0:T(8,128)}), f32[8,64,256]{2,1,0:T(8,128)S(1)}, u32[]{:S(2)}, u32[]{:S(2)}) async-start(f32[8,64,256]{2,1,0:T(8,128)} %get-tuple-element.14), calls=%async_computation.1 | async-start | bytes 1048576 | tf_op jit(solution)/shard_map/all_to_all | solution.py:28
  42.5 27.2 %collective-permute-start.6 = (bf16[2,256,256]{2,1,0:T(8,128)(2,1)S(1)}, bf16[2,256,256]{2,1,0:T(8,128)(2,1)S(1)}, u32[]{:S(2)}, u32[]{:S(2)}) collective-permute-start(bf16[2,256,256]{2,1,0:T(8,128)(2,1)S(1)} %get-tuple-element.16), channel_id=1, source_target_pairs={{128,0},{0,128},{384,256},{256,384},{129,1},{1,129},{385,257},{257... | collective-permute-start | bytes 786440 | tf_op jit(solution)/shard_map/ppermute | solution.py:40
  51.5 22.5 %all-to-all-start.2 = ((bf16[8,64,256]{2,1,0:T(8,128)(2,1)}), bf16[8,64,256]{2,1,0:T(8,128)(2,1)S(1)}, u32[]{:S(2)}, u32[]{:S(2)}) async-start(bf16[8,64,256]{2,1,0:T(8,128)(2,1)} %get-tuple-element.15), calls=%async_computation.2 | async-start | bytes 524288 | tf_op jit(solution)/shard_map/all_to_all | solution.py:28
  57.0 12.8 %collective-permute-start.7 = (bf16[64,256]{1,0:T(8,128)(2,1)S(1)}, bf16[64,256]{1,0:T(8,128)(2,1)S(1)}, u32[]{:S(2)}, u32[]{:S(2)}) collective-permute-start(bf16[64,256]{1,0:T(8,128)(2,1)S(1)} %get-tuple-element.17.refs_3_), channel_id=1, source_target_pairs={{128,0},{0,128},{384,256},{256,384},{129,1},{1,129},{385,257},{257... | collective-permute-start | bytes 98312 | tf_op jit(solution)/shard_map/ppermute | solution.py:40
  63.3 6.7 %collective-permute-start.8 = (bf16[64,256]{1,0:T(8,128)(2,1)S(1)}, bf16[64,256]{1,0:T(8,128)(2,1)S(1)}, u32[]{:S(2)}, u32[]{:S(2)}) collective-permute-start(bf16[64,256]{1,0:T(8,128)(2,1)S(1)} %get-tuple-element.17.refs_3_), channel_id=1, source_target_pairs={{256,0},{384,128},{0,256},{128,384},{257,1},{385,129},{1,257},{129... | collective-permute-start | bytes 98312 | tf_op jit(solution)/shard_map/ppermute | solution.py:40
  66.4 7.6 %collective-permute-start.9 = (bf16[64,256]{1,0:T(8,128)(2,1)S(1)}, bf16[64,256]{1,0:T(8,128)(2,1)S(1)}, u32[]{:S(2)}, u32[]{:S(2)}) collective-permute-start(bf16[64,256]{1,0:T(8,128)(2,1)S(1)} %get-tuple-element.17.refs_3_), channel_id=1, source_target_pairs={{384,0},{256,128},{128,256},{0,384},{385,1},{257,129},{129,257},{1... | collective-permute-start | bytes 98312 | tf_op jit(solution)/shard_map/ppermute | solution.py:40
  79.3 17.9 %all-to-all-start.3 = ((f32[8,136,128]{2,1,0:T(8,128)}), f32[8,136,128]{2,1,0:T(8,128)S(1)}, u32[]{:S(2)}, u32[]{:S(2)}) async-start(f32[8,136,128]{2,1,0:T(8,128)} %get-tuple-element.19), calls=%async_computation.3 | async-start | bytes 1114112 | tf_op jit(solution)/shard_map/all_to_all | solution.py:28
  84.1 10.1 %collective-permute-start.12 = (bf16[144,256]{1,0:T(8,128)(2,1)S(1)}, bf16[144,256]{1,0:T(8,128)(2,1)S(1)}, u32[]{:S(2)}, u32[]{:S(2)}) collective-permute-start(bf16[144,256]{1,0:T(8,128)(2,1)S(1)} %get-tuple-element.20), channel_id=1, source_target_pairs={{384,0},{256,128},{128,256},{0,384},{385,1},{257,129},{129,257},{1... | collective-permute-start | bytes 221192 | tf_op jit(solution)/shard_map/ppermute | solution.py:40
  87.4 8.3 %collective-permute-start.11 = (bf16[144,256]{1,0:T(8,128)(2,1)S(1)}, bf16[144,256]{1,0:T(8,128)(2,1)S(1)}, u32[]{:S(2)}, u32[]{:S(2)}) collective-permute-start(bf16[144,256]{1,0:T(8,128)(2,1)S(1)} %get-tuple-element.20), channel_id=1, source_target_pairs={{256,0},{384,128},{0,256},{128,384},{257,1},{385,129},{1,257},{129... | collective-permute-start | bytes 221192 | tf_op jit(solution)/shard_map/ppermute | solution.py:40
  89.5 7.7 %collective-permute-start.10 = (bf16[144,256]{1,0:T(8,128)(2,1)S(1)}, bf16[144,256]{1,0:T(8,128)(2,1)S(1)}, u32[]{:S(2)}, u32[]{:S(2)}) collective-permute-start(bf16[144,256]{1,0:T(8,128)(2,1)S(1)} %get-tuple-element.20), channel_id=1, source_target_pairs={{128,0},{0,128},{384,256},{256,384},{129,1},{1,129},{385,257},{257... | collective-permute-start | bytes 221192 | tf_op jit(solution)/shard_map/ppermute | solution.py:40
  98.5 35.9 %all-to-all-start.4 = ((bf16[4,4,144,256]{3,2,1,0:T(8,128)(2,1)}), bf16[4,4,144,256]{3,2,1,0:T(8,128)(2,1)S(1)}, u32[]{:S(2)}, u32[]{:S(2)}) async-start(bf16[4,4,144,256]{3,2,1,0:T(8,128)(2,1)} %broadcast_in_dim.2), calls=%async_computation.4 | async-start | bytes 2359296 | tf_op jit(solution)/shard_map/all_to_all | solution.py:28
  103.3 22.0 %collective-permute-start.15 = (bf16[64,256]{1,0:T(8,128)(2,1)S(1)}, bf16[64,256]{1,0:T(8,128)(2,1)S(1)}, u32[]{:S(2)}, u32[]{:S(2)}) collective-permute-start(bf16[64,256]{1,0:T(8,128)(2,1)S(1)} %get-tuple-element.21), channel_id=1, source_target_pairs={{12,0},{0,4},{4,8},{8,12},{13,1},{1,5},{5,9},{9,13},{14,2},{2,6},{... | collective-permute-start | bytes 98312 | tf_op jit(solution)/shard_map/ppermute | solution.py:36
  111.2 14.6 %collective-permute-start.14 = (bf16[64,256]{1,0:T(8,128)(2,1)S(1)}, bf16[64,256]{1,0:T(8,128)(2,1)S(1)}, u32[]{:S(2)}, u32[]{:S(2)}) collective-permute-start(bf16[64,256]{1,0:T(8,128)(2,1)S(1)} %get-tuple-element.21), channel_id=1, source_target_pairs={{8,0},{12,4},{0,8},{4,12},{9,1},{13,5},{1,9},{5,13},{10,2},{14,6},... | collective-permute-start | bytes 98312 | tf_op jit(solution)/shard_map/ppermute | solution.py:36
  121.4 9.7 %collective-permute-start.13 = (bf16[64,256]{1,0:T(8,128)(2,1)S(1)}, bf16[64,256]{1,0:T(8,128)(2,1)S(1)}, u32[]{:S(2)}, u32[]{:S(2)}) collective-permute-start(bf16[64,256]{1,0:T(8,128)(2,1)S(1)} %get-tuple-element.21), channel_id=1, source_target_pairs={{4,0},{8,4},{12,8},{0,12},{5,1},{9,5},{13,9},{1,13},{6,2},{10,6},{... | collective-permute-start | bytes 98312 | tf_op jit(solution)/shard_map/ppermute | solution.py:36
  131.1 3.2 %collective-permute-start.16 = (bf16[4,64,256]{2,1,0:T(8,128)(2,1)S(1)}, bf16[4,64,256]{2,1,0:T(8,128)(2,1)S(1)}, u32[]{:S(2)}, u32[]{:S(2)}) collective-permute-start(bf16[4,64,256]{2,1,0:T(8,128)(2,1)S(1)} %pad_maximum_fusion.3.refs_1_), channel_id=1, source_target_pairs={{0,16},{16,0},{1,17},{17,1},{2,18},{18,2},{3,19},{19,3},{4,20},{20... | collective-permute-start | bytes 393224 | tf_op jit(solution)/shard_map/ppermute | solution.py:21
  136.2 12.2 %all-to-all-start.5 = ((f32[8,72,128]{2,1,0:T(8,128)}), f32[8,72,128]{2,1,0:T(8,128)S(1)}, u32[]{:S(2)}, u32[]{:S(2)}) async-start(f32[8,72,128]{2,1,0:T(8,128)} %shard_map.78), calls=%async_computation.5 | async-start | bytes 589824 | tf_op jit(solution)/shard_map/all_to_all | solution.py:28
  (4 other events, 33.0 us)

commit v7 on v6

--- a/solution.py
+++ b/solution.py
@@ -160,9 +160,9 @@
     new_ref[:, HEAD:] = total[:, 3 * HEAD :].astype(jnp.bfloat16)
 
 
-def attention_kernel(meta, q_ref, cache_ref, n0, n1, n2, n3, out_ref):
+def attention_kernel(meta, q_ref, cache_ref, new, out_ref):
     length, my_z, y, c = meta[0], meta[1], meta[2], meta[3]
-    slots, new_slots = cache_ref.shape[1], n0.shape[0]
+    slots, new_slots = cache_ref.shape[1], new.shape[1]
     rows = q_ref.shape[1]
     count = 4
     lanes = count * 2 * rows
@@ -171,8 +171,7 @@
     lane = lax.broadcasted_iota(jnp.int32, (new_slots, lanes), 1)
     row = lax.broadcasted_iota(jnp.int32, (8, 2 * rows), 0)
     cached = [((my_z ^ k) * NY + y) * NC + c for k in PAIRS]
-    fresh = [((my_z ^ k) * NY + y) * NC + c for k in range(NZ)]
-    new = jnp.stack([n[...] for n in (n0, n1, n2, n3)])
+    fresh = [((my_z ^ k) * NY + y) * NC + c for k in PAIRS]
     for first in range(0, NY * NC, count):
         query = jnp.concatenate(
             [
@@ -342,12 +341,13 @@
         held=(out_block,),
     )
     all_queries = exchange(queries, ("y", "c"))
-    all_new = [new] + [from_pair(new, "z", k, NZ) for k in range(1, NZ)]
+    all_new = jnp.stack([new, from_pair(new, "z", 2, NZ)])
+    all_new = jnp.concatenate([all_new, from_pair(all_new, "z", 1, NZ)])
 
     state, out_block = call(
         attention_kernel,
         [((NY * NC, HEAD + 8, 2 * tok_rows), f32)],
-        (meta, all_queries, cache, *all_new),
+        (meta, all_queries, cache, all_new),
         scalars=1,
         flops=4 * 512 * 2560 * 128,
         held=(out_block,),

time: 151 us -> 147 us (0.974)
  starting transfers between devices: 101 us -> 98 us
    ppermute x11 -> x10, starting transfers between devices: 41.2 us -> 37.9 us  [from_pair(): return lax.ppermute(x, axis, [(i ^ bit, i) for i in range(size)])]
    ppermute x11 -> x10, waiting for transfers between devices: 14.6 us -> 14.4 us  [from_pair(): return lax.ppermute(x, axis, [(i ^ bit, i) for i in range(size)])]
  transfers between devices with their start and end apart: 23 -> 22, of which waited for: 11 -> 10; matrix products, arithmetic and copies ran while one was open for 1% -> 1% of each run, Pallas kernels for 1% -> 1%
where the time goes in v7:
time: 147 us; the launch traced here: 146 us
  starting transfers between devices  98 us (67%)
  waiting for transfers between devices  29.8 us (20%)
  Pallas kernels  12.3 us (8%)
  local copies, waits for them, and re-layouts  3.98 us (3%)
    ppermute x10, starting transfers between devices, from_pair(): return lax.ppermute(x, axis, [(i ^ bit, i) for i in range(size)])  37.9 us
    all_to_all x6, starting transfers between devices, exchange(): return lax.all_to_all(x, axis, 0, 0, tiled=True)  33.4 us
    ppermute x3, starting transfers between devices, from_next(): return lax.ppermute(x, axis, [((i + step) % size, i) for i in range(size)])  22.1 us
    ppermute x10, waiting for transfers between devices, from_pair(): return lax.ppermute(x, axis, [(i ^ bit, i) for i in range(size)])  14.4 us
    pallas_call x7, Pallas kernels, call(): pl.pallas_call(body, out_shape=shapes, in_specs=specs + [pl.BlockSpec(mem...  12.3 us
    all_to_all x6, waiting for transfers between devices, exchange(): return lax.all_to_all(x, axis, 0, 0, tiled=True)  8.55 us
    ppermute x3, waiting for transfers between devices, from_next(): return lax.ppermute(x, axis, [((i + step) % size, i) for i in range(size)])  5.53 us
    ppermute x2, starting transfers between devices, swap_core(): return lax.ppermute(x, 'c', [(0, 1), (1, 0)])  3.98 us
  transfers between devices with their start and end apart: 22, of which 10 were waited for; matrix products, arithmetic and copies ran while one was open for 1% of the time, Pallas kernels for 1%

profile of v7, /device:TPU:24, one launch (start us, length us, event | category | flops | bytes accessed | tf_op | source)
XLA Modules:
  0.0 145.6 jit_solution(18413452112243032377)
XLA Ops:
  2.6 2.1 %shard_map.73 = bf16[8,64,1152]{2,1,0:T(8,128)(2,1)} custom-call(s32[5]{0:T(128)S(1)} %stack.81.refs_0_, bf16[64,4608]{1,0:T(8,128)(2,1)S(1)} %copy-done, f32[1,4608]{1,0:T(1,128)S(1)} %reshape.15.refs_2_), custom_call_target="tpu_custom_call" | custom-call | flops 1769472 | bytes 608276 | tf_op jit(solution)/shard_map/pallas_call | solution.py:276
  4.7 9.2 %all-to-all-start = ((bf16[8,64,1152]{2,1,0:T(8,128)(2,1)}), bf16[8,64,1152]{2,1,0:T(8,128)(2,1)S(1)}, u32[]{:S(2)}, u32[]{:S(2)}) async-start(bf16[8,64,1152]{2,1,0:T(8,128)(2,1)} %shard_map.73), calls=%async_computation | async-start | bytes 2359296 | tf_op jit(solution)/shard_map/all_to_all | solution.py:28
  14.0 2.1 %collective-permute-start = (bf16[144,256]{1,0:T(8,128)(2,1)S(1)}, bf16[144,256]{1,0:T(8,128)(2,1)S(1)}, u32[]{:S(2)}, u32[]{:S(2)}) collective-permute-start(bf16[144,256]{1,0:T(8,128)(2,1)S(1)} %get-tuple-element.24), channel_id=1, source_target_pairs={{0,16},{16,0},{1,17},{17,1},{2,18},{18,2},{3,19},{19,3},{4,20},{20... | collective-permute-start | bytes 221192 | tf_op jit(solution)/shard_map/ppermute | solution.py:21
  18.1 2.7 %collective-permute-start.1 = (bf16[2,144,256]{2,1,0:T(8,128)(2,1)S(1)}, bf16[2,144,256]{2,1,0:T(8,128)(2,1)S(1)}, u32[]{:S(2)}, u32[]{:S(2)}) collective-permute-start(bf16[2,144,256]{2,1,0:T(8,128)(2,1)S(1)} %maximum_select_fusion.refs_1_), channel_id=1, source_target_pairs={{128,0},{0,128},{384,256},{256,384},{129,1},{1,129},{385,257},{257... | collective-permute-start | bytes 442376 | tf_op jit(solution)/shard_map/ppermute | solution.py:40
  20.8 4.1 %collective-permute-start.2 = (bf16[2,144,256]{2,1,0:T(8,128)(2,1)S(1)}, bf16[2,144,256]{2,1,0:T(8,128)(2,1)S(1)}, u32[]{:S(2)}, u32[]{:S(2)}) collective-permute-start(bf16[2,144,256]{2,1,0:T(8,128)(2,1)S(1)} %maximum_select_fusion.refs_1_), channel_id=1, source_target_pairs={{256,0},{384,128},{0,256},{128,384},{257,1},{385,129},{1,257},{129... | collective-permute-start | bytes 442376 | tf_op jit(solution)/shard_map/ppermute | solution.py:40
  24.8 3.4 %collective-permute-start.3 = (bf16[2,144,256]{2,1,0:T(8,128)(2,1)S(1)}, bf16[2,144,256]{2,1,0:T(8,128)(2,1)S(1)}, u32[]{:S(2)}, u32[]{:S(2)}) collective-permute-start(bf16[2,144,256]{2,1,0:T(8,128)(2,1)S(1)} %maximum_select_fusion.refs_1_), channel_id=1, source_target_pairs={{384,0},{256,128},{128,256},{0,384},{385,1},{257,129},{129,257},{1... | collective-permute-start | bytes 442376 | tf_op jit(solution)/shard_map/ppermute | solution.py:40
  30.5 5.8 %collective-permute-done.2.refs_3_ = bf16[2,144,256]{2,1,0:T(8,128)(2,1)S(1)} collective-permute-done((bf16[2,144,256]{2,1,0:T(8,128)(2,1)S(1)}, bf16[2,144,256]{2,1,0:T(8,128)(2,1)S(1)}, u32[]{:S(2)}, u32[]{:S(2)}) %collective-permute-start.2) | collective-permute-done | bytes 147488 | tf_op jit(solution)/shard_map/ppermute | solution.py:40
  37.6 4.8 %all-to-all-start.1 = ((f32[8,64,256]{2,1,0:T(8,128)}), f32[8,64,256]{2,1,0:T(8,128)S(1)}, u32[]{:S(2)}, u32[]{:S(2)}) async-start(f32[8,64,256]{2,1,0:T(8,128)} %get-tuple-element.14), calls=%async_computation.1 | async-start | bytes 1048576 | tf_op jit(solution)/shard_map/all_to_all | solution.py:28
  42.5 6.4 %collective-permute-start.6 = (bf16[2,256,256]{2,1,0:T(8,128)(2,1)S(1)}, bf16[2,256,256]{2,1,0:T(8,128)(2,1)S(1)}, u32[]{:S(2)}, u32[]{:S(2)}) collective-permute-start(bf16[2,256,256]{2,1,0:T(8,128)(2,1)S(1)} %get-tuple-element.16), channel_id=1, source_target_pairs={{128,0},{0,128},{384,256},{256,384},{129,1},{1,129},{385,257},{257... | collective-permute-start | bytes 786440 | tf_op jit(solution)/shard_map/ppermute | solution.py:40
  51.5 7.4 %collective-permute-start.7 = (bf16[64,256]{1,0:T(8,128)(2,1)S(1)}, bf16[64,256]{1,0:T(8,128)(2,1)S(1)}, u32[]{:S(2)}, u32[]{:S(2)}) collective-permute-start(bf16[64,256]{1,0:T(8,128)(2,1)S(1)} %get-tuple-element.17), channel_id=1, source_target_pairs={{256,0},{384,128},{0,256},{128,384},{257,1},{385,129},{1,257},{129... | collective-permute-start | bytes 98312 | tf_op jit(solution)/shard_map/ppermute | solution.py:40
  58.9 5.4 %all-to-all-start.2 = ((bf16[8,64,256]{2,1,0:T(8,128)(2,1)}), bf16[8,64,256]{2,1,0:T(8,128)(2,1)S(1)}, u32[]{:S(2)}, u32[]{:S(2)}) async-start(bf16[8,64,256]{2,1,0:T(8,128)(2,1)} %get-tuple-element.15), calls=%async_computation.2 | async-start | bytes 524288 | tf_op jit(solution)/shard_map/all_to_all | solution.py:28
  66.5 4.0 %collective-permute-done.8 = bf16[2,64,256]{2,1,0:T(8,128)(2,1)S(1)} collective-permute-done((bf16[2,64,256]{2,1,0:T(8,128)(2,1)S(1)}, bf16[2,64,256]{2,1,0:T(8,128)(2,1)S(1)}, u32[]{:S(2)}, u32[]{:S(2)}) %collective-permute-start.8) | collective-permute-done | bytes 65568 | tf_op jit(solution)/shard_map/ppermute | solution.py:40
  70.5 5.3 %shard_map.76 = (f32[8,136,128]{2,1,0:T(8,128)}, bf16[144,256]{1,0:T(8,128)(2,1)S(1)}) custom-call(s32[5]{0:T(128)S(1)} %stack.81.refs_0_, bf16[8,64,256]{2,1,0:T(8,128)(2,1)S(1)} %all-to-all-done.2.refs_1_, bf16[4,256,256]{2,1,0:T(8,128)(2,1)S(1)} %pad_maximum_fusion.refs_2_, ...), custom_call_target="tpu_custom_call", output_to_operand_aliasing={{1}: (4, {})} | custom-call | flops 671088640 | bytes 917524 | tf_op jit(solution)/shard_map/pallas_call | solution.py:276
  75.9 4.8 %all-to-all-start.3 = ((f32[8,136,128]{2,1,0:T(8,128)}), f32[8,136,128]{2,1,0:T(8,128)S(1)}, u32[]{:S(2)}, u32[]{:S(2)}) async-start(f32[8,136,128]{2,1,0:T(8,128)} %get-tuple-element.19), calls=%async_computation.3 | async-start | bytes 1114112 | tf_op jit(solution)/shard_map/all_to_all | solution.py:28
  80.7 3.2 %collective-permute-start.11 = (bf16[144,256]{1,0:T(8,128)(2,1)S(1)}, bf16[144,256]{1,0:T(8,128)(2,1)S(1)}, u32[]{:S(2)}, u32[]{:S(2)}) collective-permute-start(bf16[144,256]{1,0:T(8,128)(2,1)S(1)} %get-tuple-element.20), channel_id=1, source_target_pairs={{384,0},{256,128},{128,256},{0,384},{385,1},{257,129},{129,257},{1... | collective-permute-start | bytes 221192 | tf_op jit(solution)/shard_map/ppermute | solution.py:40
  83.9 2.2 %collective-permute-start.10 = (bf16[144,256]{1,0:T(8,128)(2,1)S(1)}, bf16[144,256]{1,0:T(8,128)(2,1)S(1)}, u32[]{:S(2)}, u32[]{:S(2)}) collective-permute-start(bf16[144,256]{1,0:T(8,128)(2,1)S(1)} %get-tuple-element.20), channel_id=1, source_target_pairs={{256,0},{384,128},{0,256},{128,384},{257,1},{385,129},{1,257},{129... | collective-permute-start | bytes 221192 | tf_op jit(solution)/shard_map/ppermute | solution.py:40
  86.1 4.7 %collective-permute-start.9 = (bf16[144,256]{1,0:T(8,128)(2,1)S(1)}, bf16[144,256]{1,0:T(8,128)(2,1)S(1)}, u32[]{:S(2)}, u32[]{:S(2)}) collective-permute-start(bf16[144,256]{1,0:T(8,128)(2,1)S(1)} %get-tuple-element.20), channel_id=1, source_target_pairs={{128,0},{0,128},{384,256},{256,384},{129,1},{1,129},{385,257},{257... | collective-permute-start | bytes 221192 | tf_op jit(solution)/shard_map/ppermute | solution.py:40
  95.1 4.8 %all-to-all-start.4 = ((bf16[4,4,144,256]{3,2,1,0:T(8,128)(2,1)}), bf16[4,4,144,256]{3,2,1,0:T(8,128)(2,1)S(1)}, u32[]{:S(2)}, u32[]{:S(2)}) async-start(bf16[4,4,144,256]{3,2,1,0:T(8,128)(2,1)} %broadcast_in_dim.2), calls=%async_computation.4 | async-start | bytes 2359296 | tf_op jit(solution)/shard_map/all_to_all | solution.py:28
  99.9 7.9 %collective-permute-start.14 = (bf16[64,256]{1,0:T(8,128)(2,1)S(1)}, bf16[64,256]{1,0:T(8,128)(2,1)S(1)}, u32[]{:S(2)}, u32[]{:S(2)}) collective-permute-start(bf16[64,256]{1,0:T(8,128)(2,1)S(1)} %get-tuple-element.21), channel_id=1, source_target_pairs={{12,0},{0,4},{4,8},{8,12},{13,1},{1,5},{5,9},{9,13},{14,2},{2,6},{... | collective-permute-start | bytes 98312 | tf_op jit(solution)/shard_map/ppermute | solution.py:36
  107.8 10.0 %collective-permute-start.13 = (bf16[64,256]{1,0:T(8,128)(2,1)S(1)}, bf16[64,256]{1,0:T(8,128)(2,1)S(1)}, u32[]{:S(2)}, u32[]{:S(2)}) collective-permute-start(bf16[64,256]{1,0:T(8,128)(2,1)S(1)} %get-tuple-element.21), channel_id=1, source_target_pairs={{8,0},{12,4},{0,8},{4,12},{9,1},{13,5},{1,9},{5,13},{10,2},{14,6},... | collective-permute-start | bytes 98312 | tf_op jit(solution)/shard_map/ppermute | solution.py:36
  117.8 4.2 %collective-permute-start.12 = (bf16[64,256]{1,0:T(8,128)(2,1)S(1)}, bf16[64,256]{1,0:T(8,128)(2,1)S(1)}, u32[]{:S(2)}, u32[]{:S(2)}) collective-permute-start(bf16[64,256]{1,0:T(8,128)(2,1)S(1)} %get-tuple-element.21), channel_id=1, source_target_pairs={{4,0},{8,4},{12,8},{0,12},{5,1},{9,5},{13,9},{1,13},{6,2},{10,6},{... | collective-permute-start | bytes 98312 | tf_op jit(solution)/shard_map/ppermute | solution.py:36
  122.5 5.1 %collective-permute-done.12 = bf16[64,256]{1,0:T(8,128)(2,1)S(1)} collective-permute-done((bf16[64,256]{1,0:T(8,128)(2,1)S(1)}, bf16[64,256]{1,0:T(8,128)(2,1)S(1)}, u32[]{:S(2)}, u32[]{:S(2)}) %collective-permute-start.12) | collective-permute-done | bytes 32800 | tf_op jit(solution)/shard_map/ppermute | solution.py:36
  132.6 4.3 %all-to-all-start.5 = ((f32[8,72,128]{2,1,0:T(8,128)}), f32[8,72,128]{2,1,0:T(8,128)S(1)}, u32[]{:S(2)}, u32[]{:S(2)}) async-start(f32[8,72,128]{2,1,0:T(8,128)} %shard_map.78), calls=%async_computation.5 | async-start | bytes 589824 | tf_op jit(solution)/shard_map/all_to_all | solution.py:28
  137.8 7.0 %all-to-all-done.5.refs_0_ = f32[8,72,128]{2,1,0:T(8,128)S(1)} async-done(((f32[8,72,128]{2,1,0:T(8,128)}), f32[8,72,128]{2,1,0:T(8,128)S(1)}, u32[]{:S(2)}, u32[]{:S(2)}) %all-to-all-start.5) | async-done | bytes 294944 | tf_op jit(solution)/shard_map/all_to_all | solution.py:28
  (55 shorter events, 23.7 us)
Async XLA Ops:
  4.7 11.4 %copy-start.3 = (bf16[256,128]{1,0:T(8,128)(2,1)S(1)}, bf16[256,128]{1,0:T(8,128)(2,1)}, u32[]{:S(2)}) copy-start(bf16[256,128]{1,0:T(8,128)(2,1)} %param.12) | copy-start | bytes 196612
  4.7 23.5 %copy-start.4 = (bf16[256,144]{0,1:T(8,128)(2,1)S(1)}, bf16[256,144]{0,1:T(8,128)(2,1)}, u32[]{:S(2)}) copy-start(bf16[256,144]{0,1:T(8,128)(2,1)} %param.10) | copy-start | bytes 221188
  4.7 31.6 %all-to-all-start = ((bf16[8,64,1152]{2,1,0:T(8,128)(2,1)}), bf16[8,64,1152]{2,1,0:T(8,128)(2,1)S(1)}, u32[]{:S(2)}, u32[]{:S(2)}) async-start(bf16[8,64,1152]{2,1,0:T(8,128)(2,1)} %shard_map.73), calls=%async_computation | async-start | bytes 2359296 | tf_op jit(solution)/shard_map/all_to_all | solution.py:28
  14.0 4.1 %collective-permute-start = (bf16[144,256]{1,0:T(8,128)(2,1)S(1)}, bf16[144,256]{1,0:T(8,128)(2,1)S(1)}, u32[]{:S(2)}, u32[]{:S(2)}) collective-permute-start(bf16[144,256]{1,0:T(8,128)(2,1)S(1)} %get-tuple-element.24), channel_id=1, source_target_pairs={{0,16},{16,0},{1,17},{17,1},{2,18},{18,2},{3,19},{19,3},{4,20},{20... | collective-permute-start | bytes 221192 | tf_op jit(solution)/shard_map/ppermute | solution.py:21
  16.1 12.8 %collective-permute-start.4 = (bf16[256,256]{1,0:T(8,128)(2,1)S(1)}, bf16[256,256]{1,0:T(8,128)(2,1)S(1)}, u32[]{:S(2)}, u32[]{:S(2)}) collective-permute-start(bf16[256,256]{1,0:T(8,128)(2,1)S(1)} %constant_dynamic-update-slice_fusion), channel_id=1, source_target_pairs={{256,0},{384,128},{0,256},{128,384},{257,1},{385,129},{1,257},{129... | collective-permute-start | bytes 393224 | tf_op jit(solution)/shard_map/ppermute | solution.py:40
  18.1 12.4 %collective-permute-start.1 = (bf16[2,144,256]{2,1,0:T(8,128)(2,1)S(1)}, bf16[2,144,256]{2,1,0:T(8,128)(2,1)S(1)}, u32[]{:S(2)}, u32[]{:S(2)}) collective-permute-start(bf16[2,144,256]{2,1,0:T(8,128)(2,1)S(1)} %maximum_select_fusion.refs_1_), channel_id=1, source_target_pairs={{128,0},{0,128},{384,256},{256,384},{129,1},{1,129},{385,257},{257... | collective-permute-start | bytes 442376 | tf_op jit(solution)/shard_map/ppermute | solution.py:40
  20.8 15.5 %collective-permute-start.2 = (bf16[2,144,256]{2,1,0:T(8,128)(2,1)S(1)}, bf16[2,144,256]{2,1,0:T(8,128)(2,1)S(1)}, u32[]{:S(2)}, u32[]{:S(2)}) collective-permute-start(bf16[2,144,256]{2,1,0:T(8,128)(2,1)S(1)} %maximum_select_fusion.refs_1_), channel_id=1, source_target_pairs={{256,0},{384,128},{0,256},{128,384},{257,1},{385,129},{1,257},{129... | collective-permute-start | bytes 442376 | tf_op jit(solution)/shard_map/ppermute | solution.py:40
  24.8 11.5 %collective-permute-start.3 = (bf16[2,144,256]{2,1,0:T(8,128)(2,1)S(1)}, bf16[2,144,256]{2,1,0:T(8,128)(2,1)S(1)}, u32[]{:S(2)}, u32[]{:S(2)}) collective-permute-start(bf16[2,144,256]{2,1,0:T(8,128)(2,1)S(1)} %maximum_select_fusion.refs_1_), channel_id=1, source_target_pairs={{384,0},{256,128},{128,256},{0,384},{385,1},{257,129},{129,257},{1... | collective-permute-start | bytes 442376 | tf_op jit(solution)/shard_map/ppermute | solution.py:40
  28.2 20.9 %collective-permute-start.5 = (bf16[144,256]{1,0:T(8,128)(2,1)S(1)}, bf16[144,256]{1,0:T(8,128)(2,1)S(1)}, u32[]{:S(2)}, u32[]{:S(2)}) collective-permute-start(bf16[144,256]{1,0:T(8,128)(2,1)S(1)} %bitcast.37), channel_id=1, source_target_pairs={{0,0},{4,128},{8,256},{12,384},{128,4},{132,132},{136,260},{140,38... | collective-permute-start | bytes 221192 | tf_op jit(solution)/shard_map/ppermute | solution.py:318
  37.6 13.1 %all-to-all-start.1 = ((f32[8,64,256]{2,1,0:T(8,128)}), f32[8,64,256]{2,1,0:T(8,128)S(1)}, u32[]{:S(2)}, u32[]{:S(2)}) async-start(f32[8,64,256]{2,1,0:T(8,128)} %get-tuple-element.14), calls=%async_computation.1 | async-start | bytes 1048576 | tf_op jit(solution)/shard_map/all_to_all | solution.py:28
  42.5 23.9 %collective-permute-start.6 = (bf16[2,256,256]{2,1,0:T(8,128)(2,1)S(1)}, bf16[2,256,256]{2,1,0:T(8,128)(2,1)S(1)}, u32[]{:S(2)}, u32[]{:S(2)}) collective-permute-start(bf16[2,256,256]{2,1,0:T(8,128)(2,1)S(1)} %get-tuple-element.16), channel_id=1, source_target_pairs={{128,0},{0,128},{384,256},{256,384},{129,1},{1,129},{385,257},{257... | collective-permute-start | bytes 786440 | tf_op jit(solution)/shard_map/ppermute | solution.py:40
  51.5 12.8 %collective-permute-start.7 = (bf16[64,256]{1,0:T(8,128)(2,1)S(1)}, bf16[64,256]{1,0:T(8,128)(2,1)S(1)}, u32[]{:S(2)}, u32[]{:S(2)}) collective-permute-start(bf16[64,256]{1,0:T(8,128)(2,1)S(1)} %get-tuple-element.17), channel_id=1, source_target_pairs={{256,0},{384,128},{0,256},{128,384},{257,1},{385,129},{1,257},{129... | collective-permute-start | bytes 98312 | tf_op jit(solution)/shard_map/ppermute | solution.py:40
  58.9 11.6 %all-to-all-start.2 = ((bf16[8,64,256]{2,1,0:T(8,128)(2,1)}), bf16[8,64,256]{2,1,0:T(8,128)(2,1)S(1)}, u32[]{:S(2)}, u32[]{:S(2)}) async-start(bf16[8,64,256]{2,1,0:T(8,128)(2,1)} %get-tuple-element.15), calls=%async_computation.2 | async-start | bytes 524288 | tf_op jit(solution)/shard_map/all_to_all | solution.py:28
  64.4 6.2 %collective-permute-start.8 = (bf16[2,64,256]{2,1,0:T(8,128)(2,1)S(1)}, bf16[2,64,256]{2,1,0:T(8,128)(2,1)S(1)}, u32[]{:S(2)}, u32[]{:S(2)}) collective-permute-start(bf16[2,64,256]{2,1,0:T(8,128)(2,1)S(1)} %pad_maximum_fusion.5), channel_id=1, source_target_pairs={{128,0},{0,128},{384,256},{256,384},{129,1},{1,129},{385,257},{257... | collective-permute-start | bytes 196616 | tf_op jit(solution)/shard_map/ppermute | solution.py:40
  75.9 17.9 %all-to-all-start.3 = ((f32[8,136,128]{2,1,0:T(8,128)}), f32[8,136,128]{2,1,0:T(8,128)S(1)}, u32[]{:S(2)}, u32[]{:S(2)}) async-start(f32[8,136,128]{2,1,0:T(8,128)} %get-tuple-element.19), calls=%async_computation.3 | async-start | bytes 1114112 | tf_op jit(solution)/shard_map/all_to_all | solution.py:28
  80.7 10.1 %collective-permute-start.11 = (bf16[144,256]{1,0:T(8,128)(2,1)S(1)}, bf16[144,256]{1,0:T(8,128)(2,1)S(1)}, u32[]{:S(2)}, u32[]{:S(2)}) collective-permute-start(bf16[144,256]{1,0:T(8,128)(2,1)S(1)} %get-tuple-element.20), channel_id=1, source_target_pairs={{384,0},{256,128},{128,256},{0,384},{385,1},{257,129},{129,257},{1... | collective-permute-start | bytes 221192 | tf_op jit(solution)/shard_map/ppermute | solution.py:40
  83.9 8.4 %collective-permute-start.10 = (bf16[144,256]{1,0:T(8,128)(2,1)S(1)}, bf16[144,256]{1,0:T(8,128)(2,1)S(1)}, u32[]{:S(2)}, u32[]{:S(2)}) collective-permute-start(bf16[144,256]{1,0:T(8,128)(2,1)S(1)} %get-tuple-element.20), channel_id=1, source_target_pairs={{256,0},{384,128},{0,256},{128,384},{257,1},{385,129},{1,257},{129... | collective-permute-start | bytes 221192 | tf_op jit(solution)/shard_map/ppermute | solution.py:40
  86.1 7.6 %collective-permute-start.9 = (bf16[144,256]{1,0:T(8,128)(2,1)S(1)}, bf16[144,256]{1,0:T(8,128)(2,1)S(1)}, u32[]{:S(2)}, u32[]{:S(2)}) collective-permute-start(bf16[144,256]{1,0:T(8,128)(2,1)S(1)} %get-tuple-element.20), channel_id=1, source_target_pairs={{128,0},{0,128},{384,256},{256,384},{129,1},{1,129},{385,257},{257... | collective-permute-start | bytes 221192 | tf_op jit(solution)/shard_map/ppermute | solution.py:40
  95.1 35.7 %all-to-all-start.4 = ((bf16[4,4,144,256]{3,2,1,0:T(8,128)(2,1)}), bf16[4,4,144,256]{3,2,1,0:T(8,128)(2,1)S(1)}, u32[]{:S(2)}, u32[]{:S(2)}) async-start(bf16[4,4,144,256]{3,2,1,0:T(8,128)(2,1)} %broadcast_in_dim.2), calls=%async_computation.4 | async-start | bytes 2359296 | tf_op jit(solution)/shard_map/all_to_all | solution.py:28
  99.9 22.1 %collective-permute-start.14 = (bf16[64,256]{1,0:T(8,128)(2,1)S(1)}, bf16[64,256]{1,0:T(8,128)(2,1)S(1)}, u32[]{:S(2)}, u32[]{:S(2)}) collective-permute-start(bf16[64,256]{1,0:T(8,128)(2,1)S(1)} %get-tuple-element.21), channel_id=1, source_target_pairs={{12,0},{0,4},{4,8},{8,12},{13,1},{1,5},{5,9},{9,13},{14,2},{2,6},{... | collective-permute-start | bytes 98312 | tf_op jit(solution)/shard_map/ppermute | solution.py:36
  107.8 14.7 %collective-permute-start.13 = (bf16[64,256]{1,0:T(8,128)(2,1)S(1)}, bf16[64,256]{1,0:T(8,128)(2,1)S(1)}, u32[]{:S(2)}, u32[]{:S(2)}) collective-permute-start(bf16[64,256]{1,0:T(8,128)(2,1)S(1)} %get-tuple-element.21), channel_id=1, source_target_pairs={{8,0},{12,4},{0,8},{4,12},{9,1},{13,5},{1,9},{5,13},{10,2},{14,6},... | collective-permute-start | bytes 98312 | tf_op jit(solution)/shard_map/ppermute | solution.py:36
  117.8 9.7 %collective-permute-start.12 = (bf16[64,256]{1,0:T(8,128)(2,1)S(1)}, bf16[64,256]{1,0:T(8,128)(2,1)S(1)}, u32[]{:S(2)}, u32[]{:S(2)}) collective-permute-start(bf16[64,256]{1,0:T(8,128)(2,1)S(1)} %get-tuple-element.21), channel_id=1, source_target_pairs={{4,0},{8,4},{12,8},{0,12},{5,1},{9,5},{13,9},{1,13},{6,2},{10,6},{... | collective-permute-start | bytes 98312 | tf_op jit(solution)/shard_map/ppermute | solution.py:36
  127.6 3.2 %collective-permute-start.15 = (bf16[4,64,256]{2,1,0:T(8,128)(2,1)S(1)}, bf16[4,64,256]{2,1,0:T(8,128)(2,1)S(1)}, u32[]{:S(2)}, u32[]{:S(2)}) collective-permute-start(bf16[4,64,256]{2,1,0:T(8,128)(2,1)S(1)} %pad_maximum_fusion.4.refs_1_), channel_id=1, source_target_pairs={{0,16},{16,0},{1,17},{17,1},{2,18},{18,2},{3,19},{19,3},{4,20},{20... | collective-permute-start | bytes 393224 | tf_op jit(solution)/shard_map/ppermute | solution.py:21
  132.6 12.2 %all-to-all-start.5 = ((f32[8,72,128]{2,1,0:T(8,128)}), f32[8,72,128]{2,1,0:T(8,128)S(1)}, u32[]{:S(2)}, u32[]{:S(2)}) async-start(f32[8,72,128]{2,1,0:T(8,128)} %shard_map.78), calls=%async_computation.5 | async-start | bytes 589824 | tf_op jit(solution)/shard_map/all_to_all | solution.py:28
  (3 other events, 21.7 us)

commit v8 on v7

--- a/solution.py
+++ b/solution.py
@@ -206,7 +206,9 @@
             out_ref[first + i, HEAD:, :] = jnp.where(row == 0, highest[:, part], denom[:, part])
 
 
-def merge_kernel(state_ref, out_ref):
+def merge_kernel(state_ref, block_ref, out_ref, copies_ref):
+    for i in range(NY):
+        copies_ref[i] = block_ref[...]
     rows = out_ref.shape[0]
     bests = [state_ref[i, HEAD : HEAD + 1, :] for i in range(NY * NC)]
     highest = bests[0]
@@ -225,40 +227,33 @@
 
 def output_kernel(meta, att_ref, other_ref, weight_ref, out_ref):
     rows = att_ref.shape[1]
+    half = weight_ref.shape[2] // 2
     z, c, w = meta[1], meta[3], meta[4]
-    places = [lax.rem((z ^ k) + NW - w, NW) for k in range(NZ)]
+    steps = [lax.rem((z ^ k) + NW - w, NW) for k in PAIRS]
+    places = [jnp.where(step < 2, step, 5 - step) for step in steps]
     att = [jnp.concatenate([att_ref[at], other_ref[at]], axis=0) for at in places]
     for x in range(NX):
-        place = x * NC
         total = 0.0
         for k in range(NW):
             total = total + lax.dot_general(
+                weight_ref[x, k],
                 att[k],
-                weight_ref[x, k],
                 (((1,), (1,)), ((), ())),
                 preferred_element_type=jnp.float32,
             )
-        rest = total[:, HEAD:]
         for i, core in enumerate((c, 1 - c)):
-            out_ref[place + core, :rows] = total[i * rows : (i + 1) * rows, :HEAD]
-            out_ref[place + core, rows:] = jnp.concatenate(
-                [rest[i * rows + g * 8 : i * rows + g * 8 + 8] for g in range(rows // 8)], axis=1
-            )
+            part = total[:, i * rows : (i + 1) * rows]
+            out_ref[x * NC + core] = jnp.concatenate([part[:half], part[half:]], axis=1)
 
 
 def last_kernel(part_ref, residual_ref, out_ref):
     rows = out_ref.shape[0]
-    half = out_ref.shape[1] // NC
-    wide = half - HEAD
+    columns = []
     for j in range(NC):
         total = (part_ref[j] + part_ref[NC + j]) + (part_ref[2 * NC + j] + part_ref[3 * NC + j])
-        rest = total[rows:]
-        rest = jnp.concatenate(
-            [rest[:, g * wide : (g + 1) * wide] for g in range(rows // 8)], axis=0
-        )
-        total = jnp.concatenate([total[:rows], rest], axis=1)
-        at = slice(j * half, (j + 1) * half)
-        out_ref[:, at] = (residual_ref[:, at].astype(jnp.float32) + total).astype(jnp.bfloat16)
+        columns += [total[:, :rows], total[:, rows:]]
+    total = jnp.transpose(jnp.concatenate(columns, axis=0))
+    out_ref[...] = (residual_ref[...].astype(jnp.float32) + total).astype(jnp.bfloat16)
 
 
 def call(kernel, out, operands, scalars=0, flops=0, scratch=(), held=()):
@@ -344,21 +339,24 @@
     all_new = jnp.stack([new, from_pair(new, "z", 2, NZ)])
     all_new = jnp.concatenate([all_new, from_pair(all_new, "z", 1, NZ)])
 
-    state, out_block = call(
+    out_pair = jnp.stack([out_block, from_pair(out_block, "z", 2, NZ)])
+    state, out_pair = call(
         attention_kernel,
         [((NY * NC, HEAD + 8, 2 * tok_rows), f32)],
         (meta, all_queries, cache, all_new),
         scalars=1,
         flops=4 * 512 * 2560 * 128,
-        held=(out_block,),
+        held=(out_pair,),
     )
     states = exchange(state, ("y", "c"))
-    out_z = jnp.stack([out_block] + [from_pair(out_block, "z", k, NZ) for k in range(1, NZ)])
-    attention, out_z = call(
-        merge_kernel, [((tok_rows, 2 * HEAD), bf16)], (states,), held=(out_z,)
-    )
-    out_weights = exchange(copies(out_z, NY), "y")
-    attention = jnp.stack([attention] + [from_next(attention, "w", k, NW) for k in range(1, NW)])
+    out_z = jnp.concatenate([out_pair, from_pair(out_pair, "z", 1, NZ)])
+    attention, out_copies = call(
+        merge_kernel,
+        [((tok_rows, 2 * HEAD), bf16), ((NY,) + out_z.shape, bf16)],
+        (states, out_z),
+    )
+    out_weights = exchange(out_copies, "y")
+    attention = jnp.stack([attention] + [from_next(attention, "w", k, NW) for k in (1, 3, 2)])
     att_other = swap_core(attention)
     width = D // (NW * NX)
     terms = call(

time: 147 us -> 147 us (level)
  starting transfers between devices: 98 us -> 94.7 us
  waiting for transfers between devices: 29.8 us -> 32.6 us
    ppermute x10 -> x9, starting transfers between devices: 37.9 us -> 33.9 us  [from_pair(): return lax.ppermute(x, axis, [(i ^ bit, i) for i in range(size)])]
    ppermute x10 -> x9, waiting for transfers between devices: 14.4 us -> 16.4 us  [from_pair(): return lax.ppermute(x, axis, [(i ^ bit, i) for i in range(size)])]
  transfers between devices with their start and end apart: 22 -> 21, of which waited for: 10 -> 11; matrix products, arithmetic and copies ran while one was open for 1% -> 1% of each run, Pallas kernels for 1% -> 1%
where the time goes in v8:
time: 147 us; the launch traced here: 145 us
  starting transfers between devices  94.7 us (64%)
  waiting for transfers between devices  32.6 us (22%)
  Pallas kernels  13.4 us (9%)
  local copies, waits for them, and re-layouts  2.86 us (2%)
    all_to_all x6, starting transfers between devices, exchange(): return lax.all_to_all(x, axis, 0, 0, tiled=True)  34.1 us
    ppermute x9, starting transfers between devices, from_pair(): return lax.ppermute(x, axis, [(i ^ bit, i) for i in range(size)])  33.9 us
    ppermute x3, starting transfers between devices, from_next(): return lax.ppermute(x, axis, [((i + step) % size, i) for i in range(size)])  22.1 us
    ppermute x9, waiting for transfers between devices, from_pair(): return lax.ppermute(x, axis, [(i ^ bit, i) for i in range(size)])  16.4 us
    pallas_call x7, Pallas kernels, call(): pl.pallas_call(body, out_shape=shapes, in_specs=specs + [pl.BlockSpec(mem...  13.4 us
    all_to_all x6, waiting for transfers between devices, exchange(): return lax.all_to_all(x, axis, 0, 0, tiled=True)  9.37 us
    ppermute x3, waiting for transfers between devices, from_next(): return lax.ppermute(x, axis, [((i + step) % size, i) for i in range(size)])  5.47 us
    ppermute x2, starting transfers between devices, swap_core(): return lax.ppermute(x, 'c', [(0, 1), (1, 0)])  3.98 us
  transfers between devices with their start and end apart: 21, of which 11 were waited for; matrix products, arithmetic and copies ran while one was open for 1% of the time, Pallas kernels for 1%

profile of v8, /device:TPU:24, one launch (start us, length us, event | category | flops | bytes accessed | tf_op | source)
XLA Modules:
  0.0 145.1 jit_solution(3981124328355053589)
XLA Ops:
  2.6 2.1 %shard_map.73 = bf16[8,64,1152]{2,1,0:T(8,128)(2,1)} custom-call(s32[5]{0:T(128)S(1)} %stack.75.refs_0_, bf16[64,4608]{1,0:T(8,128)(2,1)S(1)} %copy-done, f32[1,4608]{1,0:T(1,128)S(1)} %reshape.14.refs_2_), custom_call_target="tpu_custom_call" | custom-call | flops 1769472 | bytes 608276 | tf_op jit(solution)/shard_map/pallas_call | solution.py:271
  4.7 9.2 %all-to-all-start = ((bf16[8,64,1152]{2,1,0:T(8,128)(2,1)}), bf16[8,64,1152]{2,1,0:T(8,128)(2,1)S(1)}, u32[]{:S(2)}, u32[]{:S(2)}) async-start(bf16[8,64,1152]{2,1,0:T(8,128)(2,1)} %shard_map.73), calls=%async_computation | async-start | bytes 2359296 | tf_op jit(solution)/shard_map/all_to_all | solution.py:28
  14.0 2.1 %collective-permute-start = (bf16[144,256]{1,0:T(8,128)(2,1)S(1)}, bf16[144,256]{1,0:T(8,128)(2,1)S(1)}, u32[]{:S(2)}, u32[]{:S(2)}) collective-permute-start(bf16[144,256]{1,0:T(8,128)(2,1)S(1)} %get-tuple-element.24), channel_id=1, source_target_pairs={{0,16},{16,0},{1,17},{17,1},{2,18},{18,2},{3,19},{19,3},{4,20},{20... | collective-permute-start | bytes 221192 | tf_op jit(solution)/shard_map/ppermute | solution.py:21
  18.1 2.7 %collective-permute-start.1 = (bf16[2,144,256]{2,1,0:T(8,128)(2,1)S(1)}, bf16[2,144,256]{2,1,0:T(8,128)(2,1)S(1)}, u32[]{:S(2)}, u32[]{:S(2)}) collective-permute-start(bf16[2,144,256]{2,1,0:T(8,128)(2,1)S(1)} %maximum_select_fusion.refs_1_), channel_id=1, source_target_pairs={{128,0},{0,128},{384,256},{256,384},{129,1},{1,129},{385,257},{257... | collective-permute-start | bytes 442376 | tf_op jit(solution)/shard_map/ppermute | solution.py:40
  20.8 4.1 %collective-permute-start.2 = (bf16[2,144,256]{2,1,0:T(8,128)(2,1)S(1)}, bf16[2,144,256]{2,1,0:T(8,128)(2,1)S(1)}, u32[]{:S(2)}, u32[]{:S(2)}) collective-permute-start(bf16[2,144,256]{2,1,0:T(8,128)(2,1)S(1)} %maximum_select_fusion.refs_1_), channel_id=1, source_target_pairs={{256,0},{384,128},{0,256},{128,384},{257,1},{385,129},{1,257},{129... | collective-permute-start | bytes 442376 | tf_op jit(solution)/shard_map/ppermute | solution.py:40
  24.8 3.4 %collective-permute-start.3 = (bf16[2,144,256]{2,1,0:T(8,128)(2,1)S(1)}, bf16[2,144,256]{2,1,0:T(8,128)(2,1)S(1)}, u32[]{:S(2)}, u32[]{:S(2)}) collective-permute-start(bf16[2,144,256]{2,1,0:T(8,128)(2,1)S(1)} %maximum_select_fusion.refs_1_), channel_id=1, source_target_pairs={{384,0},{256,128},{128,256},{0,384},{385,1},{257,129},{129,257},{1... | collective-permute-start | bytes 442376 | tf_op jit(solution)/shard_map/ppermute | solution.py:40
  30.5 5.8 %collective-permute-done.2.refs_3_ = bf16[2,144,256]{2,1,0:T(8,128)(2,1)S(1)} collective-permute-done((bf16[2,144,256]{2,1,0:T(8,128)(2,1)S(1)}, bf16[2,144,256]{2,1,0:T(8,128)(2,1)S(1)}, u32[]{:S(2)}, u32[]{:S(2)}) %collective-permute-start.2) | collective-permute-done | bytes 147488 | tf_op jit(solution)/shard_map/ppermute | solution.py:40
  37.6 4.8 %all-to-all-start.1 = ((f32[8,64,256]{2,1,0:T(8,128)}), f32[8,64,256]{2,1,0:T(8,128)S(1)}, u32[]{:S(2)}, u32[]{:S(2)}) async-start(f32[8,64,256]{2,1,0:T(8,128)} %get-tuple-element.14), calls=%async_computation.1 | async-start | bytes 1048576 | tf_op jit(solution)/shard_map/all_to_all | solution.py:28
  42.5 6.4 %collective-permute-start.6 = (bf16[2,256,256]{2,1,0:T(8,128)(2,1)S(1)}, bf16[2,256,256]{2,1,0:T(8,128)(2,1)S(1)}, u32[]{:S(2)}, u32[]{:S(2)}) collective-permute-start(bf16[2,256,256]{2,1,0:T(8,128)(2,1)S(1)} %get-tuple-element.16), channel_id=1, source_target_pairs={{128,0},{0,128},{384,256},{256,384},{129,1},{1,129},{385,257},{257... | collective-permute-start | bytes 786440 | tf_op jit(solution)/shard_map/ppermute | solution.py:40
  51.5 7.4 %collective-permute-start.7 = (bf16[64,256]{1,0:T(8,128)(2,1)S(1)}, bf16[64,256]{1,0:T(8,128)(2,1)S(1)}, u32[]{:S(2)}, u32[]{:S(2)}) collective-permute-start(bf16[64,256]{1,0:T(8,128)(2,1)S(1)} %get-tuple-element.17), channel_id=1, source_target_pairs={{256,0},{384,128},{0,256},{128,384},{257,1},{385,129},{1,257},{129... | collective-permute-start | bytes 98312 | tf_op jit(solution)/shard_map/ppermute | solution.py:40
  59.0 5.4 %all-to-all-start.2 = ((bf16[8,64,256]{2,1,0:T(8,128)(2,1)}), bf16[8,64,256]{2,1,0:T(8,128)(2,1)S(1)}, u32[]{:S(2)}, u32[]{:S(2)}) async-start(bf16[8,64,256]{2,1,0:T(8,128)(2,1)} %get-tuple-element.15), calls=%async_computation.2 | async-start | bytes 524288 | tf_op jit(solution)/shard_map/all_to_all | solution.py:28
  66.4 3.8 %collective-permute-start.8 = (bf16[2,64,256]{2,1,0:T(8,128)(2,1)S(1)}, bf16[2,64,256]{2,1,0:T(8,128)(2,1)S(1)}, u32[]{:S(2)}, u32[]{:S(2)}) collective-permute-start(bf16[2,64,256]{2,1,0:T(8,128)(2,1)S(1)} %pad_maximum_fusion.6), channel_id=1, source_target_pairs={{128,0},{0,128},{384,256},{256,384},{129,1},{1,129},{385,257},{257... | collective-permute-start | bytes 196616 | tf_op jit(solution)/shard_map/ppermute | solution.py:40
  70.2 2.6 %collective-permute-done.9 = bf16[144,256]{1,0:T(8,128)(2,1)S(1)} collective-permute-done((bf16[144,256]{1,0:T(8,128)(2,1)S(1)}, bf16[144,256]{1,0:T(8,128)(2,1)S(1)}, u32[]{:S(2)}, u32[]{:S(2)}) %collective-permute-start.9) | collective-permute-done | bytes 73760 | tf_op jit(solution)/shard_map/ppermute | solution.py:40
  73.9 5.3 %shard_map.76 = (f32[8,136,128]{2,1,0:T(8,128)}, bf16[2,144,256]{2,1,0:T(8,128)(2,1)S(1)}) custom-call(s32[5]{0:T(128)S(1)} %stack.75.refs_0_, bf16[8,64,256]{2,1,0:T(8,128)(2,1)S(1)} %all-to-all-done.2.refs_1_, bf16[4,256,256]{2,1,0:T(8,128)(2,1)S(1)} %pad_maximum_fusion.refs_2_, ...), custom_call_target="tpu_custom_call", output_to_operand_aliasing={{1}: (4, {})} | custom-call | flops 671088640 | bytes 917524 | tf_op jit(solution)/shard_map/pallas_call | solution.py:271
  79.3 4.8 %all-to-all-start.3 = ((f32[8,136,128]{2,1,0:T(8,128)}), f32[8,136,128]{2,1,0:T(8,128)S(1)}, u32[]{:S(2)}, u32[]{:S(2)}) async-start(f32[8,136,128]{2,1,0:T(8,128)} %get-tuple-element.19), calls=%async_computation.3 | async-start | bytes 1114112 | tf_op jit(solution)/shard_map/all_to_all | solution.py:28
  84.0 2.4 %collective-permute-start.10 = (bf16[2,144,256]{2,1,0:T(8,128)(2,1)S(1)}, bf16[2,144,256]{2,1,0:T(8,128)(2,1)S(1)}, u32[]{:S(2)}, u32[]{:S(2)}) collective-permute-start(bf16[2,144,256]{2,1,0:T(8,128)(2,1)S(1)} %get-tuple-element.20), channel_id=1, source_target_pairs={{128,0},{0,128},{384,256},{256,384},{129,1},{1,129},{385,257},{257... | collective-permute-start | bytes 442376 | tf_op jit(solution)/shard_map/ppermute | solution.py:40
  86.5 5.4 %collective-permute-done.10 = bf16[2,144,256]{2,1,0:T(8,128)(2,1)S(1)} collective-permute-done((bf16[2,144,256]{2,1,0:T(8,128)(2,1)S(1)}, bf16[2,144,256]{2,1,0:T(8,128)(2,1)S(1)}, u32[]{:S(2)}, u32[]{:S(2)}) %collective-permute-start.10) | collective-permute-done | bytes 147488 | tf_op jit(solution)/shard_map/ppermute | solution.py:40
  93.9 5.6 %all-to-all-start.4 = ((bf16[4,4,144,256]{3,2,1,0:T(8,128)(2,1)}), bf16[4,4,144,256]{3,2,1,0:T(8,128)(2,1)S(1)}, u32[]{:S(2)}, u32[]{:S(2)}) async-start(bf16[4,4,144,256]{3,2,1,0:T(8,128)(2,1)} %get-tuple-element.22), calls=%async_computation.4 | async-start | bytes 2359296 | tf_op jit(solution)/shard_map/all_to_all | solution.py:28
  99.4 12.3 %collective-permute-start.13 = (bf16[64,256]{1,0:T(8,128)(2,1)S(1)}, bf16[64,256]{1,0:T(8,128)(2,1)S(1)}, u32[]{:S(2)}, u32[]{:S(2)}) collective-permute-start(bf16[64,256]{1,0:T(8,128)(2,1)S(1)} %get-tuple-element.21), channel_id=1, source_target_pairs={{8,0},{12,4},{0,8},{4,12},{9,1},{13,5},{1,9},{5,13},{10,2},{14,6},... | collective-permute-start | bytes 98312 | tf_op jit(solution)/shard_map/ppermute | solution.py:36
  111.8 5.1 %collective-permute-start.12 = (bf16[64,256]{1,0:T(8,128)(2,1)S(1)}, bf16[64,256]{1,0:T(8,128)(2,1)S(1)}, u32[]{:S(2)}, u32[]{:S(2)}) collective-permute-start(bf16[64,256]{1,0:T(8,128)(2,1)S(1)} %get-tuple-element.21), channel_id=1, source_target_pairs={{12,0},{0,4},{4,8},{8,12},{13,1},{1,5},{5,9},{9,13},{14,2},{2,6},{... | collective-permute-start | bytes 98312 | tf_op jit(solution)/shard_map/ppermute | solution.py:36
  116.9 4.6 %collective-permute-start.11 = (bf16[64,256]{1,0:T(8,128)(2,1)S(1)}, bf16[64,256]{1,0:T(8,128)(2,1)S(1)}, u32[]{:S(2)}, u32[]{:S(2)}) collective-permute-start(bf16[64,256]{1,0:T(8,128)(2,1)S(1)} %get-tuple-element.21), channel_id=1, source_target_pairs={{4,0},{8,4},{12,8},{0,12},{5,1},{9,5},{13,9},{1,13},{6,2},{10,6},{... | collective-permute-start | bytes 98312 | tf_op jit(solution)/shard_map/ppermute | solution.py:36
  121.7 5.4 %collective-permute-done.11 = bf16[64,256]{1,0:T(8,128)(2,1)S(1)} collective-permute-done((bf16[64,256]{1,0:T(8,128)(2,1)S(1)}, bf16[64,256]{1,0:T(8,128)(2,1)S(1)}, u32[]{:S(2)}, u32[]{:S(2)}) %collective-permute-start.11) | collective-permute-done | bytes 32800 | tf_op jit(solution)/shard_map/ppermute | solution.py:36
  132.1 4.3 %all-to-all-start.5 = ((f32[8,72,128]{2,1,0:T(8,128)}), f32[8,72,128]{2,1,0:T(8,128)S(1)}, u32[]{:S(2)}, u32[]{:S(2)}) async-start(f32[8,72,128]{2,1,0:T(8,128)} %shard_map.78), calls=%async_computation.5 | async-start | bytes 589824 | tf_op jit(solution)/shard_map/all_to_all | solution.py:28
  137.3 7.0 %all-to-all-done.5.refs_0_ = f32[8,72,128]{2,1,0:T(8,128)S(1)} async-done(((f32[8,72,128]{2,1,0:T(8,128)}), f32[8,72,128]{2,1,0:T(8,128)S(1)}, u32[]{:S(2)}, u32[]{:S(2)}) %all-to-all-start.5) | async-done | bytes 294944 | tf_op jit(solution)/shard_map/all_to_all | solution.py:28
  (53 shorter events, 22.1 us)
Async XLA Ops:
  4.7 11.3 %copy-start.2 = (bf16[256,128]{1,0:T(8,128)(2,1)S(1)}, bf16[256,128]{1,0:T(8,128)(2,1)}, u32[]{:S(2)}) copy-start(bf16[256,128]{1,0:T(8,128)(2,1)} %param.11) | copy-start | bytes 196612
  4.7 11.4 %copy-start.3 = (bf16[256,128]{1,0:T(8,128)(2,1)S(1)}, bf16[256,128]{1,0:T(8,128)(2,1)}, u32[]{:S(2)}) copy-start(bf16[256,128]{1,0:T(8,128)(2,1)} %param.12) | copy-start | bytes 196612
  4.7 23.5 %copy-start.4 = (bf16[256,144]{0,1:T(8,128)(2,1)S(1)}, bf16[256,144]{0,1:T(8,128)(2,1)}, u32[]{:S(2)}) copy-start(bf16[256,144]{0,1:T(8,128)(2,1)} %param.10) | copy-start | bytes 221188
  4.7 31.6 %all-to-all-start = ((bf16[8,64,1152]{2,1,0:T(8,128)(2,1)}), bf16[8,64,1152]{2,1,0:T(8,128)(2,1)S(1)}, u32[]{:S(2)}, u32[]{:S(2)}) async-start(bf16[8,64,1152]{2,1,0:T(8,128)(2,1)} %shard_map.73), calls=%async_computation | async-start | bytes 2359296 | tf_op jit(solution)/shard_map/all_to_all | solution.py:28
  14.0 4.1 %collective-permute-start = (bf16[144,256]{1,0:T(8,128)(2,1)S(1)}, bf16[144,256]{1,0:T(8,128)(2,1)S(1)}, u32[]{:S(2)}, u32[]{:S(2)}) collective-permute-start(bf16[144,256]{1,0:T(8,128)(2,1)S(1)} %get-tuple-element.24), channel_id=1, source_target_pairs={{0,16},{16,0},{1,17},{17,1},{2,18},{18,2},{3,19},{19,3},{4,20},{20... | collective-permute-start | bytes 221192 | tf_op jit(solution)/shard_map/ppermute | solution.py:21
  16.1 12.8 %collective-permute-start.4 = (bf16[256,256]{1,0:T(8,128)(2,1)S(1)}, bf16[256,256]{1,0:T(8,128)(2,1)S(1)}, u32[]{:S(2)}, u32[]{:S(2)}) collective-permute-start(bf16[256,256]{1,0:T(8,128)(2,1)S(1)} %constant_dynamic-update-slice_fusion), channel_id=1, source_target_pairs={{256,0},{384,128},{0,256},{128,384},{257,1},{385,129},{1,257},{129... | collective-permute-start | bytes 393224 | tf_op jit(solution)/shard_map/ppermute | solution.py:40
  18.1 12.4 %collective-permute-start.1 = (bf16[2,144,256]{2,1,0:T(8,128)(2,1)S(1)}, bf16[2,144,256]{2,1,0:T(8,128)(2,1)S(1)}, u32[]{:S(2)}, u32[]{:S(2)}) collective-permute-start(bf16[2,144,256]{2,1,0:T(8,128)(2,1)S(1)} %maximum_select_fusion.refs_1_), channel_id=1, source_target_pairs={{128,0},{0,128},{384,256},{256,384},{129,1},{1,129},{385,257},{257... | collective-permute-start | bytes 442376 | tf_op jit(solution)/shard_map/ppermute | solution.py:40
  20.8 15.5 %collective-permute-start.2 = (bf16[2,144,256]{2,1,0:T(8,128)(2,1)S(1)}, bf16[2,144,256]{2,1,0:T(8,128)(2,1)S(1)}, u32[]{:S(2)}, u32[]{:S(2)}) collective-permute-start(bf16[2,144,256]{2,1,0:T(8,128)(2,1)S(1)} %maximum_select_fusion.refs_1_), channel_id=1, source_target_pairs={{256,0},{384,128},{0,256},{128,384},{257,1},{385,129},{1,257},{129... | collective-permute-start | bytes 442376 | tf_op jit(solution)/shard_map/ppermute | solution.py:40
  24.8 11.5 %collective-permute-start.3 = (bf16[2,144,256]{2,1,0:T(8,128)(2,1)S(1)}, bf16[2,144,256]{2,1,0:T(8,128)(2,1)S(1)}, u32[]{:S(2)}, u32[]{:S(2)}) collective-permute-start(bf16[2,144,256]{2,1,0:T(8,128)(2,1)S(1)} %maximum_select_fusion.refs_1_), channel_id=1, source_target_pairs={{384,0},{256,128},{128,256},{0,384},{385,1},{257,129},{129,257},{1... | collective-permute-start | bytes 442376 | tf_op jit(solution)/shard_map/ppermute | solution.py:40
  28.2 20.9 %collective-permute-start.5 = (bf16[144,256]{1,0:T(8,128)(2,1)S(1)}, bf16[144,256]{1,0:T(8,128)(2,1)S(1)}, u32[]{:S(2)}, u32[]{:S(2)}) collective-permute-start(bf16[144,256]{1,0:T(8,128)(2,1)S(1)} %bitcast.33), channel_id=1, source_target_pairs={{0,0},{4,128},{8,256},{12,384},{128,4},{132,132},{136,260},{140,38... | collective-permute-start | bytes 221192 | tf_op jit(solution)/shard_map/ppermute | solution.py:313
  37.6 13.1 %all-to-all-start.1 = ((f32[8,64,256]{2,1,0:T(8,128)}), f32[8,64,256]{2,1,0:T(8,128)S(1)}, u32[]{:S(2)}, u32[]{:S(2)}) async-start(f32[8,64,256]{2,1,0:T(8,128)} %get-tuple-element.14), calls=%async_computation.1 | async-start | bytes 1048576 | tf_op jit(solution)/shard_map/all_to_all | solution.py:28
  42.5 16.5 %collective-permute-start.6 = (bf16[2,256,256]{2,1,0:T(8,128)(2,1)S(1)}, bf16[2,256,256]{2,1,0:T(8,128)(2,1)S(1)}, u32[]{:S(2)}, u32[]{:S(2)}) collective-permute-start(bf16[2,256,256]{2,1,0:T(8,128)(2,1)S(1)} %get-tuple-element.16), channel_id=1, source_target_pairs={{128,0},{0,128},{384,256},{256,384},{129,1},{1,129},{385,257},{257... | collective-permute-start | bytes 786440 | tf_op jit(solution)/shard_map/ppermute | solution.py:40
  51.5 14.8 %collective-permute-start.7 = (bf16[64,256]{1,0:T(8,128)(2,1)S(1)}, bf16[64,256]{1,0:T(8,128)(2,1)S(1)}, u32[]{:S(2)}, u32[]{:S(2)}) collective-permute-start(bf16[64,256]{1,0:T(8,128)(2,1)S(1)} %get-tuple-element.17), channel_id=1, source_target_pairs={{256,0},{384,128},{0,256},{128,384},{257,1},{385,129},{1,257},{129... | collective-permute-start | bytes 98312 | tf_op jit(solution)/shard_map/ppermute | solution.py:40
  59.0 14.9 %all-to-all-start.2 = ((bf16[8,64,256]{2,1,0:T(8,128)(2,1)}), bf16[8,64,256]{2,1,0:T(8,128)(2,1)S(1)}, u32[]{:S(2)}, u32[]{:S(2)}) async-start(bf16[8,64,256]{2,1,0:T(8,128)(2,1)} %get-tuple-element.15), calls=%async_computation.2 | async-start | bytes 524288 | tf_op jit(solution)/shard_map/all_to_all | solution.py:28
  64.4 8.4 %collective-permute-start.9 = (bf16[144,256]{1,0:T(8,128)(2,1)S(1)}, bf16[144,256]{1,0:T(8,128)(2,1)S(1)}, u32[]{:S(2)}, u32[]{:S(2)}) collective-permute-start(bf16[144,256]{1,0:T(8,128)(2,1)S(1)} %get-tuple-element.18), channel_id=1, source_target_pairs={{256,0},{384,128},{0,256},{128,384},{257,1},{385,129},{1,257},{129... | collective-permute-start | bytes 221192 | tf_op jit(solution)/shard_map/ppermute | solution.py:40
  66.4 7.5 %collective-permute-start.8 = (bf16[2,64,256]{2,1,0:T(8,128)(2,1)S(1)}, bf16[2,64,256]{2,1,0:T(8,128)(2,1)S(1)}, u32[]{:S(2)}, u32[]{:S(2)}) collective-permute-start(bf16[2,64,256]{2,1,0:T(8,128)(2,1)S(1)} %pad_maximum_fusion.6), channel_id=1, source_target_pairs={{128,0},{0,128},{384,256},{256,384},{129,1},{1,129},{385,257},{257... | collective-permute-start | bytes 196616 | tf_op jit(solution)/shard_map/ppermute | solution.py:40
  79.3 13.4 %all-to-all-start.3 = ((f32[8,136,128]{2,1,0:T(8,128)}), f32[8,136,128]{2,1,0:T(8,128)S(1)}, u32[]{:S(2)}, u32[]{:S(2)}) async-start(f32[8,136,128]{2,1,0:T(8,128)} %get-tuple-element.19), calls=%async_computation.3 | async-start | bytes 1114112 | tf_op jit(solution)/shard_map/all_to_all | solution.py:28
  84.0 7.8 %collective-permute-start.10 = (bf16[2,144,256]{2,1,0:T(8,128)(2,1)S(1)}, bf16[2,144,256]{2,1,0:T(8,128)(2,1)S(1)}, u32[]{:S(2)}, u32[]{:S(2)}) collective-permute-start(bf16[2,144,256]{2,1,0:T(8,128)(2,1)S(1)} %get-tuple-element.20), channel_id=1, source_target_pairs={{128,0},{0,128},{384,256},{256,384},{129,1},{1,129},{385,257},{257... | collective-permute-start | bytes 442376 | tf_op jit(solution)/shard_map/ppermute | solution.py:40
  93.9 36.4 %all-to-all-start.4 = ((bf16[4,4,144,256]{3,2,1,0:T(8,128)(2,1)}), bf16[4,4,144,256]{3,2,1,0:T(8,128)(2,1)S(1)}, u32[]{:S(2)}, u32[]{:S(2)}) async-start(bf16[4,4,144,256]{3,2,1,0:T(8,128)(2,1)} %get-tuple-element.22), calls=%async_computation.4 | async-start | bytes 2359296 | tf_op jit(solution)/shard_map/all_to_all | solution.py:28
  99.4 22.1 %collective-permute-start.13 = (bf16[64,256]{1,0:T(8,128)(2,1)S(1)}, bf16[64,256]{1,0:T(8,128)(2,1)S(1)}, u32[]{:S(2)}, u32[]{:S(2)}) collective-permute-start(bf16[64,256]{1,0:T(8,128)(2,1)S(1)} %get-tuple-element.21), channel_id=1, source_target_pairs={{8,0},{12,4},{0,8},{4,12},{9,1},{13,5},{1,9},{5,13},{10,2},{14,6},... | collective-permute-start | bytes 98312 | tf_op jit(solution)/shard_map/ppermute | solution.py:36
  111.8 9.9 %collective-permute-start.12 = (bf16[64,256]{1,0:T(8,128)(2,1)S(1)}, bf16[64,256]{1,0:T(8,128)(2,1)S(1)}, u32[]{:S(2)}, u32[]{:S(2)}) collective-permute-start(bf16[64,256]{1,0:T(8,128)(2,1)S(1)} %get-tuple-element.21), channel_id=1, source_target_pairs={{12,0},{0,4},{4,8},{8,12},{13,1},{1,5},{5,9},{9,13},{14,2},{2,6},{... | collective-permute-start | bytes 98312 | tf_op jit(solution)/shard_map/ppermute | solution.py:36
  116.9 10.1 %collective-permute-start.11 = (bf16[64,256]{1,0:T(8,128)(2,1)S(1)}, bf16[64,256]{1,0:T(8,128)(2,1)S(1)}, u32[]{:S(2)}, u32[]{:S(2)}) collective-permute-start(bf16[64,256]{1,0:T(8,128)(2,1)S(1)} %get-tuple-element.21), channel_id=1, source_target_pairs={{4,0},{8,4},{12,8},{0,12},{5,1},{9,5},{13,9},{1,13},{6,2},{10,6},{... | collective-permute-start | bytes 98312 | tf_op jit(solution)/shard_map/ppermute | solution.py:36
  127.0 3.2 %collective-permute-start.14 = (bf16[4,64,256]{2,1,0:T(8,128)(2,1)S(1)}, bf16[4,64,256]{2,1,0:T(8,128)(2,1)S(1)}, u32[]{:S(2)}, u32[]{:S(2)}) collective-permute-start(bf16[4,64,256]{2,1,0:T(8,128)(2,1)S(1)} %pad_maximum_fusion.5.refs_1_), channel_id=1, source_target_pairs={{0,16},{16,0},{1,17},{17,1},{2,18},{18,2},{3,19},{19,3},{4,20},{20... | collective-permute-start | bytes 393224 | tf_op jit(solution)/shard_map/ppermute | solution.py:21
  132.1 12.2 %all-to-all-start.5 = ((f32[8,72,128]{2,1,0:T(8,128)}), f32[8,72,128]{2,1,0:T(8,128)S(1)}, u32[]{:S(2)}, u32[]{:S(2)}) async-start(f32[8,72,128]{2,1,0:T(8,128)} %shard_map.78), calls=%async_computation.5 | async-start | bytes 589824 | tf_op jit(solution)/shard_map/all_to_all | solution.py:28
  (2 other events, 10.3 us)

commit v9 on v8

--- a/solution.py
+++ b/solution.py
@@ -329,11 +329,10 @@
     cosine, sine_part = jnp.cos(angles), jnp.sin(angles)
     cosine = jnp.concatenate([cosine, cosine], axis=1)
     sine_part = jnp.concatenate([-sine_part, sine_part], axis=1)
-    queries, new, out_block = call(
+    queries, new = call(
         rotary_kernel,
         [((NY * NC, tok_rows, 2 * HEAD), bf16), ((tok_rows, 2 * HEAD), bf16)],
         (partial, cosine, sine_part),
-        held=(out_block,),
     )
     all_queries = exchange(queries, ("y", "c"))
     all_new = jnp.stack([new, from_pair(new, "z", 2, NZ)])

time: 147 us -> 144 us (0.980)
  starting transfers between devices: 94.7 us -> 92.4 us
    ppermute x9, starting transfers between devices: 33.9 us -> 31.4 us  [from_pair(): return lax.ppermute(x, axis, [(i ^ bit, i) for i in range(size)])]
    all_to_all x6, waiting for transfers between devices: 9.37 us -> 7.78 us  [exchange(): return lax.all_to_all(x, axis, 0, 0, tiled=True)]
  transfers between devices with their start and end apart: 21 -> 21, of which waited for: 11 -> 9; matrix products, arithmetic and copies ran while one was open for 1% -> 1% of each run, Pallas kernels for 1% -> 1%
where the time goes in v9:
time: 144 us; the launch traced here: 143 us
  starting transfers between devices  92.4 us (64%)
  waiting for transfers between devices  32.8 us (23%)
  Pallas kernels  13.4 us (9%)
  local copies, waits for them, and re-layouts  2.86 us (2%)
    all_to_all x6, starting transfers between devices, exchange(): return lax.all_to_all(x, axis, 0, 0, tiled=True)  34.2 us
    ppermute x9, starting transfers between devices, from_pair(): return lax.ppermute(x, axis, [(i ^ bit, i) for i in range(size)])  31.4 us
    ppermute x3, starting transfers between devices, from_next(): return lax.ppermute(x, axis, [((i + step) % size, i) for i in range(size)])  22.1 us
    ppermute x9, waiting for transfers between devices, from_pair(): return lax.ppermute(x, axis, [(i ^ bit, i) for i in range(size)])  17.1 us
    pallas_call x7, Pallas kernels, call(): pl.pallas_call(body, out_shape=shapes, in_specs=specs + [pl.BlockSpec(mem...  13.4 us
    all_to_all x6, waiting for transfers between devices, exchange(): return lax.all_to_all(x, axis, 0, 0, tiled=True)  7.78 us
    ppermute x3, waiting for transfers between devices, from_next(): return lax.ppermute(x, axis, [((i + step) % size, i) for i in range(size)])  6.55 us
    ppermute x2, starting transfers between devices, swap_core(): return lax.ppermute(x, 'c', [(0, 1), (1, 0)])  3.98 us
  transfers between devices with their start and end apart: 21, of which 9 were waited for; matrix products, arithmetic and copies ran while one was open for 1% of the time, Pallas kernels for 1%

profile of v9, /device:TPU:24, one launch (start us, length us, event | category | flops | bytes accessed | tf_op | source)
XLA Modules:
  0.0 142.9 jit_solution(5413136940285875471)
XLA Ops:
  2.6 2.1 %shard_map.73 = bf16[8,64,1152]{2,1,0:T(8,128)(2,1)} custom-call(s32[5]{0:T(128)S(1)} %stack.75.refs_0_, bf16[64,4608]{1,0:T(8,128)(2,1)S(1)} %copy-done, f32[1,4608]{1,0:T(1,128)S(1)} %reshape.14.refs_2_), custom_call_target="tpu_custom_call" | custom-call | flops 1769472 | bytes 608276 | tf_op jit(solution)/shard_map/pallas_call | solution.py:271
  4.7 9.2 %all-to-all-start = ((bf16[8,64,1152]{2,1,0:T(8,128)(2,1)}), bf16[8,64,1152]{2,1,0:T(8,128)(2,1)S(1)}, u32[]{:S(2)}, u32[]{:S(2)}) async-start(bf16[8,64,1152]{2,1,0:T(8,128)(2,1)} %shard_map.73), calls=%async_computation | async-start | bytes 2359296 | tf_op jit(solution)/shard_map/all_to_all | solution.py:28
  14.0 2.1 %collective-permute-start = (bf16[144,256]{1,0:T(8,128)(2,1)S(1)}, bf16[144,256]{1,0:T(8,128)(2,1)S(1)}, u32[]{:S(2)}, u32[]{:S(2)}) collective-permute-start(bf16[144,256]{1,0:T(8,128)(2,1)S(1)} %get-tuple-element.22), channel_id=1, source_target_pairs={{0,16},{16,0},{1,17},{17,1},{2,18},{18,2},{3,19},{19,3},{4,20},{20... | collective-permute-start | bytes 221192 | tf_op jit(solution)/shard_map/ppermute | solution.py:21
  18.1 2.7 %collective-permute-start.1 = (bf16[2,144,256]{2,1,0:T(8,128)(2,1)S(1)}, bf16[2,144,256]{2,1,0:T(8,128)(2,1)S(1)}, u32[]{:S(2)}, u32[]{:S(2)}) collective-permute-start(bf16[2,144,256]{2,1,0:T(8,128)(2,1)S(1)} %maximum_select_fusion.refs_1_), channel_id=1, source_target_pairs={{128,0},{0,128},{384,256},{256,384},{129,1},{1,129},{385,257},{257... | collective-permute-start | bytes 442376 | tf_op jit(solution)/shard_map/ppermute | solution.py:40
  20.8 4.1 %collective-permute-start.2 = (bf16[2,144,256]{2,1,0:T(8,128)(2,1)S(1)}, bf16[2,144,256]{2,1,0:T(8,128)(2,1)S(1)}, u32[]{:S(2)}, u32[]{:S(2)}) collective-permute-start(bf16[2,144,256]{2,1,0:T(8,128)(2,1)S(1)} %maximum_select_fusion.refs_1_), channel_id=1, source_target_pairs={{256,0},{384,128},{0,256},{128,384},{257,1},{385,129},{1,257},{129... | collective-permute-start | bytes 442376 | tf_op jit(solution)/shard_map/ppermute | solution.py:40
  24.8 3.4 %collective-permute-start.3 = (bf16[2,144,256]{2,1,0:T(8,128)(2,1)S(1)}, bf16[2,144,256]{2,1,0:T(8,128)(2,1)S(1)}, u32[]{:S(2)}, u32[]{:S(2)}) collective-permute-start(bf16[2,144,256]{2,1,0:T(8,128)(2,1)S(1)} %maximum_select_fusion.refs_1_), channel_id=1, source_target_pairs={{384,0},{256,128},{128,256},{0,384},{385,1},{257,129},{129,257},{1... | collective-permute-start | bytes 442376 | tf_op jit(solution)/shard_map/ppermute | solution.py:40
  30.5 5.8 %collective-permute-done.2.refs_3_ = bf16[2,144,256]{2,1,0:T(8,128)(2,1)S(1)} collective-permute-done((bf16[2,144,256]{2,1,0:T(8,128)(2,1)S(1)}, bf16[2,144,256]{2,1,0:T(8,128)(2,1)S(1)}, u32[]{:S(2)}, u32[]{:S(2)}) %collective-permute-start.2) | collective-permute-done | bytes 147488 | tf_op jit(solution)/shard_map/ppermute | solution.py:40
  37.6 4.8 %all-to-all-start.1 = ((f32[8,64,256]{2,1,0:T(8,128)}), f32[8,64,256]{2,1,0:T(8,128)S(1)}, u32[]{:S(2)}, u32[]{:S(2)}) async-start(f32[8,64,256]{2,1,0:T(8,128)} %get-tuple-element.13), calls=%async_computation.1 | async-start | bytes 1048576 | tf_op jit(solution)/shard_map/all_to_all | solution.py:28
  42.7 7.4 %collective-permute-start.9 = (bf16[144,256]{1,0:T(8,128)(2,1)S(1)}, bf16[144,256]{1,0:T(8,128)(2,1)S(1)}, u32[]{:S(2)}, u32[]{:S(2)}) collective-permute-start(bf16[144,256]{1,0:T(8,128)(2,1)S(1)} %collective-permute-done.8), channel_id=1, source_target_pairs={{256,0},{384,128},{0,256},{128,384},{257,1},{385,129},{1,257},{129... | collective-permute-start | bytes 221192 | tf_op jit(solution)/shard_map/ppermute | solution.py:40
  50.1 2.0 %collective-permute-start.5 = (bf16[2,256,256]{2,1,0:T(8,128)(2,1)S(1)}, bf16[2,256,256]{2,1,0:T(8,128)(2,1)S(1)}, u32[]{:S(2)}, u32[]{:S(2)}) collective-permute-start(bf16[2,256,256]{2,1,0:T(8,128)(2,1)S(1)} %get-tuple-element.15), channel_id=1, source_target_pairs={{128,0},{0,128},{384,256},{256,384},{129,1},{1,129},{385,257},{257... | collective-permute-start | bytes 786440 | tf_op jit(solution)/shard_map/ppermute | solution.py:40
  53.0 5.9 %collective-permute-start.6 = (bf16[64,256]{1,0:T(8,128)(2,1)S(1)}, bf16[64,256]{1,0:T(8,128)(2,1)S(1)}, u32[]{:S(2)}, u32[]{:S(2)}) collective-permute-start(bf16[64,256]{1,0:T(8,128)(2,1)S(1)} %get-tuple-element.16), channel_id=1, source_target_pairs={{256,0},{384,128},{0,256},{128,384},{257,1},{385,129},{1,257},{129... | collective-permute-start | bytes 98312 | tf_op jit(solution)/shard_map/ppermute | solution.py:40
  59.0 5.4 %all-to-all-start.2 = ((bf16[8,64,256]{2,1,0:T(8,128)(2,1)}), bf16[8,64,256]{2,1,0:T(8,128)(2,1)S(1)}, u32[]{:S(2)}, u32[]{:S(2)}) async-start(bf16[8,64,256]{2,1,0:T(8,128)(2,1)} %get-tuple-element.14), calls=%async_computation.2 | async-start | bytes 524288 | tf_op jit(solution)/shard_map/all_to_all | solution.py:28
  66.5 4.0 %collective-permute-done.7 = bf16[2,64,256]{2,1,0:T(8,128)(2,1)S(1)} collective-permute-done((bf16[2,64,256]{2,1,0:T(8,128)(2,1)S(1)}, bf16[2,64,256]{2,1,0:T(8,128)(2,1)S(1)}, u32[]{:S(2)}, u32[]{:S(2)}) %collective-permute-start.7) | collective-permute-done | bytes 65568 | tf_op jit(solution)/shard_map/ppermute | solution.py:40
  70.6 5.3 %shard_map.76 = (f32[8,136,128]{2,1,0:T(8,128)}, bf16[2,144,256]{2,1,0:T(8,128)(2,1)S(1)}) custom-call(s32[5]{0:T(128)S(1)} %stack.75.refs_0_, bf16[8,64,256]{2,1,0:T(8,128)(2,1)S(1)} %all-to-all-done.2.refs_1_, bf16[4,256,256]{2,1,0:T(8,128)(2,1)S(1)} %pad_maximum_fusion.refs_2_, ...), custom_call_target="tpu_custom_call", output_to_operand_aliasing={{1}: (4, {})} | custom-call | flops 671088640 | bytes 917524 | tf_op jit(solution)/shard_map/pallas_call | solution.py:271
  75.9 4.8 %all-to-all-start.3 = ((f32[8,136,128]{2,1,0:T(8,128)}), f32[8,136,128]{2,1,0:T(8,128)S(1)}, u32[]{:S(2)}, u32[]{:S(2)}) async-start(f32[8,136,128]{2,1,0:T(8,128)} %get-tuple-element.17), calls=%async_computation.3 | async-start | bytes 1114112 | tf_op jit(solution)/shard_map/all_to_all | solution.py:28
  80.7 2.1 %collective-permute-start.10 = (bf16[2,144,256]{2,1,0:T(8,128)(2,1)S(1)}, bf16[2,144,256]{2,1,0:T(8,128)(2,1)S(1)}, u32[]{:S(2)}, u32[]{:S(2)}) collective-permute-start(bf16[2,144,256]{2,1,0:T(8,128)(2,1)S(1)} %get-tuple-element.18), channel_id=1, source_target_pairs={{128,0},{0,128},{384,256},{256,384},{129,1},{1,129},{385,257},{257... | collective-permute-start | bytes 442376 | tf_op jit(solution)/shard_map/ppermute | solution.py:40
  82.8 5.7 %collective-permute-done.10 = bf16[2,144,256]{2,1,0:T(8,128)(2,1)S(1)} collective-permute-done((bf16[2,144,256]{2,1,0:T(8,128)(2,1)S(1)}, bf16[2,144,256]{2,1,0:T(8,128)(2,1)S(1)}, u32[]{:S(2)}, u32[]{:S(2)}) %collective-permute-start.10) | collective-permute-done | bytes 147488 | tf_op jit(solution)/shard_map/ppermute | solution.py:40
  90.5 5.6 %all-to-all-start.4 = ((bf16[4,4,144,256]{3,2,1,0:T(8,128)(2,1)}), bf16[4,4,144,256]{3,2,1,0:T(8,128)(2,1)S(1)}, u32[]{:S(2)}, u32[]{:S(2)}) async-start(bf16[4,4,144,256]{3,2,1,0:T(8,128)(2,1)} %get-tuple-element.20), calls=%async_computation.4 | async-start | bytes 2359296 | tf_op jit(solution)/shard_map/all_to_all | solution.py:28
  96.1 12.4 %collective-permute-start.13 = (bf16[64,256]{1,0:T(8,128)(2,1)S(1)}, bf16[64,256]{1,0:T(8,128)(2,1)S(1)}, u32[]{:S(2)}, u32[]{:S(2)}) collective-permute-start(bf16[64,256]{1,0:T(8,128)(2,1)S(1)} %get-tuple-element.19), channel_id=1, source_target_pairs={{8,0},{12,4},{0,8},{4,12},{9,1},{13,5},{1,9},{5,13},{10,2},{14,6},... | collective-permute-start | bytes 98312 | tf_op jit(solution)/shard_map/ppermute | solution.py:36
  108.5 5.9 %collective-permute-start.12 = (bf16[64,256]{1,0:T(8,128)(2,1)S(1)}, bf16[64,256]{1,0:T(8,128)(2,1)S(1)}, u32[]{:S(2)}, u32[]{:S(2)}) collective-permute-start(bf16[64,256]{1,0:T(8,128)(2,1)S(1)} %get-tuple-element.19), channel_id=1, source_target_pairs={{12,0},{0,4},{4,8},{8,12},{13,1},{1,5},{5,9},{9,13},{14,2},{2,6},{... | collective-permute-start | bytes 98312 | tf_op jit(solution)/shard_map/ppermute | solution.py:36
  114.3 3.9 %collective-permute-start.11 = (bf16[64,256]{1,0:T(8,128)(2,1)S(1)}, bf16[64,256]{1,0:T(8,128)(2,1)S(1)}, u32[]{:S(2)}, u32[]{:S(2)}) collective-permute-start(bf16[64,256]{1,0:T(8,128)(2,1)S(1)} %get-tuple-element.19), channel_id=1, source_target_pairs={{4,0},{8,4},{12,8},{0,12},{5,1},{9,5},{13,9},{1,13},{6,2},{10,6},{... | collective-permute-start | bytes 98312 | tf_op jit(solution)/shard_map/ppermute | solution.py:36
  118.6 6.2 %collective-permute-done.11 = bf16[64,256]{1,0:T(8,128)(2,1)S(1)} collective-permute-done((bf16[64,256]{1,0:T(8,128)(2,1)S(1)}, bf16[64,256]{1,0:T(8,128)(2,1)S(1)}, u32[]{:S(2)}, u32[]{:S(2)}) %collective-permute-start.11) | collective-permute-done | bytes 32800 | tf_op jit(solution)/shard_map/ppermute | solution.py:36
  129.9 4.4 %all-to-all-start.5 = ((f32[8,72,128]{2,1,0:T(8,128)}), f32[8,72,128]{2,1,0:T(8,128)S(1)}, u32[]{:S(2)}, u32[]{:S(2)}) async-start(f32[8,72,128]{2,1,0:T(8,128)} %shard_map.78), calls=%async_computation.5 | async-start | bytes 589824 | tf_op jit(solution)/shard_map/all_to_all | solution.py:28
  135.2 7.0 %all-to-all-done.5.refs_0_ = f32[8,72,128]{2,1,0:T(8,128)S(1)} async-done(((f32[8,72,128]{2,1,0:T(8,128)}), f32[8,72,128]{2,1,0:T(8,128)S(1)}, u32[]{:S(2)}, u32[]{:S(2)}) %all-to-all-start.5) | async-done | bytes 294944 | tf_op jit(solution)/shard_map/all_to_all | solution.py:28
  (53 shorter events, 19.8 us)
Async XLA Ops:
  4.7 11.3 %copy-start.2 = (bf16[256,128]{1,0:T(8,128)(2,1)S(1)}, bf16[256,128]{1,0:T(8,128)(2,1)}, u32[]{:S(2)}) copy-start(bf16[256,128]{1,0:T(8,128)(2,1)} %param.11) | copy-start | bytes 196612
  4.7 11.4 %copy-start.3 = (bf16[256,128]{1,0:T(8,128)(2,1)S(1)}, bf16[256,128]{1,0:T(8,128)(2,1)}, u32[]{:S(2)}) copy-start(bf16[256,128]{1,0:T(8,128)(2,1)} %param.12) | copy-start | bytes 196612
  4.7 23.5 %copy-start.4 = (bf16[256,144]{0,1:T(8,128)(2,1)S(1)}, bf16[256,144]{0,1:T(8,128)(2,1)}, u32[]{:S(2)}) copy-start(bf16[256,144]{0,1:T(8,128)(2,1)} %param.10) | copy-start | bytes 221188
  4.7 31.6 %all-to-all-start = ((bf16[8,64,1152]{2,1,0:T(8,128)(2,1)}), bf16[8,64,1152]{2,1,0:T(8,128)(2,1)S(1)}, u32[]{:S(2)}, u32[]{:S(2)}) async-start(bf16[8,64,1152]{2,1,0:T(8,128)(2,1)} %shard_map.73), calls=%async_computation | async-start | bytes 2359296 | tf_op jit(solution)/shard_map/all_to_all | solution.py:28
  14.0 4.1 %collective-permute-start = (bf16[144,256]{1,0:T(8,128)(2,1)S(1)}, bf16[144,256]{1,0:T(8,128)(2,1)S(1)}, u32[]{:S(2)}, u32[]{:S(2)}) collective-permute-start(bf16[144,256]{1,0:T(8,128)(2,1)S(1)} %get-tuple-element.22), channel_id=1, source_target_pairs={{0,16},{16,0},{1,17},{17,1},{2,18},{18,2},{3,19},{19,3},{4,20},{20... | collective-permute-start | bytes 221192 | tf_op jit(solution)/shard_map/ppermute | solution.py:21
  16.1 12.8 %collective-permute-start.4 = (bf16[256,256]{1,0:T(8,128)(2,1)S(1)}, bf16[256,256]{1,0:T(8,128)(2,1)S(1)}, u32[]{:S(2)}, u32[]{:S(2)}) collective-permute-start(bf16[256,256]{1,0:T(8,128)(2,1)S(1)} %constant_dynamic-update-slice_fusion), channel_id=1, source_target_pairs={{256,0},{384,128},{0,256},{128,384},{257,1},{385,129},{1,257},{129... | collective-permute-start | bytes 393224 | tf_op jit(solution)/shard_map/ppermute | solution.py:40
  18.1 12.4 %collective-permute-start.1 = (bf16[2,144,256]{2,1,0:T(8,128)(2,1)S(1)}, bf16[2,144,256]{2,1,0:T(8,128)(2,1)S(1)}, u32[]{:S(2)}, u32[]{:S(2)}) collective-permute-start(bf16[2,144,256]{2,1,0:T(8,128)(2,1)S(1)} %maximum_select_fusion.refs_1_), channel_id=1, source_target_pairs={{128,0},{0,128},{384,256},{256,384},{129,1},{1,129},{385,257},{257... | collective-permute-start | bytes 442376 | tf_op jit(solution)/shard_map/ppermute | solution.py:40
  20.8 15.5 %collective-permute-start.2 = (bf16[2,144,256]{2,1,0:T(8,128)(2,1)S(1)}, bf16[2,144,256]{2,1,0:T(8,128)(2,1)S(1)}, u32[]{:S(2)}, u32[]{:S(2)}) collective-permute-start(bf16[2,144,256]{2,1,0:T(8,128)(2,1)S(1)} %maximum_select_fusion.refs_1_), channel_id=1, source_target_pairs={{256,0},{384,128},{0,256},{128,384},{257,1},{385,129},{1,257},{129... | collective-permute-start | bytes 442376 | tf_op jit(solution)/shard_map/ppermute | solution.py:40
  24.8 11.5 %collective-permute-start.3 = (bf16[2,144,256]{2,1,0:T(8,128)(2,1)S(1)}, bf16[2,144,256]{2,1,0:T(8,128)(2,1)S(1)}, u32[]{:S(2)}, u32[]{:S(2)}) collective-permute-start(bf16[2,144,256]{2,1,0:T(8,128)(2,1)S(1)} %maximum_select_fusion.refs_1_), channel_id=1, source_target_pairs={{384,0},{256,128},{128,256},{0,384},{385,1},{257,129},{129,257},{1... | collective-permute-start | bytes 442376 | tf_op jit(solution)/shard_map/ppermute | solution.py:40
  28.2 14.4 %collective-permute-start.8 = (bf16[144,256]{1,0:T(8,128)(2,1)S(1)}, bf16[144,256]{1,0:T(8,128)(2,1)S(1)}, u32[]{:S(2)}, u32[]{:S(2)}) collective-permute-start(bf16[144,256]{1,0:T(8,128)(2,1)S(1)} %bitcast.33), channel_id=1, source_target_pairs={{0,0},{4,128},{8,256},{12,384},{128,4},{132,132},{136,260},{140,38... | collective-permute-start | bytes 221192 | tf_op jit(solution)/shard_map/ppermute | solution.py:313
  37.6 14.6 %all-to-all-start.1 = ((f32[8,64,256]{2,1,0:T(8,128)}), f32[8,64,256]{2,1,0:T(8,128)S(1)}, u32[]{:S(2)}, u32[]{:S(2)}) async-start(f32[8,64,256]{2,1,0:T(8,128)} %get-tuple-element.13), calls=%async_computation.1 | async-start | bytes 1048576 | tf_op jit(solution)/shard_map/all_to_all | solution.py:28
  42.7 16.2 %collective-permute-start.9 = (bf16[144,256]{1,0:T(8,128)(2,1)S(1)}, bf16[144,256]{1,0:T(8,128)(2,1)S(1)}, u32[]{:S(2)}, u32[]{:S(2)}) collective-permute-start(bf16[144,256]{1,0:T(8,128)(2,1)S(1)} %collective-permute-done.8), channel_id=1, source_target_pairs={{256,0},{384,128},{0,256},{128,384},{257,1},{385,129},{1,257},{129... | collective-permute-start | bytes 221192 | tf_op jit(solution)/shard_map/ppermute | solution.py:40
  50.1 16.4 %collective-permute-start.5 = (bf16[2,256,256]{2,1,0:T(8,128)(2,1)S(1)}, bf16[2,256,256]{2,1,0:T(8,128)(2,1)S(1)}, u32[]{:S(2)}, u32[]{:S(2)}) collective-permute-start(bf16[2,256,256]{2,1,0:T(8,128)(2,1)S(1)} %get-tuple-element.15), channel_id=1, source_target_pairs={{128,0},{0,128},{384,256},{256,384},{129,1},{1,129},{385,257},{257... | collective-permute-start | bytes 786440 | tf_op jit(solution)/shard_map/ppermute | solution.py:40
  53.0 11.3 %collective-permute-start.6 = (bf16[64,256]{1,0:T(8,128)(2,1)S(1)}, bf16[64,256]{1,0:T(8,128)(2,1)S(1)}, u32[]{:S(2)}, u32[]{:S(2)}) collective-permute-start(bf16[64,256]{1,0:T(8,128)(2,1)S(1)} %get-tuple-element.16), channel_id=1, source_target_pairs={{256,0},{384,128},{0,256},{128,384},{257,1},{385,129},{1,257},{129... | collective-permute-start | bytes 98312 | tf_op jit(solution)/shard_map/ppermute | solution.py:40
  59.0 11.6 %all-to-all-start.2 = ((bf16[8,64,256]{2,1,0:T(8,128)(2,1)}), bf16[8,64,256]{2,1,0:T(8,128)(2,1)S(1)}, u32[]{:S(2)}, u32[]{:S(2)}) async-start(bf16[8,64,256]{2,1,0:T(8,128)(2,1)} %get-tuple-element.14), calls=%async_computation.2 | async-start | bytes 524288 | tf_op jit(solution)/shard_map/all_to_all | solution.py:28
  64.4 6.2 %collective-permute-start.7 = (bf16[2,64,256]{2,1,0:T(8,128)(2,1)S(1)}, bf16[2,64,256]{2,1,0:T(8,128)(2,1)S(1)}, u32[]{:S(2)}, u32[]{:S(2)}) collective-permute-start(bf16[2,64,256]{2,1,0:T(8,128)(2,1)S(1)} %pad_maximum_fusion.6), channel_id=1, source_target_pairs={{128,0},{0,128},{384,256},{256,384},{129,1},{1,129},{385,257},{257... | collective-permute-start | bytes 196616 | tf_op jit(solution)/shard_map/ppermute | solution.py:40
  75.9 13.4 %all-to-all-start.3 = ((f32[8,136,128]{2,1,0:T(8,128)}), f32[8,136,128]{2,1,0:T(8,128)S(1)}, u32[]{:S(2)}, u32[]{:S(2)}) async-start(f32[8,136,128]{2,1,0:T(8,128)} %get-tuple-element.17), calls=%async_computation.3 | async-start | bytes 1114112 | tf_op jit(solution)/shard_map/all_to_all | solution.py:28
  80.7 7.8 %collective-permute-start.10 = (bf16[2,144,256]{2,1,0:T(8,128)(2,1)S(1)}, bf16[2,144,256]{2,1,0:T(8,128)(2,1)S(1)}, u32[]{:S(2)}, u32[]{:S(2)}) collective-permute-start(bf16[2,144,256]{2,1,0:T(8,128)(2,1)S(1)} %get-tuple-element.18), channel_id=1, source_target_pairs={{128,0},{0,128},{384,256},{256,384},{129,1},{1,129},{385,257},{257... | collective-permute-start | bytes 442376 | tf_op jit(solution)/shard_map/ppermute | solution.py:40
  90.5 37.5 %all-to-all-start.4 = ((bf16[4,4,144,256]{3,2,1,0:T(8,128)(2,1)}), bf16[4,4,144,256]{3,2,1,0:T(8,128)(2,1)S(1)}, u32[]{:S(2)}, u32[]{:S(2)}) async-start(bf16[4,4,144,256]{3,2,1,0:T(8,128)(2,1)} %get-tuple-element.20), calls=%async_computation.4 | async-start | bytes 2359296 | tf_op jit(solution)/shard_map/all_to_all | solution.py:28
  96.1 22.1 %collective-permute-start.13 = (bf16[64,256]{1,0:T(8,128)(2,1)S(1)}, bf16[64,256]{1,0:T(8,128)(2,1)S(1)}, u32[]{:S(2)}, u32[]{:S(2)}) collective-permute-start(bf16[64,256]{1,0:T(8,128)(2,1)S(1)} %get-tuple-element.19), channel_id=1, source_target_pairs={{8,0},{12,4},{0,8},{4,12},{9,1},{13,5},{1,9},{5,13},{10,2},{14,6},... | collective-permute-start | bytes 98312 | tf_op jit(solution)/shard_map/ppermute | solution.py:36
  108.5 10.1 %collective-permute-start.12 = (bf16[64,256]{1,0:T(8,128)(2,1)S(1)}, bf16[64,256]{1,0:T(8,128)(2,1)S(1)}, u32[]{:S(2)}, u32[]{:S(2)}) collective-permute-start(bf16[64,256]{1,0:T(8,128)(2,1)S(1)} %get-tuple-element.19), channel_id=1, source_target_pairs={{12,0},{0,4},{4,8},{8,12},{13,1},{1,5},{5,9},{9,13},{14,2},{2,6},{... | collective-permute-start | bytes 98312 | tf_op jit(solution)/shard_map/ppermute | solution.py:36
  114.3 10.5 %collective-permute-start.11 = (bf16[64,256]{1,0:T(8,128)(2,1)S(1)}, bf16[64,256]{1,0:T(8,128)(2,1)S(1)}, u32[]{:S(2)}, u32[]{:S(2)}) collective-permute-start(bf16[64,256]{1,0:T(8,128)(2,1)S(1)} %get-tuple-element.19), channel_id=1, source_target_pairs={{4,0},{8,4},{12,8},{0,12},{5,1},{9,5},{13,9},{1,13},{6,2},{10,6},{... | collective-permute-start | bytes 98312 | tf_op jit(solution)/shard_map/ppermute | solution.py:36
  124.8 3.2 %collective-permute-start.14 = (bf16[4,64,256]{2,1,0:T(8,128)(2,1)S(1)}, bf16[4,64,256]{2,1,0:T(8,128)(2,1)S(1)}, u32[]{:S(2)}, u32[]{:S(2)}) collective-permute-start(bf16[4,64,256]{2,1,0:T(8,128)(2,1)S(1)} %pad_maximum_fusion.5.refs_1_), channel_id=1, source_target_pairs={{0,16},{16,0},{1,17},{17,1},{2,18},{18,2},{3,19},{19,3},{4,20},{20... | collective-permute-start | bytes 393224 | tf_op jit(solution)/shard_map/ppermute | solution.py:21
  129.9 12.2 %all-to-all-start.5 = ((f32[8,72,128]{2,1,0:T(8,128)}), f32[8,72,128]{2,1,0:T(8,128)S(1)}, u32[]{:S(2)}, u32[]{:S(2)}) async-start(f32[8,72,128]{2,1,0:T(8,128)} %shard_map.78), calls=%async_computation.5 | async-start | bytes 589824 | tf_op jit(solution)/shard_map/all_to_all | solution.py:28
  (2 other events, 10.3 us)

commit v10 on v9

--- a/solution.py
+++ b/solution.py
@@ -232,17 +232,18 @@
     steps = [lax.rem((z ^ k) + NW - w, NW) for k in PAIRS]
     places = [jnp.where(step < 2, step, 5 - step) for step in steps]
     att = [jnp.concatenate([att_ref[at], other_ref[at]], axis=0) for at in places]
+    columns = weight_ref.shape[2]
+    total = 0.0
+    for k in range(NW):
+        total = total + lax.dot_general(
+            weight_ref[:, k].reshape(NX * columns, weight_ref.shape[3]),
+            att[k],
+            (((1,), (1,)), ((), ())),
+            preferred_element_type=jnp.float32,
+        )
     for x in range(NX):
-        total = 0.0
-        for k in range(NW):
-            total = total + lax.dot_general(
-                weight_ref[x, k],
-                att[k],
-                (((1,), (1,)), ((), ())),
-                preferred_element_type=jnp.float32,
-            )
         for i, core in enumerate((c, 1 - c)):
-            part = total[:, i * rows : (i + 1) * rows]
+            part = total[x * columns : (x + 1) * columns, i * rows : (i + 1) * rows]
             out_ref[x * NC + core] = jnp.concatenate([part[:half], part[half:]], axis=1)
 
 

time: 144 us -> 144 us (level)
  no operation moved by 1% of the time
where the time goes in v10:
time: 144 us; the launch traced here: 143 us
  starting transfers between devices  92.4 us (64%)
  waiting for transfers between devices  32.8 us (23%)
  Pallas kernels  13.4 us (9%)
  local copies, waits for them, and re-layouts  2.86 us (2%)
    all_to_all x6, starting transfers between devices, exchange(): return lax.all_to_all(x, axis, 0, 0, tiled=True)  34.2 us
    ppermute x9, starting transfers between devices, from_pair(): return lax.ppermute(x, axis, [(i ^ bit, i) for i in range(size)])  31.4 us
    ppermute x3, starting transfers between devices, from_next(): return lax.ppermute(x, axis, [((i + step) % size, i) for i in range(size)])  22.1 us
    ppermute x9, waiting for transfers between devices, from_pair(): return lax.ppermute(x, axis, [(i ^ bit, i) for i in range(size)])  17.1 us
    pallas_call x7, Pallas kernels, call(): pl.pallas_call(body, out_shape=shapes, in_specs=specs + [pl.BlockSpec(mem...  13.4 us
    all_to_all x6, waiting for transfers between devices, exchange(): return lax.all_to_all(x, axis, 0, 0, tiled=True)  7.78 us
    ppermute x3, waiting for transfers between devices, from_next(): return lax.ppermute(x, axis, [((i + step) % size, i) for i in range(size)])  6.55 us
    ppermute x2, starting transfers between devices, swap_core(): return lax.ppermute(x, 'c', [(0, 1), (1, 0)])  3.98 us
  transfers between devices with their start and end apart: 21, of which 9 were waited for; matrix products, arithmetic and copies ran while one was open for 1% of the time, Pallas kernels for 1%

profile of v10, /device:TPU:24, one launch (start us, length us, event | category | flops | bytes accessed | tf_op | source)
XLA Modules:
  0.0 142.9 jit_solution(5574357384163397947)
XLA Ops:
  2.6 2.1 %shard_map.73 = bf16[8,64,1152]{2,1,0:T(8,128)(2,1)} custom-call(s32[5]{0:T(128)S(1)} %stack.75.refs_0_, bf16[64,4608]{1,0:T(8,128)(2,1)S(1)} %copy-done, f32[1,4608]{1,0:T(1,128)S(1)} %reshape.14.refs_2_), custom_call_target="tpu_custom_call" | custom-call | flops 1769472 | bytes 608276 | tf_op jit(solution)/shard_map/pallas_call | solution.py:272
  4.7 9.2 %all-to-all-start = ((bf16[8,64,1152]{2,1,0:T(8,128)(2,1)}), bf16[8,64,1152]{2,1,0:T(8,128)(2,1)S(1)}, u32[]{:S(2)}, u32[]{:S(2)}) async-start(bf16[8,64,1152]{2,1,0:T(8,128)(2,1)} %shard_map.73), calls=%async_computation | async-start | bytes 2359296 | tf_op jit(solution)/shard_map/all_to_all | solution.py:28
  14.0 2.1 %collective-permute-start = (bf16[144,256]{1,0:T(8,128)(2,1)S(1)}, bf16[144,256]{1,0:T(8,128)(2,1)S(1)}, u32[]{:S(2)}, u32[]{:S(2)}) collective-permute-start(bf16[144,256]{1,0:T(8,128)(2,1)S(1)} %get-tuple-element.22), channel_id=1, source_target_pairs={{0,16},{16,0},{1,17},{17,1},{2,18},{18,2},{3,19},{19,3},{4,20},{20... | collective-permute-start | bytes 221192 | tf_op jit(solution)/shard_map/ppermute | solution.py:21
  18.1 2.7 %collective-permute-start.1 = (bf16[2,144,256]{2,1,0:T(8,128)(2,1)S(1)}, bf16[2,144,256]{2,1,0:T(8,128)(2,1)S(1)}, u32[]{:S(2)}, u32[]{:S(2)}) collective-permute-start(bf16[2,144,256]{2,1,0:T(8,128)(2,1)S(1)} %maximum_select_fusion.refs_1_), channel_id=1, source_target_pairs={{128,0},{0,128},{384,256},{256,384},{129,1},{1,129},{385,257},{257... | collective-permute-start | bytes 442376 | tf_op jit(solution)/shard_map/ppermute | solution.py:40
  20.8 4.1 %collective-permute-start.2 = (bf16[2,144,256]{2,1,0:T(8,128)(2,1)S(1)}, bf16[2,144,256]{2,1,0:T(8,128)(2,1)S(1)}, u32[]{:S(2)}, u32[]{:S(2)}) collective-permute-start(bf16[2,144,256]{2,1,0:T(8,128)(2,1)S(1)} %maximum_select_fusion.refs_1_), channel_id=1, source_target_pairs={{256,0},{384,128},{0,256},{128,384},{257,1},{385,129},{1,257},{129... | collective-permute-start | bytes 442376 | tf_op jit(solution)/shard_map/ppermute | solution.py:40
  24.8 3.4 %collective-permute-start.3 = (bf16[2,144,256]{2,1,0:T(8,128)(2,1)S(1)}, bf16[2,144,256]{2,1,0:T(8,128)(2,1)S(1)}, u32[]{:S(2)}, u32[]{:S(2)}) collective-permute-start(bf16[2,144,256]{2,1,0:T(8,128)(2,1)S(1)} %maximum_select_fusion.refs_1_), channel_id=1, source_target_pairs={{384,0},{256,128},{128,256},{0,384},{385,1},{257,129},{129,257},{1... | collective-permute-start | bytes 442376 | tf_op jit(solution)/shard_map/ppermute | solution.py:40
  30.5 5.8 %collective-permute-done.2.refs_3_ = bf16[2,144,256]{2,1,0:T(8,128)(2,1)S(1)} collective-permute-done((bf16[2,144,256]{2,1,0:T(8,128)(2,1)S(1)}, bf16[2,144,256]{2,1,0:T(8,128)(2,1)S(1)}, u32[]{:S(2)}, u32[]{:S(2)}) %collective-permute-start.2) | collective-permute-done | bytes 147488 | tf_op jit(solution)/shard_map/ppermute | solution.py:40
  37.6 4.8 %all-to-all-start.1 = ((f32[8,64,256]{2,1,0:T(8,128)}), f32[8,64,256]{2,1,0:T(8,128)S(1)}, u32[]{:S(2)}, u32[]{:S(2)}) async-start(f32[8,64,256]{2,1,0:T(8,128)} %get-tuple-element.13), calls=%async_computation.1 | async-start | bytes 1048576 | tf_op jit(solution)/shard_map/all_to_all | solution.py:28
  42.7 7.4 %collective-permute-start.9 = (bf16[144,256]{1,0:T(8,128)(2,1)S(1)}, bf16[144,256]{1,0:T(8,128)(2,1)S(1)}, u32[]{:S(2)}, u32[]{:S(2)}) collective-permute-start(bf16[144,256]{1,0:T(8,128)(2,1)S(1)} %collective-permute-done.8), channel_id=1, source_target_pairs={{256,0},{384,128},{0,256},{128,384},{257,1},{385,129},{1,257},{129... | collective-permute-start | bytes 221192 | tf_op jit(solution)/shard_map/ppermute | solution.py:40
  50.1 2.0 %collective-permute-start.5 = (bf16[2,256,256]{2,1,0:T(8,128)(2,1)S(1)}, bf16[2,256,256]{2,1,0:T(8,128)(2,1)S(1)}, u32[]{:S(2)}, u32[]{:S(2)}) collective-permute-start(bf16[2,256,256]{2,1,0:T(8,128)(2,1)S(1)} %get-tuple-element.15), channel_id=1, source_target_pairs={{128,0},{0,128},{384,256},{256,384},{129,1},{1,129},{385,257},{257... | collective-permute-start | bytes 786440 | tf_op jit(solution)/shard_map/ppermute | solution.py:40
  53.0 5.9 %collective-permute-start.6 = (bf16[64,256]{1,0:T(8,128)(2,1)S(1)}, bf16[64,256]{1,0:T(8,128)(2,1)S(1)}, u32[]{:S(2)}, u32[]{:S(2)}) collective-permute-start(bf16[64,256]{1,0:T(8,128)(2,1)S(1)} %get-tuple-element.16), channel_id=1, source_target_pairs={{256,0},{384,128},{0,256},{128,384},{257,1},{385,129},{1,257},{129... | collective-permute-start | bytes 98312 | tf_op jit(solution)/shard_map/ppermute | solution.py:40
  59.0 5.4 %all-to-all-start.2 = ((bf16[8,64,256]{2,1,0:T(8,128)(2,1)}), bf16[8,64,256]{2,1,0:T(8,128)(2,1)S(1)}, u32[]{:S(2)}, u32[]{:S(2)}) async-start(bf16[8,64,256]{2,1,0:T(8,128)(2,1)} %get-tuple-element.14), calls=%async_computation.2 | async-start | bytes 524288 | tf_op jit(solution)/shard_map/all_to_all | solution.py:28
  66.5 4.0 %collective-permute-done.7 = bf16[2,64,256]{2,1,0:T(8,128)(2,1)S(1)} collective-permute-done((bf16[2,64,256]{2,1,0:T(8,128)(2,1)S(1)}, bf16[2,64,256]{2,1,0:T(8,128)(2,1)S(1)}, u32[]{:S(2)}, u32[]{:S(2)}) %collective-permute-start.7) | collective-permute-done | bytes 65568 | tf_op jit(solution)/shard_map/ppermute | solution.py:40
  70.6 5.3 %shard_map.76 = (f32[8,136,128]{2,1,0:T(8,128)}, bf16[2,144,256]{2,1,0:T(8,128)(2,1)S(1)}) custom-call(s32[5]{0:T(128)S(1)} %stack.75.refs_0_, bf16[8,64,256]{2,1,0:T(8,128)(2,1)S(1)} %all-to-all-done.2.refs_1_, bf16[4,256,256]{2,1,0:T(8,128)(2,1)S(1)} %pad_maximum_fusion.refs_2_, ...), custom_call_target="tpu_custom_call", output_to_operand_aliasing={{1}: (4, {})} | custom-call | flops 671088640 | bytes 917524 | tf_op jit(solution)/shard_map/pallas_call | solution.py:272
  75.9 4.8 %all-to-all-start.3 = ((f32[8,136,128]{2,1,0:T(8,128)}), f32[8,136,128]{2,1,0:T(8,128)S(1)}, u32[]{:S(2)}, u32[]{:S(2)}) async-start(f32[8,136,128]{2,1,0:T(8,128)} %get-tuple-element.17), calls=%async_computation.3 | async-start | bytes 1114112 | tf_op jit(solution)/shard_map/all_to_all | solution.py:28
  80.7 2.1 %collective-permute-start.10 = (bf16[2,144,256]{2,1,0:T(8,128)(2,1)S(1)}, bf16[2,144,256]{2,1,0:T(8,128)(2,1)S(1)}, u32[]{:S(2)}, u32[]{:S(2)}) collective-permute-start(bf16[2,144,256]{2,1,0:T(8,128)(2,1)S(1)} %get-tuple-element.18), channel_id=1, source_target_pairs={{128,0},{0,128},{384,256},{256,384},{129,1},{1,129},{385,257},{257... | collective-permute-start | bytes 442376 | tf_op jit(solution)/shard_map/ppermute | solution.py:40
  82.8 5.7 %collective-permute-done.10 = bf16[2,144,256]{2,1,0:T(8,128)(2,1)S(1)} collective-permute-done((bf16[2,144,256]{2,1,0:T(8,128)(2,1)S(1)}, bf16[2,144,256]{2,1,0:T(8,128)(2,1)S(1)}, u32[]{:S(2)}, u32[]{:S(2)}) %collective-permute-start.10) | collective-permute-done | bytes 147488 | tf_op jit(solution)/shard_map/ppermute | solution.py:40
  90.5 5.6 %all-to-all-start.4 = ((bf16[4,4,144,256]{3,2,1,0:T(8,128)(2,1)}), bf16[4,4,144,256]{3,2,1,0:T(8,128)(2,1)S(1)}, u32[]{:S(2)}, u32[]{:S(2)}) async-start(bf16[4,4,144,256]{3,2,1,0:T(8,128)(2,1)} %get-tuple-element.20), calls=%async_computation.4 | async-start | bytes 2359296 | tf_op jit(solution)/shard_map/all_to_all | solution.py:28
  96.1 12.4 %collective-permute-start.13 = (bf16[64,256]{1,0:T(8,128)(2,1)S(1)}, bf16[64,256]{1,0:T(8,128)(2,1)S(1)}, u32[]{:S(2)}, u32[]{:S(2)}) collective-permute-start(bf16[64,256]{1,0:T(8,128)(2,1)S(1)} %get-tuple-element.19), channel_id=1, source_target_pairs={{8,0},{12,4},{0,8},{4,12},{9,1},{13,5},{1,9},{5,13},{10,2},{14,6},... | collective-permute-start | bytes 98312 | tf_op jit(solution)/shard_map/ppermute | solution.py:36
  108.5 5.9 %collective-permute-start.12 = (bf16[64,256]{1,0:T(8,128)(2,1)S(1)}, bf16[64,256]{1,0:T(8,128)(2,1)S(1)}, u32[]{:S(2)}, u32[]{:S(2)}) collective-permute-start(bf16[64,256]{1,0:T(8,128)(2,1)S(1)} %get-tuple-element.19), channel_id=1, source_target_pairs={{12,0},{0,4},{4,8},{8,12},{13,1},{1,5},{5,9},{9,13},{14,2},{2,6},{... | collective-permute-start | bytes 98312 | tf_op jit(solution)/shard_map/ppermute | solution.py:36
  114.3 3.9 %collective-permute-start.11 = (bf16[64,256]{1,0:T(8,128)(2,1)S(1)}, bf16[64,256]{1,0:T(8,128)(2,1)S(1)}, u32[]{:S(2)}, u32[]{:S(2)}) collective-permute-start(bf16[64,256]{1,0:T(8,128)(2,1)S(1)} %get-tuple-element.19), channel_id=1, source_target_pairs={{4,0},{8,4},{12,8},{0,12},{5,1},{9,5},{13,9},{1,13},{6,2},{10,6},{... | collective-permute-start | bytes 98312 | tf_op jit(solution)/shard_map/ppermute | solution.py:36
  118.6 6.2 %collective-permute-done.11 = bf16[64,256]{1,0:T(8,128)(2,1)S(1)} collective-permute-done((bf16[64,256]{1,0:T(8,128)(2,1)S(1)}, bf16[64,256]{1,0:T(8,128)(2,1)S(1)}, u32[]{:S(2)}, u32[]{:S(2)}) %collective-permute-start.11) | collective-permute-done | bytes 32800 | tf_op jit(solution)/shard_map/ppermute | solution.py:36
  129.9 4.4 %all-to-all-start.5 = ((f32[8,72,128]{2,1,0:T(8,128)}), f32[8,72,128]{2,1,0:T(8,128)S(1)}, u32[]{:S(2)}, u32[]{:S(2)}) async-start(f32[8,72,128]{2,1,0:T(8,128)} %shard_map.78), calls=%async_computation.5 | async-start | bytes 589824 | tf_op jit(solution)/shard_map/all_to_all | solution.py:28
  135.2 7.0 %all-to-all-done.5.refs_0_ = f32[8,72,128]{2,1,0:T(8,128)S(1)} async-done(((f32[8,72,128]{2,1,0:T(8,128)}), f32[8,72,128]{2,1,0:T(8,128)S(1)}, u32[]{:S(2)}, u32[]{:S(2)}) %all-to-all-start.5) | async-done | bytes 294944 | tf_op jit(solution)/shard_map/all_to_all | solution.py:28
  (53 shorter events, 19.8 us)
Async XLA Ops:
  4.7 11.3 %copy-start.2 = (bf16[256,128]{1,0:T(8,128)(2,1)S(1)}, bf16[256,128]{1,0:T(8,128)(2,1)}, u32[]{:S(2)}) copy-start(bf16[256,128]{1,0:T(8,128)(2,1)} %param.11) | copy-start | bytes 196612
  4.7 11.4 %copy-start.3 = (bf16[256,128]{1,0:T(8,128)(2,1)S(1)}, bf16[256,128]{1,0:T(8,128)(2,1)}, u32[]{:S(2)}) copy-start(bf16[256,128]{1,0:T(8,128)(2,1)} %param.12) | copy-start | bytes 196612
  4.7 23.5 %copy-start.4 = (bf16[256,144]{0,1:T(8,128)(2,1)S(1)}, bf16[256,144]{0,1:T(8,128)(2,1)}, u32[]{:S(2)}) copy-start(bf16[256,144]{0,1:T(8,128)(2,1)} %param.10) | copy-start | bytes 221188
  4.7 31.6 %all-to-all-start = ((bf16[8,64,1152]{2,1,0:T(8,128)(2,1)}), bf16[8,64,1152]{2,1,0:T(8,128)(2,1)S(1)}, u32[]{:S(2)}, u32[]{:S(2)}) async-start(bf16[8,64,1152]{2,1,0:T(8,128)(2,1)} %shard_map.73), calls=%async_computation | async-start | bytes 2359296 | tf_op jit(solution)/shard_map/all_to_all | solution.py:28
  14.0 4.1 %collective-permute-start = (bf16[144,256]{1,0:T(8,128)(2,1)S(1)}, bf16[144,256]{1,0:T(8,128)(2,1)S(1)}, u32[]{:S(2)}, u32[]{:S(2)}) collective-permute-start(bf16[144,256]{1,0:T(8,128)(2,1)S(1)} %get-tuple-element.22), channel_id=1, source_target_pairs={{0,16},{16,0},{1,17},{17,1},{2,18},{18,2},{3,19},{19,3},{4,20},{20... | collective-permute-start | bytes 221192 | tf_op jit(solution)/shard_map/ppermute | solution.py:21
  16.1 12.8 %collective-permute-start.4 = (bf16[256,256]{1,0:T(8,128)(2,1)S(1)}, bf16[256,256]{1,0:T(8,128)(2,1)S(1)}, u32[]{:S(2)}, u32[]{:S(2)}) collective-permute-start(bf16[256,256]{1,0:T(8,128)(2,1)S(1)} %constant_dynamic-update-slice_fusion), channel_id=1, source_target_pairs={{256,0},{384,128},{0,256},{128,384},{257,1},{385,129},{1,257},{129... | collective-permute-start | bytes 393224 | tf_op jit(solution)/shard_map/ppermute | solution.py:40
  18.1 12.4 %collective-permute-start.1 = (bf16[2,144,256]{2,1,0:T(8,128)(2,1)S(1)}, bf16[2,144,256]{2,1,0:T(8,128)(2,1)S(1)}, u32[]{:S(2)}, u32[]{:S(2)}) collective-permute-start(bf16[2,144,256]{2,1,0:T(8,128)(2,1)S(1)} %maximum_select_fusion.refs_1_), channel_id=1, source_target_pairs={{128,0},{0,128},{384,256},{256,384},{129,1},{1,129},{385,257},{257... | collective-permute-start | bytes 442376 | tf_op jit(solution)/shard_map/ppermute | solution.py:40
  20.8 15.5 %collective-permute-start.2 = (bf16[2,144,256]{2,1,0:T(8,128)(2,1)S(1)}, bf16[2,144,256]{2,1,0:T(8,128)(2,1)S(1)}, u32[]{:S(2)}, u32[]{:S(2)}) collective-permute-start(bf16[2,144,256]{2,1,0:T(8,128)(2,1)S(1)} %maximum_select_fusion.refs_1_), channel_id=1, source_target_pairs={{256,0},{384,128},{0,256},{128,384},{257,1},{385,129},{1,257},{129... | collective-permute-start | bytes 442376 | tf_op jit(solution)/shard_map/ppermute | solution.py:40
  24.8 11.5 %collective-permute-start.3 = (bf16[2,144,256]{2,1,0:T(8,128)(2,1)S(1)}, bf16[2,144,256]{2,1,0:T(8,128)(2,1)S(1)}, u32[]{:S(2)}, u32[]{:S(2)}) collective-permute-start(bf16[2,144,256]{2,1,0:T(8,128)(2,1)S(1)} %maximum_select_fusion.refs_1_), channel_id=1, source_target_pairs={{384,0},{256,128},{128,256},{0,384},{385,1},{257,129},{129,257},{1... | collective-permute-start | bytes 442376 | tf_op jit(solution)/shard_map/ppermute | solution.py:40
  28.2 14.4 %collective-permute-start.8 = (bf16[144,256]{1,0:T(8,128)(2,1)S(1)}, bf16[144,256]{1,0:T(8,128)(2,1)S(1)}, u32[]{:S(2)}, u32[]{:S(2)}) collective-permute-start(bf16[144,256]{1,0:T(8,128)(2,1)S(1)} %bitcast.33), channel_id=1, source_target_pairs={{0,0},{4,128},{8,256},{12,384},{128,4},{132,132},{136,260},{140,38... | collective-permute-start | bytes 221192 | tf_op jit(solution)/shard_map/ppermute | solution.py:314
  37.6 14.6 %all-to-all-start.1 = ((f32[8,64,256]{2,1,0:T(8,128)}), f32[8,64,256]{2,1,0:T(8,128)S(1)}, u32[]{:S(2)}, u32[]{:S(2)}) async-start(f32[8,64,256]{2,1,0:T(8,128)} %get-tuple-element.13), calls=%async_computation.1 | async-start | bytes 1048576 | tf_op jit(solution)/shard_map/all_to_all | solution.py:28
  42.7 16.2 %collective-permute-start.9 = (bf16[144,256]{1,0:T(8,128)(2,1)S(1)}, bf16[144,256]{1,0:T(8,128)(2,1)S(1)}, u32[]{:S(2)}, u32[]{:S(2)}) collective-permute-start(bf16[144,256]{1,0:T(8,128)(2,1)S(1)} %collective-permute-done.8), channel_id=1, source_target_pairs={{256,0},{384,128},{0,256},{128,384},{257,1},{385,129},{1,257},{129... | collective-permute-start | bytes 221192 | tf_op jit(solution)/shard_map/ppermute | solution.py:40
  50.1 16.4 %collective-permute-start.5 = (bf16[2,256,256]{2,1,0:T(8,128)(2,1)S(1)}, bf16[2,256,256]{2,1,0:T(8,128)(2,1)S(1)}, u32[]{:S(2)}, u32[]{:S(2)}) collective-permute-start(bf16[2,256,256]{2,1,0:T(8,128)(2,1)S(1)} %get-tuple-element.15), channel_id=1, source_target_pairs={{128,0},{0,128},{384,256},{256,384},{129,1},{1,129},{385,257},{257... | collective-permute-start | bytes 786440 | tf_op jit(solution)/shard_map/ppermute | solution.py:40
  53.0 11.3 %collective-permute-start.6 = (bf16[64,256]{1,0:T(8,128)(2,1)S(1)}, bf16[64,256]{1,0:T(8,128)(2,1)S(1)}, u32[]{:S(2)}, u32[]{:S(2)}) collective-permute-start(bf16[64,256]{1,0:T(8,128)(2,1)S(1)} %get-tuple-element.16), channel_id=1, source_target_pairs={{256,0},{384,128},{0,256},{128,384},{257,1},{385,129},{1,257},{129... | collective-permute-start | bytes 98312 | tf_op jit(solution)/shard_map/ppermute | solution.py:40
  59.0 11.6 %all-to-all-start.2 = ((bf16[8,64,256]{2,1,0:T(8,128)(2,1)}), bf16[8,64,256]{2,1,0:T(8,128)(2,1)S(1)}, u32[]{:S(2)}, u32[]{:S(2)}) async-start(bf16[8,64,256]{2,1,0:T(8,128)(2,1)} %get-tuple-element.14), calls=%async_computation.2 | async-start | bytes 524288 | tf_op jit(solution)/shard_map/all_to_all | solution.py:28
  64.4 6.2 %collective-permute-start.7 = (bf16[2,64,256]{2,1,0:T(8,128)(2,1)S(1)}, bf16[2,64,256]{2,1,0:T(8,128)(2,1)S(1)}, u32[]{:S(2)}, u32[]{:S(2)}) collective-permute-start(bf16[2,64,256]{2,1,0:T(8,128)(2,1)S(1)} %pad_maximum_fusion.6), channel_id=1, source_target_pairs={{128,0},{0,128},{384,256},{256,384},{129,1},{1,129},{385,257},{257... | collective-permute-start | bytes 196616 | tf_op jit(solution)/shard_map/ppermute | solution.py:40
  75.9 13.4 %all-to-all-start.3 = ((f32[8,136,128]{2,1,0:T(8,128)}), f32[8,136,128]{2,1,0:T(8,128)S(1)}, u32[]{:S(2)}, u32[]{:S(2)}) async-start(f32[8,136,128]{2,1,0:T(8,128)} %get-tuple-element.17), calls=%async_computation.3 | async-start | bytes 1114112 | tf_op jit(solution)/shard_map/all_to_all | solution.py:28
  80.7 7.8 %collective-permute-start.10 = (bf16[2,144,256]{2,1,0:T(8,128)(2,1)S(1)}, bf16[2,144,256]{2,1,0:T(8,128)(2,1)S(1)}, u32[]{:S(2)}, u32[]{:S(2)}) collective-permute-start(bf16[2,144,256]{2,1,0:T(8,128)(2,1)S(1)} %get-tuple-element.18), channel_id=1, source_target_pairs={{128,0},{0,128},{384,256},{256,384},{129,1},{1,129},{385,257},{257... | collective-permute-start | bytes 442376 | tf_op jit(solution)/shard_map/ppermute | solution.py:40
  90.5 37.5 %all-to-all-start.4 = ((bf16[4,4,144,256]{3,2,1,0:T(8,128)(2,1)}), bf16[4,4,144,256]{3,2,1,0:T(8,128)(2,1)S(1)}, u32[]{:S(2)}, u32[]{:S(2)}) async-start(bf16[4,4,144,256]{3,2,1,0:T(8,128)(2,1)} %get-tuple-element.20), calls=%async_computation.4 | async-start | bytes 2359296 | tf_op jit(solution)/shard_map/all_to_all | solution.py:28
  96.1 22.1 %collective-permute-start.13 = (bf16[64,256]{1,0:T(8,128)(2,1)S(1)}, bf16[64,256]{1,0:T(8,128)(2,1)S(1)}, u32[]{:S(2)}, u32[]{:S(2)}) collective-permute-start(bf16[64,256]{1,0:T(8,128)(2,1)S(1)} %get-tuple-element.19), channel_id=1, source_target_pairs={{8,0},{12,4},{0,8},{4,12},{9,1},{13,5},{1,9},{5,13},{10,2},{14,6},... | collective-permute-start | bytes 98312 | tf_op jit(solution)/shard_map/ppermute | solution.py:36
  108.5 10.1 %collective-permute-start.12 = (bf16[64,256]{1,0:T(8,128)(2,1)S(1)}, bf16[64,256]{1,0:T(8,128)(2,1)S(1)}, u32[]{:S(2)}, u32[]{:S(2)}) collective-permute-start(bf16[64,256]{1,0:T(8,128)(2,1)S(1)} %get-tuple-element.19), channel_id=1, source_target_pairs={{12,0},{0,4},{4,8},{8,12},{13,1},{1,5},{5,9},{9,13},{14,2},{2,6},{... | collective-permute-start | bytes 98312 | tf_op jit(solution)/shard_map/ppermute | solution.py:36
  114.3 10.5 %collective-permute-start.11 = (bf16[64,256]{1,0:T(8,128)(2,1)S(1)}, bf16[64,256]{1,0:T(8,128)(2,1)S(1)}, u32[]{:S(2)}, u32[]{:S(2)}) collective-permute-start(bf16[64,256]{1,0:T(8,128)(2,1)S(1)} %get-tuple-element.19), channel_id=1, source_target_pairs={{4,0},{8,4},{12,8},{0,12},{5,1},{9,5},{13,9},{1,13},{6,2},{10,6},{... | collective-permute-start | bytes 98312 | tf_op jit(solution)/shard_map/ppermute | solution.py:36
  124.8 3.2 %collective-permute-start.14 = (bf16[4,64,256]{2,1,0:T(8,128)(2,1)S(1)}, bf16[4,64,256]{2,1,0:T(8,128)(2,1)S(1)}, u32[]{:S(2)}, u32[]{:S(2)}) collective-permute-start(bf16[4,64,256]{2,1,0:T(8,128)(2,1)S(1)} %pad_maximum_fusion.5.refs_1_), channel_id=1, source_target_pairs={{0,16},{16,0},{1,17},{17,1},{2,18},{18,2},{3,19},{19,3},{4,20},{20... | collective-permute-start | bytes 393224 | tf_op jit(solution)/shard_map/ppermute | solution.py:21
  129.9 12.3 %all-to-all-start.5 = ((f32[8,72,128]{2,1,0:T(8,128)}), f32[8,72,128]{2,1,0:T(8,128)S(1)}, u32[]{:S(2)}, u32[]{:S(2)}) async-start(f32[8,72,128]{2,1,0:T(8,128)} %shard_map.78), calls=%async_computation.5 | async-start | bytes 589824 | tf_op jit(solution)/shard_map/all_to_all | solution.py:28
  (2 other events, 10.3 us)
